TPU v7x, 32 devices: a whole 2x2x4 slice. The times are simulated.
32 devices in a mesh: dx: 4 (over z), dy: 8 (over y, x, core).
Axes of the slice: x: 2, y: 2, z: 4, core: 2. Of those that a mesh axis runs over, the one named last changes fastest.
Arguments:
- orbitals: bfloat16 [56, 112, 13, 256], P('dx', 'dy'), may hold values from -6 to 6
- elem_mats: bfloat16 [8, 16, 2, 512, 512], P('dx', 'dy'), as said below
- conn: int32 [8, 16, 2, 512], P('dx', 'dy'), may hold values from 0 to 3374, as said below
Outputs:
- filtered: float32 [56, 112, 13, 256], P('dx', 'dy')
Inputs may be any that keep to these rules, and one draw needn't show every extreme that they name: conn[e1, e2, e3, k] is ((7 (e1 mod 2) + a) (15) + 7 (e2 mod 2) + b) * 15 + 7 e3 + c for a node (a, b, c) of the element, 0 <= a, b, c <= 7, and each of the element's 512 nodes appears exactly once. `elem_mats`: each element's matrix is symmetric.
All inputs are finite; a program needn't handle non-finite values.
Results may differ from a plain program's by a relative error of at most 0.0059.
Values may be sent and summed in bfloat16 or wider, within the bound.
No kernel may reach another device: no remote copies, remote signals or barrier semaphores. Data moves between devices by JAX's collectives and lax.ppermute only.
A program may use at most 128 MiB of HBM per device.

v0:
```python
import math

import jax
import jax.numpy as jnp
from jax import lax
from jax.sharding import PartitionSpec as P

filter_center = 1.5
filter_half = 4.0


def shifted(block, axis, distance):
    devices = range(lax.axis_size(axis))
    route = [(i - distance, i) for i in devices if i - distance in devices]
    return lax.ppermute(block, axis, route)


def apply_operator(field, elem_mats, conn):
    bands = field.shape[3]
    padded = jnp.pad(field, ((0, 0), (0, 0), (1, 1), (0, 0)))
    lower_plane = shifted(padded[-1], "dx", 1)
    extended = jnp.concatenate([lower_plane[None], padded], axis=0)
    side_plane = shifted(extended[:, -1], "dy", 1)
    extended = jnp.concatenate([side_plane[:, None], extended], axis=1)
    width = extended.shape[0]
    depth = extended.shape[2]
    flat = extended.reshape(-1, bands)
    nodes = elem_mats.shape[-1]
    count = elem_mats.shape[0] * elem_mats.shape[1] * elem_mats.shape[2]
    links = conn.reshape(-1)
    rows = jnp.take(flat, links, axis=0).reshape(count, nodes, bands)
    product = jnp.einsum(
        "eij,ejb->eib",
        elem_mats.reshape(count, nodes, nodes),
        rows,
        preferred_element_type=jnp.float32,
    )
    summed = (
        jnp.zeros((flat.shape[0], bands), jnp.float32).at[links].add(product.reshape(-1, bands))
    )
    summed = summed.reshape(width, width, depth, bands)
    back_y = shifted(summed[:, 0], "dy", -1)
    summed = summed[:, 1:].at[:, -1].add(back_y)
    back_x = shifted(summed[0], "dx", -1)
    summed = summed[1:].at[-1].add(back_x)
    return summed[:, :, 1:-1]


def gram_of(left, right):
    return jnp.einsum("rb,rc->bc", left, right, precision=lax.Precision.HIGHEST)


def shards(orbitals, elem_mats, conn):
    previous = orbitals.astype(jnp.float32)
    image = apply_operator(orbitals, elem_mats, conn)
    current = (image - filter_center * previous) / filter_half
    for turn in range(2):
        field = current.astype(jnp.bfloat16)
        image = apply_operator(field, elem_mats, conn)
        following = 2.0 * (image - filter_center * current) / filter_half - previous
        previous, current = (current, following)
    bands = current.shape[3]
    columns = current.reshape(-1, bands)
    gram_local = gram_of(columns, columns)
    gram_total = lax.psum(gram_local, ("dx", "dy"))
    lower = jnp.linalg.cholesky(gram_total)
    identity = jnp.eye(bands, dtype=jnp.float32)
    inverse_lower = lax.linalg.triangular_solve(lower, identity, left_side=True, lower=True)
    basis = jnp.einsum("rb,cb->rc", columns, inverse_lower, precision=lax.Precision.HIGHEST)
    scale = math.sqrt(columns.shape[0] * lax.axis_size(("dx", "dy")))
    return (basis * scale).reshape(current.shape)


def solution(mesh):
    in_specs = (
        P("dx", "dy", None, None),
        P("dx", "dy", None, None, None),
        P("dx", "dy", None, None),
    )
    out_specs = P("dx", "dy", None, None)
    return jax.shard_map(shards, mesh=mesh, in_specs=in_specs, out_specs=out_specs, check_vma=False)
```

profile of v0, /device:TPU:0, one launch (start us, length us, event | category | flops | bytes accessed | tf_op | source)
XLA Modules:
  0.0 498.1 jit_solution(1638879936248798844)
XLA Ops:
  6.5 1.9 copy.22
  8.5 4.9 collective-permute-start
  19.7 2.6 reshape.312
  22.3 17.0 %gather_fusion = bf16[4096,256]{1,0:T(8,128)(2,1)} fusion(bf16[3375,256]{1,0:T(8,128)(2,1)S(1)} %reshape.312, s32[4096]{0:T(1024)S(1)} %fusion.33), kind=kCustom, calls=%fused_computation.clone | custom fusion | bytes 4210688 | tf_op jit(solution)/shard_map/jit(_take)/gather | solution.py:31
  39.3 2.1 broadcast_select_fusion
  42.1 3.3 convolution_bitcast_fusion.2
  45.5 5.4 %copy.26 = f32[8,512,256]{2,1,0:T(8,128)} copy(f32[8,512,256]{1,2,0:T(8,128)} %convolution_bitcast_fusion.2) | data formatting | bytes 8388608 | tf_op jit(solution)/shard_map/eij,ejb->eib/dot_general | solution.py:32
  50.9 23.7 %scatter_custom_fusion = f32[3375,256]{1,0:T(8,128)S(1)} fusion(s32[4096]{0:T(1024)S(1)} %bitcast.143, f32[4096,256]{1,0:T(8,128)} %bitcast.129, f32[]{:T(128)} %constant.229.clone.1), kind=kCustom, calls=%fused_computation.31 | custom fusion | flops 1048576 | bytes 3456512 | tf_op jit(solution)/shard_map/scatter-add | solution.py:39
  74.5 2.2 reshape.317
  79.4 4.7 collective-permute-done.2
  86.0 6.7 %collective-permute-done.3 = f32[14,15,256]{2,1,0:T(8,128)S(1)} collective-permute-done((f32[14,15,256]{2,1,0:T(8,128)S(1)}, f32[14,15,256]{2,1,0:T(8,128)S(1)}, u32[]{:S(2)}, u32[]{:S(2)}) %collective-permute-start.3) | collective-permute-done | bytes 215072 | tf_op jit(solution)/shard_map/ppermute | solution.py:15
  94.5 3.9 collective-permute-start.4
  100.8 5.7 %collective-permute-start.5 = (bf16[15,15,256]{2,1,0:T(8,128)(2,1)S(1)}, bf16[15,15,256]{2,1,0:T(8,128)(2,1)S(1)}, u32[]{:S(2)}, u32[]{:S(2)}) collective-permute-start(bf16[15,15,256]{2,1,0:T(8,128)(2,1)S(1)} %fusion.26), channel_id=1, source_target_pairs={{0,1},{1,2},{2,3},{3,4},{4,5},{5,6},{6,7},{8,9},{9,10},{10,11},{11... | collective-permute-start | bytes 345608 | tf_op jit(solution)/shard_map/ppermute | solution.py:15
  108.5 2.6 reshape.320
  111.1 17.0 %gather_fusion.1 = bf16[4096,256]{1,0:T(8,128)(2,1)} fusion(bf16[3375,256]{1,0:T(8,128)(2,1)S(1)} %reshape.320, s32[4096]{0:T(1024)S(1)} %fusion.33), kind=kCustom, calls=%fused_computation.1.clone | custom fusion | bytes 4210688 | tf_op jit(solution)/shard_map/jit(_take)/gather | solution.py:31
  128.1 2.1 broadcast_select_fusion.1
  130.9 3.3 convolution_bitcast_fusion.1
  134.3 5.4 %copy.32 = f32[8,512,256]{2,1,0:T(8,128)} copy(f32[8,512,256]{1,2,0:T(8,128)} %convolution_bitcast_fusion.1) | data formatting | bytes 8388608 | tf_op jit(solution)/shard_map/eij,ejb->eib/dot_general | solution.py:32
  139.6 24.8 %scatter_custom_fusion.1 = f32[3375,256]{1,0:T(8,128)} fusion(s32[4096]{0:T(1024)S(1)} %bitcast.144, f32[4096,256]{1,0:T(8,128)} %bitcast.130, f32[]{:T(128)} %constant.229.clone.1), kind=kCustom, calls=%fused_computation.29 | custom fusion | flops 1048576 | bytes 3456512 | tf_op jit(solution)/shard_map/scatter-add | solution.py:39
  164.4 4.7 reshape.323
  171.8 5.6 %collective-permute-done.6 = f32[15,15,256]{2,1,0:T(8,128)S(1)} collective-permute-done((f32[15,15,256]{2,1,0:T(8,128)S(1)}, f32[15,15,256]{2,1,0:T(8,128)S(1)}, u32[]{:S(2)}, u32[]{:S(2)}) %collective-permute-start.6) | collective-permute-done | bytes 230432 | tf_op jit(solution)/shard_map/ppermute | solution.py:15
  179.4 6.8 %collective-permute-done.7 = f32[14,15,256]{2,1,0:T(8,128)S(1)} collective-permute-done((f32[14,15,256]{2,1,0:T(8,128)S(1)}, f32[14,15,256]{2,1,0:T(8,128)S(1)}, u32[]{:S(2)}, u32[]{:S(2)}) %collective-permute-start.7) | collective-permute-done | bytes 215072 | tf_op jit(solution)/shard_map/ppermute | solution.py:15
  188.0 3.9 collective-permute-start.8
  192.6 1.7 collective-permute-done.8
  194.3 5.4 %collective-permute-start.9 = (bf16[15,15,256]{2,1,0:T(8,128)(2,1)S(1)}, bf16[15,15,256]{2,1,0:T(8,128)(2,1)S(1)}, u32[]{:S(2)}, u32[]{:S(2)}) collective-permute-start(bf16[15,15,256]{2,1,0:T(8,128)(2,1)S(1)} %fusion.25), channel_id=1, source_target_pairs={{0,1},{1,2},{2,3},{3,4},{4,5},{5,6},{6,7},{8,9},{9,10},{10,11},{11... | collective-permute-start | bytes 345608 | tf_op jit(solution)/shard_map/ppermute | solution.py:15
  202.0 2.6 reshape.326
  204.6 17.0 %gather_fusion.2 = bf16[4096,256]{1,0:T(8,128)(2,1)} fusion(bf16[3375,256]{1,0:T(8,128)(2,1)S(1)} %reshape.326, s32[4096]{0:T(1024)S(1)} %fusion.33), kind=kCustom, calls=%fused_computation.2.clone | custom fusion | bytes 4210688 | tf_op jit(solution)/shard_map/jit(_take)/gather | solution.py:31
  221.7 2.1 broadcast_select_fusion.2
  224.5 3.3 convolution_bitcast_fusion
  227.8 5.4 %copy.36 = f32[8,512,256]{2,1,0:T(8,128)} copy(f32[8,512,256]{1,2,0:T(8,128)} %convolution_bitcast_fusion) | data formatting | bytes 8388608 | tf_op jit(solution)/shard_map/eij,ejb->eib/dot_general | solution.py:32
  233.2 23.7 %scatter_custom_fusion.2 = f32[3375,256]{1,0:T(8,128)S(1)} fusion(s32[4096]{0:T(1024)S(1)} %bitcast.145, f32[4096,256]{1,0:T(8,128)} %bitcast.128, f32[]{:T(128)} %constant.229.clone.1), kind=kCustom, calls=%fused_computation.27 | custom fusion | flops 1048576 | bytes 3456512 | tf_op jit(solution)/shard_map/scatter-add | solution.py:39
  256.9 2.2 reshape.329
  261.8 4.3 collective-permute-done.10
  268.1 6.8 %collective-permute-done.11 = f32[14,15,256]{2,1,0:T(8,128)S(1)} collective-permute-done((f32[14,15,256]{2,1,0:T(8,128)S(1)}, f32[14,15,256]{2,1,0:T(8,128)S(1)}, u32[]{:S(2)}, u32[]{:S(2)}) %collective-permute-start.11) | collective-permute-done | bytes 215072 | tf_op jit(solution)/shard_map/ppermute | solution.py:15
  275.0 2.4 fusion.2
  277.3 6.0 %convolution_bitcast_fusion.3 = f32[256,256]{0,1:T(8,128)} fusion(f32[14,14,13,256]{3,2,1,0:T(8,128)S(1)} %fusion.2), kind=kOutput, calls=%fused_computation.34 | convolution fusion | flops 2003828736 | bytes 2871296 | tf_op jit(solution)/shard_map/rb,rc->bc/dot_general | solution.py:50
  283.4 1.8 reshape.332
  285.3 130.6 %all-reduce.6.cloned.1.call-done = f32[256,256]{0,1:T(8,128)} async-done(((f32[256,256]{0,1:T(8,128)}), f32[256,256]{0,1:T(8,128)}) %all-reduce.6.cloned.1.call-update) | async-done | bytes 262160 | tf_op jit(solution)/shard_map/psum | solution.py:65
  417.9 11.7 %cholesky.50 = f32[128,128]{1,0:T(8,128)S(1)} custom-call(f32[128,128]{1,0:T(8,128)S(1)} %cholesky.118), custom_call_target="Cholesky" | custom-call | tf_op jit(solution)/shard_map/jit(cholesky)/cholesky | solution.py:66
  429.7 10.0 %custom-call.14 = f32[1,128,128]{1,2,0:T(8,128)S(1)} custom-call(f32[1,128,128]{2,1,0:T(8,128)S(1)} %get-tuple-element.99), custom_call_target="InvertDiagBlocksLowerTriangular" | custom-call | tf_op jit(solution)/shard_map/jit(cholesky)/cholesky | solution.py:66
  440.2 11.7 %cholesky.105 = f32[128,128]{1,0:T(8,128)S(1)} custom-call(f32[128,128]{1,0:T(8,128)S(1)} %convolution_subtract_fusion.1), custom_call_target="Cholesky" | custom-call | tf_op jit(solution)/shard_map/jit(cholesky)/cholesky | solution.py:66
  454.2 5.5 %while.7 = (s32[]{:T(128)}, f32[256,256]{1,0:T(8,128)S(1)}, s32[2,2]{1,0:T(2,128)S(1)}, f32[2,128,128]{2,1,0:T(8,128)}, s32[]{:T(128)}) while((s32[]{:T(128)}, f32[256,256]{1,0:T(8,128)S(1)}, s32[2,2]{1,0:T(2,128)S(1)}, f32[2,128,128]{2,1,0:T(8,128)}, s32[]{:T(128)}) %tuple.48), condition=%wide.while_cond.6, body=%wide.while_body.6.sunk | while | flops 2 | bytes 132705 | solution.py:68
  454.8 2.1 bitcast_dynamic-update-slice_fusion.2
  457.6 2.1 bitcast_dynamic-update-slice_fusion.2
  459.7 20.5 %custom-call.15 = f32[2,128,128]{1,2,0:T(8,128)S(1)} custom-call(f32[2,128,128]{2,1,0:T(8,128)} %get-tuple-element.85), custom_call_target="InvertDiagBlocksLowerTriangular" | custom-call | tf_op jit(solution)/shard_map/triangular_solve | solution.py:68
  481.1 3.7 convolution_multiply_fusion
  484.8 2.6 reshape.333
  487.4 3.5 copy.42
  (106 shorter events, 38.8 us)
Async XLA Ops:
  6.5 6.9 %copy-start.14 = (s32[2,2,2,512]{3,2,1,0:T(2,128)S(1)}, s32[2,2,2,512]{3,2,1,0:T(2,128)}, u32[]{:S(2)}) copy-start(s32[2,2,2,512]{3,2,1,0:T(2,128)} %param.19) | copy-start | bytes 49156
  6.5 409.3 %all-reduce.6.cloned.1.call-start = ((), (), s32[]{:S(2)}) async-start(), calls=%async_computation | async-start | bytes 524288 | tf_op jit(solution)/shard_map/psum | solution.py:65
  8.5 7.3 %collective-permute-start = (bf16[14,15,256]{2,1,0:T(8,128)(2,1)S(1)}, bf16[14,15,256]{2,1,0:T(8,128)(2,1)S(1)}, u32[]{:S(2)}, u32[]{:S(2)}) collective-permute-start(bf16[14,15,256]{2,1,0:T(8,128)(2,1)S(1)} %slice_bitcast_fusion.9), channel_id=1, source_target_pairs={{0,8},{8,16},{16,24},{1,9},{9,17},{17,25},{2,10},{10,18},{18,26},{... | collective-permute-start | bytes 322568 | tf_op jit(solution)/shard_map/ppermute | solution.py:15
  15.8 2.3 collective-permute-start.1
  39.3 2.8 copy-start.3
  76.7 7.4 %copy-start.10 = (f32[15,15,15,256]{3,2,1,0:T(8,128)S(1)}, f32[15,15,15,256]{3,2,1,0:T(8,128)}, u32[]{:S(2)}) copy-start(f32[15,15,15,256]{3,2,1,0:T(8,128)} %reshape.317) | copy-start | bytes 10368004
  77.9 6.3 %slice-start = ((f32[15,15,15,256]{3,2,1,0:T(8,128)}), f32[15,14,15,256]{3,2,1,0:T(8,128)S(1)}, s32[]{:S(2)}) async-start(f32[15,15,15,256]{3,2,1,0:T(8,128)} %reshape.317), calls=%async_computation.1 | async-start | bytes 6881280 | tf_op jit(solution)/shard_map/slice | solution.py:43
  77.9 6.3 %collective-permute-start.2 = (f32[15,15,256]{2,1,0:T(8,128)S(1)}, f32[15,15,256]{2,1,0:T(8,128)S(1)}, u32[]{:S(2)}, u32[]{:S(2)}) collective-permute-start(f32[15,15,256]{2,1,0:T(8,128)S(1)} %slice_bitcast_fusion.2), channel_id=1, source_target_pairs={{1,0},{2,1},{3,2},{4,3},{5,4},{6,5},{7,6},{9,8},{10,9},{11,10},{12... | collective-permute-start | bytes 691208 | tf_op jit(solution)/shard_map/ppermute | solution.py:15
  84.2 8.6 %copy-start.8 = (bf16[14,14,13,256]{3,1,2,0:T(8,128)(2,1)S(1)}, bf16[14,14,13,256]{3,1,2,0:T(8,128)(2,1)}, u32[]{:S(2)}) copy-start(bf16[14,14,13,256]{3,1,2,0:T(8,128)(2,1)} %param.17) | copy-start | bytes 3913732
  84.2 8.5 %collective-permute-start.3 = (f32[14,15,256]{2,1,0:T(8,128)S(1)}, f32[14,15,256]{2,1,0:T(8,128)S(1)}, u32[]{:S(2)}, u32[]{:S(2)}) collective-permute-start(f32[14,15,256]{2,1,0:T(8,128)S(1)} %slice_bitcast_fusion.6), channel_id=1, source_target_pairs={{8,0},{16,8},{24,16},{9,1},{17,9},{25,17},{10,2},{18,10},{26,18},{... | collective-permute-start | bytes 645128 | tf_op jit(solution)/shard_map/ppermute | solution.py:15
  92.8 1.7 copy-start
  94.5 6.3 %collective-permute-start.4 = (bf16[14,15,256]{2,1,0:T(8,128)(2,1)S(1)}, bf16[14,15,256]{2,1,0:T(8,128)(2,1)S(1)}, u32[]{:S(2)}, u32[]{:S(2)}) collective-permute-start(bf16[14,15,256]{2,1,0:T(8,128)(2,1)S(1)} %slice_bitcast_fusion.8), channel_id=1, source_target_pairs={{0,8},{8,16},{16,24},{1,9},{9,17},{17,25},{2,10},{10,18},{18,26},{... | collective-permute-start | bytes 322568 | tf_op jit(solution)/shard_map/ppermute | solution.py:15
  100.8 6.2 %collective-permute-start.5 = (bf16[15,15,256]{2,1,0:T(8,128)(2,1)S(1)}, bf16[15,15,256]{2,1,0:T(8,128)(2,1)S(1)}, u32[]{:S(2)}, u32[]{:S(2)}) collective-permute-start(bf16[15,15,256]{2,1,0:T(8,128)(2,1)S(1)} %fusion.26), channel_id=1, source_target_pairs={{0,1},{1,2},{2,3},{3,4},{4,5},{5,6},{6,7},{8,9},{9,10},{10,11},{11... | collective-permute-start | bytes 345608 | tf_op jit(solution)/shard_map/ppermute | solution.py:15
  128.1 2.8 copy-start.4
  169.1 8.3 %copy-start.11 = (f32[15,15,15,256]{3,2,1,0:T(8,128)S(1)}, f32[15,15,15,256]{3,2,1,0:T(8,128)}, u32[]{:S(2)}) copy-start(f32[15,15,15,256]{3,2,1,0:T(8,128)} %reshape.323) | copy-start | bytes 10368004
  170.3 7.2 %slice-start.1 = ((f32[15,15,15,256]{3,2,1,0:T(8,128)}), f32[15,14,15,256]{3,2,1,0:T(8,128)S(1)}, s32[]{:S(2)}) async-start(f32[15,15,15,256]{3,2,1,0:T(8,128)} %reshape.323), calls=%async_computation.2 | async-start | bytes 6881280 | tf_op jit(solution)/shard_map/slice | solution.py:43
  170.3 7.2 %collective-permute-start.6 = (f32[15,15,256]{2,1,0:T(8,128)S(1)}, f32[15,15,256]{2,1,0:T(8,128)S(1)}, u32[]{:S(2)}, u32[]{:S(2)}) collective-permute-start(f32[15,15,256]{2,1,0:T(8,128)S(1)} %slice_bitcast_fusion.1), channel_id=1, source_target_pairs={{1,0},{2,1},{3,2},{4,3},{5,4},{6,5},{7,6},{9,8},{10,9},{11,10},{12... | collective-permute-start | bytes 691208 | tf_op jit(solution)/shard_map/ppermute | solution.py:15
  177.5 8.7 %copy-start.1 = (f32[14,14,15,256]{3,2,1,0:T(8,128)S(1)}, f32[14,14,15,256]{3,2,1,0:T(8,128)}, u32[]{:S(2)}) copy-start(f32[14,14,15,256]{3,2,1,0:T(8,128)} %copy-done) | copy-start | bytes 9031684
  177.6 8.6 %collective-permute-start.7 = (f32[14,15,256]{2,1,0:T(8,128)S(1)}, f32[14,15,256]{2,1,0:T(8,128)S(1)}, u32[]{:S(2)}, u32[]{:S(2)}) collective-permute-start(f32[14,15,256]{2,1,0:T(8,128)S(1)} %slice_bitcast_fusion.5), channel_id=1, source_target_pairs={{8,0},{16,8},{24,16},{9,1},{17,9},{25,17},{10,2},{18,10},{26,18},{... | collective-permute-start | bytes 645128 | tf_op jit(solution)/shard_map/ppermute | solution.py:15
  186.2 1.8 copy-start.6
  188.0 6.3 %collective-permute-start.8 = (bf16[14,15,256]{2,1,0:T(8,128)(2,1)S(1)}, bf16[14,15,256]{2,1,0:T(8,128)(2,1)S(1)}, u32[]{:S(2)}, u32[]{:S(2)}) collective-permute-start(bf16[14,15,256]{2,1,0:T(8,128)(2,1)S(1)} %slice_bitcast_fusion.7), channel_id=1, source_target_pairs={{0,8},{8,16},{16,24},{1,9},{9,17},{17,25},{2,10},{10,18},{18,26},{... | collective-permute-start | bytes 322568 | tf_op jit(solution)/shard_map/ppermute | solution.py:15
  194.3 6.2 %collective-permute-start.9 = (bf16[15,15,256]{2,1,0:T(8,128)(2,1)S(1)}, bf16[15,15,256]{2,1,0:T(8,128)(2,1)S(1)}, u32[]{:S(2)}, u32[]{:S(2)}) collective-permute-start(bf16[15,15,256]{2,1,0:T(8,128)(2,1)S(1)} %fusion.25), channel_id=1, source_target_pairs={{0,1},{1,2},{2,3},{3,4},{4,5},{5,6},{6,7},{8,9},{9,10},{10,11},{11... | collective-permute-start | bytes 345608 | tf_op jit(solution)/shard_map/ppermute | solution.py:15
  221.6 2.8 copy-start.5
  259.1 7.0 %copy-start.12 = (f32[15,15,15,256]{3,2,1,0:T(8,128)S(1)}, f32[15,15,15,256]{3,2,1,0:T(8,128)}, u32[]{:S(2)}) copy-start(f32[15,15,15,256]{3,2,1,0:T(8,128)} %reshape.329) | copy-start | bytes 10368004
  260.2 5.9 %slice-start.2 = ((f32[15,15,15,256]{3,2,1,0:T(8,128)}), f32[15,14,15,256]{3,2,1,0:T(8,128)S(1)}, s32[]{:S(2)}) async-start(f32[15,15,15,256]{3,2,1,0:T(8,128)} %reshape.329), calls=%async_computation.3 | async-start | bytes 6881280 | tf_op jit(solution)/shard_map/slice | solution.py:43
  260.2 5.9 %collective-permute-start.10 = (f32[15,15,256]{2,1,0:T(8,128)S(1)}, f32[15,15,256]{2,1,0:T(8,128)S(1)}, u32[]{:S(2)}, u32[]{:S(2)}) collective-permute-start(f32[15,15,256]{2,1,0:T(8,128)S(1)} %slice_bitcast_fusion), channel_id=1, source_target_pairs={{1,0},{2,1},{3,2},{4,3},{5,4},{6,5},{7,6},{9,8},{10,9},{11,10},{12... | collective-permute-start | bytes 691208 | tf_op jit(solution)/shard_map/ppermute | solution.py:15
  261.8 13.2 %copy-start.9 = (bf16[14,14,13,256]{3,1,2,0:T(8,128)(2,1)S(1)}, bf16[14,14,13,256]{3,1,2,0:T(8,128)(2,1)}, u32[]{:S(2)}) copy-start(bf16[14,14,13,256]{3,1,2,0:T(8,128)(2,1)} %param.17) | copy-start | bytes 3913732
  266.2 8.8 %copy-start.2 = (f32[14,14,15,256]{3,2,1,0:T(8,128)S(1)}, f32[14,14,15,256]{3,2,1,0:T(8,128)}, u32[]{:S(2)}) copy-start(f32[14,14,15,256]{3,2,1,0:T(8,128)} %copy-done) | copy-start | bytes 9031684
  266.2 8.8 %copy-start.7 = (f32[14,14,15,256]{3,2,1,0:T(8,128)S(1)}, f32[14,14,15,256]{3,2,1,0:T(8,128)}, u32[]{:S(2)}) copy-start(f32[14,14,15,256]{3,2,1,0:T(8,128)} %copy-done.6) | copy-start | bytes 9031684
  266.2 8.7 %collective-permute-start.11 = (f32[14,15,256]{2,1,0:T(8,128)S(1)}, f32[14,15,256]{2,1,0:T(8,128)S(1)}, u32[]{:S(2)}, u32[]{:S(2)}) collective-permute-start(f32[14,15,256]{2,1,0:T(8,128)S(1)} %slice_bitcast_fusion.4), channel_id=1, source_target_pairs={{8,0},{16,8},{24,16},{9,1},{17,9},{25,17},{10,2},{18,10},{26,18},{... | collective-permute-start | bytes 645128 | tf_op jit(solution)/shard_map/ppermute | solution.py:15
  285.3 195.8 %copy-start.13 = (f32[2548,256]{1,0:T(8,128)S(1)}, f32[2548,256]{1,0:T(8,128)}, u32[]{:S(2)}) copy-start(f32[2548,256]{1,0:T(8,128)} %reshape.332) | copy-start | bytes 7827460
Sparse Core Ops, SparseCore 0:
  283.5 132.2 all-reduce.5
where the time goes:
time: 507 us; the launch traced here: 498 us
  waiting for transfers between devices  173 us (34%)
  other arithmetic  143 us (28%)
  local copies, waits for them, and re-layouts  111 us (22%)
  starting transfers between devices  34.3 us (7%)
  matrix products  21 us (4%)
  between operations  15.8 us (3%)
    psum x1, waiting for transfers between devices, shards(): gram_total = lax.psum(gram_local, ('dx', 'dy'))  131 us
    scatter-add x3, other arithmetic, apply_operator(): jnp.zeros((flat.shape[0], bands), jnp.float32).at[links]  72.1 us
    gather x3, local copies, waits for them, and re-layouts, apply_operator(): rows = jnp.take(flat, links, axis=0).reshape(count, nodes, bands)  51.1 us
    ppermute x12, waiting for transfers between devices, shifted(): return lax.ppermute(block, axis, route)  42.2 us
    ppermute x12, starting transfers between devices, shifted(): return lax.ppermute(block, axis, route)  34.3 us
    another operation x6, other arithmetic, shards(): lower = jnp.linalg.cholesky(gram_total)  34.3 us
    another operation x3, other arithmetic, shards(): lax.linalg.triangular_solve(lower, identity, left_side=True, lower=True)  20.5 us
    dot_general x3, local copies, waits for them, and re-layouts, apply_operator(): jnp.einsum('eij,ejb->eib', elem_mats.reshape(count, nodes, nodes), rows,...  16.2 us
  transfers between devices with their start and end apart: 13, of which 13 were waited for; matrix products, arithmetic and copies ran while one was open for 1% of the time, Pallas kernels for 0%

commit v1 on v0

v1 whole, which is shorter than its diff:
```python
import functools
import math

import jax
import jax.numpy as jnp
from jax import lax
from jax.experimental import pallas as pl
from jax.experimental.pallas import tpu as pltpu
from jax.sharding import PartitionSpec as P

filter_center = 1.5
filter_half = 4.0
AXES = ("dx", "dy")
VMEM = pl.BlockSpec(memory_space=pltpu.VMEM)
LIMIT = 48 * 1024 * 1024
LANES = 128


def partner(index, size, pairing):
    if pairing == "-":
        return index
    other = index ^ 1 if pairing == "A" else index - 1 if index % 2 == 0 else index + 1
    return other if 0 <= other < size else index


def pair_swap(value, along_x, along_y):
    size_x, size_y = lax.axis_size("dx"), lax.axis_size("dy")
    route = [
        (p * size_y + q, partner(p, size_x, along_x) * size_y + partner(q, size_y, along_y))
        for p in range(size_x)
        for q in range(size_y)
    ]
    return lax.ppermute(value, AXES, route)


def offset(value, step_x, step_y):
    size_x, size_y = lax.axis_size("dx"), lax.axis_size("dy")
    route = [
        (p * size_y + q, (p + step_x) * size_y + q + step_y)
        for p in range(size_x)
        for q in range(size_y)
        if 0 <= p + step_x < size_x and 0 <= q + step_y < size_y
    ]
    return lax.ppermute(value, AXES, route)


def xor_swap(value, axis, bits):
    return lax.ppermute(value, axis, [(i, i ^ bits) for i in range(lax.axis_size(axis))])


def total(gram):
    sizes = [lax.axis_size(axis) for axis in AXES]
    if any(size & (size - 1) or size < 2 for size in sizes):
        return lax.psum(gram, AXES)
    half = gram.shape[0] // 2
    odd = lax.axis_index("dy") % 2
    kept = lax.dynamic_slice_in_dim(gram, odd * half, half, 0)
    sent = lax.dynamic_slice_in_dim(gram, (1 - odd) * half, half, 0)
    part = kept + xor_swap(sent, "dy", 1)
    for axis, first in (("dx", 1), ("dy", 2)):
        bit = first
        while bit < lax.axis_size(axis):
            if 2 * bit < lax.axis_size(axis):
                one, two, three = [xor_swap(part, axis, bit * k) for k in (1, 2, 3)]
                part = (part + one) + (two + three)
                bit *= 4
            else:
                part = part + xor_swap(part, axis, bit)
                bit *= 2
    other = xor_swap(part, "dy", 1)
    low = jnp.where(odd == 0, part, other)
    high = jnp.where(odd == 0, other, part)
    return jnp.concatenate([low, high], axis=0)


def renumber_kernel(conn_ref, mats_ref, out_ref, *, side, width, depth, layers):
    e1, e2, e3 = (pl.program_id(k) for k in range(3))
    deg = side - 1
    rows = conn_ref[0, 0]
    node = rows[0:1]
    for k in range(1, layers):
        node = jnp.where(e3 == k, rows[k : k + 1], node)
    node = node.astype(jnp.float32)
    plane = jnp.floor((node + 0.5) * (1.0 / depth))
    first = jnp.floor((plane + 0.5) * (1.0 / width))
    c = (node - plane * depth).astype(jnp.int32) - deg * e3
    b = (plane - first * width).astype(jnp.int32) - deg * e2
    a = first.astype(jnp.int32) - deg * e1
    place = (a * side + c) * side + b
    a = jnp.where((e1 == 0) & (lax.axis_index("dx") == 0), a, 1)
    b = jnp.where((e2 == 0) & (lax.axis_index("dy") == 0), b, 1)
    c_low = jnp.where(e3 == 0, c, 1)
    c_high = jnp.where(e3 == layers - 1, c, 1)
    held = (a == 0) | (b == 0) | (c_low == 0) | (c_high == deg)
    place = jnp.where(held, -1, place)
    count = mats_ref.shape[-1]
    order = lax.broadcasted_iota(jnp.int32, (count, count), 0) == place
    order = jnp.where(order, 1.0, 0.0).astype(jnp.bfloat16)
    half = jnp.dot(order, mats_ref[0, 0, 0], preferred_element_type=jnp.float32)
    whole = lax.dot_general(
        half.astype(jnp.bfloat16),
        order,
        (((1,), (1,)), ((), ())),
        preferred_element_type=jnp.float32,
    )
    out_ref[0, 0, 0] = whole.astype(jnp.bfloat16)


def renumber(conn, elem_mats, side, width, depth):
    ex, ey, layers, count, _ = elem_mats.shape
    spot = pl.BlockSpec((1, 1, 1, count, count), lambda i, j, k: (i, j, k, 0, 0))
    return pl.pallas_call(
        functools.partial(renumber_kernel, side=side, width=width, depth=depth, layers=layers),
        out_shape=jax.ShapeDtypeStruct(elem_mats.shape, jnp.bfloat16),
        grid=(ex, ey, layers),
        in_specs=[pl.BlockSpec((1, 1, layers, count), lambda i, j, k: (i, j, 0, 0)), spot],
        out_specs=spot,
        compiler_params=pltpu.CompilerParams(vmem_limit_bytes=LIMIT),
        cost_estimate=pl.CostEstimate(
            flops=4 * ex * ey * layers * count**3,
            bytes_accessed=4 * elem_mats.size,
            transcendentals=0,
        ),
        name="renumber",
    )(conn, elem_mats)


class Grid:
    def __init__(self, elem_mats, side):
        self.ex, self.ey, self.ez = elem_mats.shape[:3]
        self.count = elem_mats.shape[3]
        self.side = side
        self.deg = side - 1
        self.nz = self.ez * self.deg - 1
        self.elements = self.ex * self.ey * self.ez

    def at(self, e1, e2, e3):
        return (e1 * self.ey + e2) * self.ez + e3

    def rows(self, a, c, number):
        start = (a * self.side + c) * self.side
        return slice(start, start + number * self.side)

    def layers(self, e3):
        low = 1 if e3 == 0 else 0
        high = self.deg - 1 if e3 == self.ez - 1 else self.deg
        return low, high - low + 1, e3 * self.deg + low - 1

    def side_rows(self, b):
        return pl.ds(b, self.side * self.side, stride=self.side)

    def line_rows(self, a, b):
        return pl.ds(a * self.side * self.side + b, self.side, stride=self.side)


def lanes(h):
    return slice(h * LANES, (h + 1) * LANES)


def multiply(g, mats_ref, field_of, w_ref):
    side, deg = g.side, g.deg
    halves = range(w_ref.shape[1])
    for e in range(g.elements):
        product = jnp.dot(mats_ref[e], field_of(e), preferred_element_type=jnp.float32)
        for h in halves:
            w_ref[e, h] = product[:, lanes(h)]

    def join(one, top, two, bottom):
        for h in halves:
            both = w_ref[one, h, top] + w_ref[two, h, bottom]
            w_ref[one, h, top] = both
            w_ref[two, h, bottom] = both

    for e1 in range(g.ex):
        for e2 in range(g.ey):
            for e3 in range(g.ez - 1):
                for a in range(side):
                    one, two = g.at(e1, e2, e3), g.at(e1, e2, e3 + 1)
                    join(one, g.rows(a, deg, 1), two, g.rows(a, 0, 1))
    for e1 in range(g.ex - 1):
        for e2 in range(g.ey):
            for e3 in range(g.ez):
                one, two = g.at(e1, e2, e3), g.at(e1 + 1, e2, e3)
                join(one, g.rows(deg, 0, side), two, g.rows(0, 0, side))
    for e1 in range(g.ex):
        for e2 in range(g.ey - 1):
            for e3 in range(g.ez):
                one, two = g.at(e1, e2, e3), g.at(e1, e2 + 1, e3)
                join(one, g.side_rows(deg), two, g.side_rows(0))


def put_x_face(g, w_ref, put):
    for h in range(w_ref.shape[1]):
        for e2 in range(g.ey):
            for e3 in range(g.ez):
                low, number, start = g.layers(e3)
                if e3 > 0:
                    low, number, start = low + 1, number - 1, start + 1
                one = w_ref[g.at(0, e2, e3), h, g.rows(0, low, number)]
                two = w_ref[g.at(g.ex - 1, e2, e3), h, g.rows(g.deg, low, number)]
                where = (
                    slice(start, start + number),
                    slice(e2 * g.side, (e2 + 1) * g.side),
                    lanes(h),
                )
                shape = (number, g.side, LANES)
                put(where, one.reshape(shape), two.reshape(shape))


def put_y_face(g, w_ref, put):
    for h in range(w_ref.shape[1]):
        for e1 in range(g.ex):
            for e3 in range(g.ez):
                one = w_ref[g.at(e1, 0, e3), h, g.side_rows(0)]
                two = w_ref[g.at(e1, g.ey - 1, e3), h, g.side_rows(g.deg)]
                put((e1 * g.ez + e3, slice(None), lanes(h)), one, two)


def line(g, w_ref, high_x, high_y, e3, h):
    e1, a = (g.ex - 1, g.deg) if high_x else (0, 0)
    e2, b = (g.ey - 1, g.deg) if high_y else (0, 0)
    return w_ref[g.at(e1, e2, e3), h, g.line_rows(a, b)]


def add_x_face(g, out_ref, high, received, factor):
    e1, a = (g.ex - 1, g.deg) if high else (0, 0)
    for h in range(out_ref.shape[1]):
        for e2 in range(g.ey):
            for e3 in range(g.ez):
                low, number, start = g.layers(e3)
                columns = slice(e2 * g.side, (e2 + 1) * g.side)
                part = received((slice(start, start + number), columns, lanes(h)))
                rows = g.rows(a, low, number)
                part = part.reshape(number * g.side, LANES)
                out_ref[g.at(e1, e2, e3), h, rows] += factor * part


def add_y_face(g, out_ref, high, received, factor):
    e2, b = (g.ey - 1, g.deg) if high else (0, 0)
    for h in range(out_ref.shape[1]):
        for e1 in range(g.ex):
            for e3 in range(g.ez):
                part = received((e1 * g.ez + e3, slice(None), lanes(h)))
                out_ref[g.at(e1, e2, e3), h, g.side_rows(b)] += factor * part


def add_line(g, out_ref, high_x, high_y, received, factor):
    e1, a = (g.ex - 1, g.deg) if high_x else (0, 0)
    e2, b = (g.ey - 1, g.deg) if high_y else (0, 0)
    for h in range(out_ref.shape[1]):
        for e3 in range(g.ez):
            part = received((slice(e3 * g.side, (e3 + 1) * g.side), lanes(h)))
            out_ref[g.at(e1, e2, e3), h, g.line_rows(a, b)] += factor * part


def send_all(g, w_ref, sends):
    even_x = lax.axis_index("dx") % 2 == 0
    even_y = lax.axis_index("dy") % 2 == 0

    def by_pair(even, one_ref, two_ref):
        def put(where, low, high):
            one_ref[where] = jnp.where(even, high, low)
            two_ref[where] = jnp.where(even, low, high)

        return put

    put_x_face(g, w_ref, by_pair(even_x, sends[0], sends[1]))
    put_y_face(g, w_ref, by_pair(even_y, sends[2], sends[3]))
    for h in range(w_ref.shape[1]):
        for e3 in range(g.ez):
            where = (slice(e3 * g.side, (e3 + 1) * g.side), lanes(h))
            at_x = [[line(g, w_ref, hx, hy, e3, h) for hy in (0, 1)] for hx in (0, 1)]
            for my in (0, 1):
                low, high = [jnp.where(even_y, at_x[hx][1 - my], at_x[hx][my]) for hx in (0, 1)]
                by_pair(even_x, sends[4 + my], sends[6 + my])(where, low, high)


def add_all(g, out_ref, received, factor):
    p, q = lax.axis_index("dx"), lax.axis_index("dy")
    even_x, even_y = p % 2 == 0, q % 2 == 0
    has_x = (p > 0, p < lax.axis_size("dx") - 1)
    has_y = (q > 0, q < lax.axis_size("dy") - 1)

    def from_pair(even, high, one, two, exists):
        value = jnp.where(even, one, two) if high else jnp.where(even, two, one)
        return jnp.where(exists, value, 0.0)

    for high in (0, 1):

        def across_x(where):
            return from_pair(even_x, high, received[0][where], received[1][where], has_x[high])

        def across_y(where):
            return from_pair(even_y, high, received[2][where], received[3][where], has_y[high])

        add_x_face(g, out_ref, high, across_x, factor)
        add_y_face(g, out_ref, high, across_y, factor)
    for hx in (0, 1):
        for hy in (0, 1):

            def diagonal(where):
                one = from_pair(even_y, hy, received[4][where], received[5][where], has_y[hy])
                two = from_pair(even_y, hy, received[6][where], received[7][where], has_y[hy])
                return from_pair(even_x, hx, one, two, has_x[hx])

            add_line(g, out_ref, hx, hy, diagonal, factor)


def field_of(y_ref, e):
    parts = [y_ref[e, h].astype(jnp.bfloat16) for h in range(y_ref.shape[1])]
    return jnp.concatenate(parts, axis=-1)


def first_kernel(*refs, g):
    orb_ref, below_x, below_y, below_xy, mats_ref, y_ref, w_ref, *sends = refs
    side = g.side
    halves = range(y_ref.shape[1])
    sub = lax.broadcasted_iota(jnp.int32, (side, LANES), 0)
    nothing = jnp.zeros((side, LANES), jnp.float32)
    rest = orb_ref.shape[2] - side
    for e1 in range(g.ex):
        for e2 in range(g.ey):
            for a in range(side):
                for h in halves:
                    y_ref[g.at(e1, e2, 0), h, g.rows(a, 0, 1)] = nothing
                    y_ref[g.at(e1, e2, g.ez - 1), h, g.rows(a, g.deg, 1)] = nothing

    def place(i, k, column, edge):
        for h in halves:
            part = column[:, lanes(h)].astype(jnp.float32)
            t0 = part[:side]
            t1 = jnp.concatenate([part[side:], nothing[: side - rest]], axis=0)
            first = jnp.broadcast_to(edge[:, lanes(h)].astype(jnp.float32), (side, LANES))
            d0 = jnp.where(sub == 0, first, pltpu.roll(t0, 1, 0))
            d1 = jnp.where(sub < 2, pltpu.roll(t0, 2, 0), pltpu.roll(t1, 2, 0))
            for e1 in range(g.ex):
                a = i - e1 * g.deg
                for e3 in range(g.ez):
                    c = k + 1 - e3 * g.deg
                    if 0 <= a <= g.deg and 0 <= c <= g.deg:
                        y_ref[g.at(e1, 0, e3), h, g.rows(a, c, 1)] = d0
                        y_ref[g.at(e1, 1, e3), h, g.rows(a, c, 1)] = d1

    for k in range(g.nz):
        place(0, k, below_x[k], below_xy[k : k + 1])
        for i in range(orb_ref.shape[0]):
            place(i + 1, k, orb_ref[i, k], below_y[i, k : k + 1])
    multiply(g, mats_ref, functools.partial(field_of, y_ref), w_ref)
    send_all(g, w_ref, sends)


def middle_kernel(*refs, g, first):
    w_old, *refs = refs
    received, refs = refs[:8], refs[8:]
    if first:
        now_ref, mats_ref, y_ref, w_ref, *sends = refs
    else:
        now_ref, older_ref, mats_ref, y_ref, w_ref, *sends = refs
    gain = (1.0 if first else 2.0) / filter_half
    for e in range(g.elements):
        for h in range(y_ref.shape[1]):
            value = gain * (w_old[e, h] - filter_center * now_ref[e, h])
            y_ref[e, h] = value if first else value - older_ref[e, h]
    add_all(g, y_ref, received, gain)
    multiply(g, mats_ref, functools.partial(field_of, y_ref), w_ref)
    if first:
        send_all(g, w_ref, sends)
        return

    def put_low(ref):
        def put(where, low, high):
            ref[where] = low

        return put

    put_x_face(g, w_ref, put_low(sends[0]))
    put_y_face(g, w_ref, put_low(sends[1]))
    for h in range(w_ref.shape[1]):
        for e3 in range(g.ez):
            rows = slice(e3 * g.side, (e3 + 1) * g.side)
            sends[2][rows, lanes(h)] = line(g, w_ref, 0, 0, e3, h)


def last_kernel(w_old, from_x, from_y, from_xy, now_ref, older_ref, out_ref, y_ref, *, g):
    side = g.side
    gain = 2.0 / filter_half
    for e in range(g.elements):
        for h in range(y_ref.shape[1]):
            value = gain * (w_old[e, h] - filter_center * now_ref[e, h])
            y_ref[e, h] = value - older_ref[e, h]
    p, q = lax.axis_index("dx"), lax.axis_index("dy")
    has_x, has_y = p < lax.axis_size("dx") - 1, q < lax.axis_size("dy") - 1
    add_x_face(g, y_ref, True, lambda w: jnp.where(has_x, from_x[w], 0.0), gain)
    add_y_face(g, y_ref, True, lambda w: jnp.where(has_y, from_y[w], 0.0), gain)
    add_line(g, y_ref, 1, 1, lambda w: jnp.where(has_x & has_y, from_xy[w], 0.0), gain)
    sub = lax.broadcasted_iota(jnp.int32, (side, LANES), 0)
    rest = 2 * g.deg - side
    for i in range(g.ex * g.deg):
        e1 = i // g.deg
        a = i + 1 - e1 * g.deg
        for k in range(g.nz):
            e3 = k // g.deg
            rows = g.rows(a, k + 1 - e3 * g.deg, 1)
            for h in range(y_ref.shape[1]):
                d0 = pltpu.roll(y_ref[g.at(e1, 0, e3), h, rows], side - 1, 0)
                d1 = pltpu.roll(y_ref[g.at(e1, 1, e3), h, rows], side - 2, 0)
                out_ref[i, k, :side, lanes(h)] = jnp.where(sub < g.deg, d0, d1)
                out_ref[i, k, side:, lanes(h)] = jnp.where(sub < rest, d1, 0.0)


def call(kernel, outs, scratch, operands, flops):
    size = sum(x.size * x.dtype.itemsize for x in (*operands, *outs))
    return pl.pallas_call(
        kernel,
        out_shape=outs,
        in_specs=[VMEM] * len(operands),
        out_specs=[VMEM] * len(outs),
        scratch_shapes=scratch,
        compiler_params=pltpu.CompilerParams(vmem_limit_bytes=LIMIT),
        cost_estimate=pl.CostEstimate(flops=flops, bytes_accessed=size, transcendentals=0),
    )(*operands)


def shards(orbitals, elem_mats, conn):
    nx, ny, nz, bands = orbitals.shape
    side = round(elem_mats.shape[-1] ** (1 / 3))
    g = Grid(elem_mats, side)
    f32 = jnp.float32
    orb = jnp.transpose(orbitals, (0, 2, 1, 3))
    below_x = offset(orb[-1], 1, 0)
    below_y = offset(orb[:, :, -1], 0, 1)
    below_xy = offset(orb[-1, :, -1], 1, 1)
    mats = renumber(conn, elem_mats, side, ny + 1, nz + 2)
    mats = mats.reshape(g.elements, g.count, g.count)

    nodes = (g.elements, bands // LANES, g.count, LANES)
    shape = jax.ShapeDtypeStruct
    x_shape = shape((nz, g.ey * side, bands), f32)
    y_shape = shape((g.ex * g.ez, side * side, bands), f32)
    line_shape = shape((g.ez * side, bands), f32)
    send_shapes = [x_shape] * 2 + [y_shape] * 2 + [line_shape] * 4
    pairings = [("A", "-"), ("B", "-"), ("-", "A"), ("-", "B")]
    pairings += [("A", "A"), ("A", "B"), ("B", "A"), ("B", "B")]
    flops = 2 * g.elements * g.count**2 * bands

    y0, w1, *sends = call(
        functools.partial(first_kernel, g=g),
        [shape(nodes, f32), shape(nodes, f32), *send_shapes],
        [],
        (orb, below_x, below_y, below_xy, mats),
        flops,
    )
    received = [pair_swap(s, *pair) for s, pair in zip(sends, pairings)]
    y1, w2, *sends = call(
        functools.partial(middle_kernel, g=g, first=True),
        [shape(nodes, f32), shape(nodes, f32), *send_shapes],
        [],
        (w1, *received, y0, mats),
        flops,
    )
    received = [pair_swap(s, *pair) for s, pair in zip(sends, pairings)]
    y2, w3, *sends = call(
        functools.partial(middle_kernel, g=g, first=False),
        [shape(nodes, f32), shape(nodes, f32), x_shape, y_shape, line_shape],
        [],
        (w2, *received, y1, y0, mats),
        flops,
    )
    received = [offset(s, *step) for s, step in zip(sends, ((-1, 0), (0, -1), (-1, -1)))]
    (y3,) = call(
        functools.partial(last_kernel, g=g),
        [shape((nx, nz, 2 * side, bands), f32)],
        [pltpu.VMEM(nodes, f32)],
        (w3, *received, y2, y1),
        flops // 100,
    )

    columns = y3.reshape(-1, bands)
    gram = jnp.einsum("rb,rc->bc", columns, columns, precision=lax.Precision.HIGHEST)
    gram = total(gram)
    lower = jnp.linalg.cholesky(gram)
    identity = jnp.eye(bands, dtype=f32)
    inverse_lower = lax.linalg.triangular_solve(lower, identity, left_side=True, lower=True)
    basis = jnp.einsum("rb,cb->rc", columns, inverse_lower, precision=lax.Precision.HIGHEST)
    scale = math.sqrt(nx * ny * nz * lax.axis_size(AXES))
    basis = (basis * scale).reshape(nx, nz, 2 * side, bands)[:, :, :ny]
    return jnp.transpose(basis, (0, 2, 1, 3))


def solution(mesh):
    in_specs = (
        P("dx", "dy", None, None),
        P("dx", "dy", None, None, None),
        P("dx", "dy", None, None),
    )
    out_specs = P("dx", "dy", None, None)
    return jax.shard_map(shards, mesh=mesh, in_specs=in_specs, out_specs=out_specs, check_vma=False)
```

time: 507 us -> 225 us (0.44); the launches traced: 498 us -> 223 us
  waiting for transfers between devices: 173 us -> 40.4 us
  local copies, waits for them, and re-layouts: 111 us -> 16.8 us
  other arithmetic: 143 us -> 56.1 us
  Pallas kernels: 0 us -> 39 us
  starting transfers between devices: 34.3 us -> 57.5 us
  between operations: 15.8 us -> 1.65 us
  matrix products: 21 us -> 12 us
    psum x1 -> x0, waiting for transfers between devices: 131 us -> none  [shards(): gram_total = lax.psum(gram_local, ('dx', 'dy'))]
    scatter-add x9 -> x0, other arithmetic: 72.3 us -> none  [the longest x3 72.1 us: apply_operator(): jnp.zeros((flat.shape[0], bands), jnp.float32).at[links]]
    gather x3 -> x0, local copies, waits for them, and re-layouts: 51.1 us -> none  [apply_operator(): rows = jnp.take(flat, links, axis=0).reshape(count, nodes, bands)]
    pallas_call x0 -> x5, Pallas kernels: none -> 39 us  [the longest x4 31.1 us: call(): pl.pallas_call(kernel, out_shape=outs, in_specs=[VMEM] * len(operands), o...]
    reshape x10 -> x0, local copies, waits for them, and re-layouts: 24.8 us -> none  [the longest x3 9.17 us: apply_operator(): summed = summed.reshape(width, width, depth, bands)]
    ppermute x12 -> x30, starting transfers between devices: 34.3 us -> 57.5 us  [the longest x16 29.3 us: pair_swap(): return lax.ppermute(value, AXES, route)]
    dot_general x3 -> x0, local copies, waits for them, and re-layouts: 16.2 us -> none  [apply_operator(): jnp.einsum('eij,ejb->eib', elem_mats.reshape(count, nodes, nodes), rows,...]
    dot_general x4 -> x1, matrix products: 15.9 us -> 4.9 us  [shards(): jnp.einsum('rb,rc->bc', columns, columns, precision=lax.Precision.HIGHEST)]
  transfers between devices with their start and end apart: 13 -> 30, of which waited for: 13 -> 13; matrix products, arithmetic and copies ran while one was open for 1% -> 0% of each run, Pallas kernels for 0% -> 4%
where the time goes in v1:
time: 225 us; the launch traced here: 223 us
  starting transfers between devices  57.5 us (26%)
  other arithmetic  56.1 us (25%)
  waiting for transfers between devices  40.4 us (18%)
  Pallas kernels  39 us (17%)
  local copies, waits for them, and re-layouts  16.8 us (7%)
  matrix products  12 us (5%)
    another operation x6, other arithmetic, shards(): lower = jnp.linalg.cholesky(gram)  34.1 us
    pallas_call x4, Pallas kernels, call(): pl.pallas_call(kernel, out_shape=outs, in_specs=[VMEM] * len(operands), o...  31.1 us
    ppermute x16, starting transfers between devices, pair_swap(): return lax.ppermute(value, AXES, route)  29.3 us
    another operation x3, other arithmetic, shards(): lax.linalg.triangular_solve(lower, identity, left_side=True, lower=True)  20.5 us
    ppermute x8, waiting for transfers between devices, xor_swap(): lax.ppermute(value, axis, [(i, i ^ bits) for i in range(lax.axis_size(axi...  17 us
    ppermute x6, starting transfers between devices, offset(): return lax.ppermute(value, AXES, route)  15.7 us
    ppermute x6, waiting for transfers between devices, offset(): return lax.ppermute(value, AXES, route)  12.4 us
    ppermute x8, starting transfers between devices, xor_swap(): lax.ppermute(value, axis, [(i, i ^ bits) for i in range(lax.axis_size(axi...  12.4 us
  transfers between devices with their start and end apart: 30, of which 13 were waited for; matrix products, arithmetic and copies ran while one was open for 0% of the time, Pallas kernels for 4%

profile of v1, /device:TPU:0, one launch (start us, length us, event | category | flops | bytes accessed | tf_op | source)
XLA Modules:
  0.0 223.4 jit_solution(8646623990500484318)
XLA Ops:
  0.0 2.0 copy.15
  2.0 4.9 %collective-permute-start = (bf16[13,14,256]{2,0,1:T(8,128)(2,1)S(1)}, bf16[13,14,256]{2,0,1:T(8,128)(2,1)S(1)}, u32[]{:S(2)}, u32[]{:S(2)}) collective-permute-start(bf16[13,14,256]{2,0,1:T(8,128)(2,1)S(1)} %slice_bitcast_fusion.2), channel_id=1, source_target_pairs={{0,8},{1,9},{2,10},{3,11},{4,12},{5,13},{6,14},{7,15},{8,16},{9,17... | collective-permute-start | bytes 279560 | tf_op jit(solution)/shard_map/ppermute | solution.py:44
  6.9 1.5 collective-permute-start.1
  8.4 5.3 %collective-permute-start.2 = (bf16[13,256]{1,0:T(8,128)(2,1)S(1)}, bf16[13,256]{1,0:T(8,128)(2,1)S(1)}, u32[]{:S(2)}, u32[]{:S(2)}) collective-permute-start(bf16[13,256]{1,0:T(8,128)(2,1)S(1)} %slice_bitcast_fusion.7), channel_id=1, source_target_pairs={{0,9},{1,10},{2,11},{3,12},{4,13},{5,14},{6,15},{8,17},{9,18},{10,... | collective-permute-start | bytes 19976 | tf_op jit(solution)/shard_map/ppermute | solution.py:44
  13.7 7.9 %renumber.1 = bf16[2,2,2,512,512]{4,3,2,1,0:T(8,128)(2,1)S(1)} custom-call(s32[2,2,2,512]{3,2,1,0:T(2,128)S(1)} %copy-done.4, bf16[2,2,2,512,512]{4,3,2,1,0:T(8,128)(2,1)} %mats_ref.1), custom_call_target="tpu_custom_call" | custom-call | flops 4294967296 | bytes 8388608 | tf_op jit(solution)/shard_map/renumber/pallas_call | solution.py:112
  21.6 1.9 copy-done
  23.7 6.6 %shard_map.37 = (f32[8,2,512,128]{3,2,1,0:T(8,128)}, f32[8,2,512,128]{3,2,1,0:T(8,128)}, f32[13,16,256]{2,1,0:T(8,128)S(1)}, f32[13,16,256]{2,1,0:T(8,128)S(1)},...) custom-call(bf16[14,13,14,256]{3,2,1,0:T(8,128)(2,1)S(1)} %bitcast.5, ...), custom_call_target="tpu_custom_call" | custom-call | flops 1073741824 | bytes 15096320 | tf_op jit(solution)/shard_map/pallas_call | solution.py:413
  30.9 1.6 collective-permute-start.3
  33.9 11.4 %collective-permute-start.7 = (f32[16,256]{1,0:T(8,128)S(1)}, f32[16,256]{1,0:T(8,128)S(1)}, u32[]{:S(2)}, u32[]{:S(2)}) collective-permute-start(f32[16,256]{1,0:T(8,128)S(1)} %get-tuple-element.35), channel_id=1, source_target_pairs={{0,9},{1,8},{2,11},{3,10},{4,13},{5,12},{6,15},{7,14},{8,1},{9,0},... | collective-permute-start | bytes 49160 | tf_op jit(solution)/shard_map/ppermute | solution.py:33
  45.3 1.4 collective-permute-done.7.refs_5_
  46.8 3.7 %collective-permute-done.8.refs_6_ = f32[16,256]{1,0:T(8,128)S(1)} collective-permute-done((f32[16,256]{1,0:T(8,128)S(1)}, f32[16,256]{1,0:T(8,128)S(1)}, u32[]{:S(2)}, u32[]{:S(2)}) %collective-permute-start.8) | collective-permute-done | bytes 16416 | tf_op jit(solution)/shard_map/ppermute | solution.py:33
  50.5 1.2 collective-permute-done.9.refs_7_
  51.7 8.6 %shard_map.38 = (f32[8,2,512,128]{3,2,1,0:T(8,128)S(1)}, f32[8,2,512,128]{3,2,1,0:T(8,128)}, f32[13,16,256]{2,1,0:T(8,128)S(1)}, f32[13,16,256]{2,1,0:T(8,128)S(...) custom-call(f32[8,2,512,128]{3,2,1,0:T(8,128)} %get-tuple-element.30, ...), custom_call_target="tpu_custom_call" | custom-call | flops 1073741824 | bytes 23003136 | tf_op jit(solution)/shard_map/pallas_call | solution.py:413
  60.3 2.0 copy-done.1
  63.2 4.3 %collective-permute-start.11 = (f32[13,16,256]{2,1,0:T(8,128)S(1)}, f32[13,16,256]{2,1,0:T(8,128)S(1)}, u32[]{:S(2)}, u32[]{:S(2)}) collective-permute-start(f32[13,16,256]{2,1,0:T(8,128)S(1)} %get-tuple-element.41), channel_id=1, source_target_pairs={{0,8},{1,9},{2,10},{3,11},{4,12},{5,13},{6,14},{7,15},{8,0},{9,1},... | collective-permute-start | bytes 638984 | tf_op jit(solution)/shard_map/ppermute | solution.py:33
  68.2 4.8 %collective-permute-start.15 = (f32[16,256]{1,0:T(8,128)S(1)}, f32[16,256]{1,0:T(8,128)S(1)}, u32[]{:S(2)}, u32[]{:S(2)}) collective-permute-start(f32[16,256]{1,0:T(8,128)S(1)} %get-tuple-element.45), channel_id=1, source_target_pairs={{0,9},{1,8},{2,11},{3,10},{4,13},{5,12},{6,15},{7,14},{8,1},{9,0},... | collective-permute-start | bytes 49160 | tf_op jit(solution)/shard_map/ppermute | solution.py:33
  72.9 1.4 collective-permute-done.15.refs_5_
  74.4 1.4 collective-permute-start.16
  75.8 2.3 %collective-permute-done.16.refs_6_ = f32[16,256]{1,0:T(8,128)S(1)} collective-permute-done((f32[16,256]{1,0:T(8,128)S(1)}, f32[16,256]{1,0:T(8,128)S(1)}, u32[]{:S(2)}, u32[]{:S(2)}) %collective-permute-start.16) | collective-permute-done | bytes 16416 | tf_op jit(solution)/shard_map/ppermute | solution.py:33
  78.1 1.7 collective-permute-start.17
  81.3 10.1 %shard_map.39 = (f32[8,2,512,128]{3,2,1,0:T(8,128)S(1)}, f32[8,2,512,128]{3,2,1,0:T(8,128)}, f32[13,16,256]{2,1,0:T(8,128)S(1)}, f32[4,64,256]{2,1,0:T(8,128)S(1)}, f32[16,256]{1,0:T(8,128)S(1)}) custom-call(f32[8,2,512,128]{3,2,1,0:T(8,128)} %get-tuple-element.40.refs_0_, f32[13,16,256]{2,1,0:T(8,128)S(1)} %collective-permute-done.11.refs_1_, ...), custom_call_target="tpu_custom_call" | custom-call | flops 1073741824 | bytes 26673152 | tf_op jit(solution)/shard_map/pallas_call | solution.py:413
  91.5 2.0 copy-done.3
  93.4 1.3 collective-permute-start.20
  94.7 1.3 collective-permute-start.19
  96.0 1.5 collective-permute-start.21
  97.5 12.4 %collective-permute-done.21.from_xy = f32[16,256]{1,0:T(8,128)S(1)} collective-permute-done((f32[16,256]{1,0:T(8,128)S(1)}, f32[16,256]{1,0:T(8,128)S(1)}, u32[]{:S(2)}, u32[]{:S(2)}) %collective-permute-start.21) | collective-permute-done | bytes 16416 | tf_op jit(solution)/shard_map/ppermute | solution.py:44
  109.9 5.7 %shard_map.40 = f32[14,13,16,256]{3,2,1,0:T(8,128)S(1)} custom-call(f32[8,2,512,128]{3,2,1,0:T(8,128)} %get-tuple-element.50.w_old, f32[13,16,256]{2,1,0:T(8,128)S(1)} %collective-permute-done.19.from_x, f32[4,64,256]{2,1,0:T(8,128)S(1)} %collective-permute-done.20.from_y, f32[16,256]{1,0:T(8,128)S(1)} %collective-permute-done.21.from_xy, ...), custom_call_target="tpu_custom_call" | custom-call | flops 10737418 | bytes 16056320 | tf_op jit(solution)/shard_map/pallas_call | solution.py:413
  115.7 4.9 %convolution_bitcast_fusion = f32[256,256]{0,1:T(8,128)S(1)} fusion(f32[14,13,16,256]{3,2,1,0:T(8,128)S(1)} %shard_map.40), kind=kOutput, calls=%fused_computation.5 | convolution fusion | flops 2290089984 | bytes 3244032 | tf_op jit(solution)/shard_map/rb,rc->bc/dot_general | solution.py:479
  120.6 2.5 %collective-permute-start.22 = (f32[128,256]{0,1:T(8,128)S(1)}, f32[128,256]{0,1:T(8,128)S(1)}, u32[]{:S(2)}, u32[]{:S(2)}) collective-permute-start(f32[128,256]{0,1:T(8,128)S(1)} %constant_dynamic-slice_fusion.1), channel_id=1, source_target_pairs={{0,1},{1,0},{2,3},{3,2},{4,5},{5,4},{6,7},{7,6},{8,9},{9,8},{10,11... | collective-permute-start | bytes 393224 | tf_op jit(solution)/shard_map/ppermute | solution.py:48
  124.1 2.4 %collective-permute-start.23 = (f32[128,256]{0,1:T(8,128)S(1)}, f32[128,256]{0,1:T(8,128)S(1)}, u32[]{:S(2)}, u32[]{:S(2)}) collective-permute-start(f32[128,256]{0,1:T(8,128)S(1)} %dynamic-slice_add_fusion), channel_id=1, source_target_pairs={{0,8},{8,0},{16,24},{24,16},{1,9},{9,1},{17,25},{25,17},{2,10},{10... | collective-permute-start | bytes 393224 | tf_op jit(solution)/shard_map/ppermute | solution.py:48
  127.4 1.6 collective-permute-start.25
  128.9 3.6 %collective-permute-done.23 = f32[128,256]{0,1:T(8,128)S(1)} collective-permute-done((f32[128,256]{0,1:T(8,128)S(1)}, f32[128,256]{0,1:T(8,128)S(1)}, u32[]{:S(2)}, u32[]{:S(2)}) %collective-permute-start.23) | collective-permute-done | bytes 131104 | tf_op jit(solution)/shard_map/ppermute | solution.py:48
  132.5 6.9 %collective-permute-done.24 = f32[128,256]{0,1:T(8,128)S(1)} collective-permute-done((f32[128,256]{0,1:T(8,128)S(1)}, f32[128,256]{0,1:T(8,128)S(1)}, u32[]{:S(2)}, u32[]{:S(2)}) %collective-permute-start.24) | collective-permute-done | bytes 131104 | tf_op jit(solution)/shard_map/ppermute | solution.py:48
  139.4 3.5 %collective-permute-start.26 = (f32[128,256]{0,1:T(8,128)S(1)}, f32[128,256]{0,1:T(8,128)S(1)}, u32[]{:S(2)}, u32[]{:S(2)}) collective-permute-start(f32[128,256]{0,1:T(8,128)S(1)} %add_add_fusion.1), channel_id=1, source_target_pairs={{0,2},{1,3},{2,0},{3,1},{4,6},{5,7},{6,4},{7,5},{8,10},{9,11},{10,... | collective-permute-start | bytes 393224 | tf_op jit(solution)/shard_map/ppermute | solution.py:48
  142.9 1.5 collective-permute-start.28
  144.5 2.5 %collective-permute-done.26 = f32[128,256]{0,1:T(8,128)S(1)} collective-permute-done((f32[128,256]{0,1:T(8,128)S(1)}, f32[128,256]{0,1:T(8,128)S(1)}, u32[]{:S(2)}, u32[]{:S(2)}) %collective-permute-start.26) | collective-permute-done | bytes 131104 | tf_op jit(solution)/shard_map/ppermute | solution.py:48
  147.0 2.3 %collective-permute-done.27 = f32[128,256]{0,1:T(8,128)S(1)} collective-permute-done((f32[128,256]{0,1:T(8,128)S(1)}, f32[128,256]{0,1:T(8,128)S(1)}, u32[]{:S(2)}, u32[]{:S(2)}) %collective-permute-start.27) | collective-permute-done | bytes 131104 | tf_op jit(solution)/shard_map/ppermute | solution.py:48
  151.5 1.1 copy.9
  153.3 11.7 %cholesky.50 = f32[128,128]{1,0:T(8,128)S(1)} custom-call(f32[128,128]{1,0:T(8,128)S(1)} %cholesky.118), custom_call_target="Cholesky" | custom-call | tf_op jit(solution)/shard_map/jit(cholesky)/cholesky | solution.py:481
  165.1 10.0 %custom-call.14 = f32[1,128,128]{1,2,0:T(8,128)S(1)} custom-call(f32[1,128,128]{2,1,0:T(8,128)S(1)} %get-tuple-element.78), custom_call_target="InvertDiagBlocksLowerTriangular" | custom-call | tf_op jit(solution)/shard_map/jit(cholesky)/cholesky | solution.py:481
  176.2 1.1 convolution_subtract_fusion.1
  177.3 11.7 %cholesky.105 = f32[128,128]{1,0:T(8,128)S(1)} custom-call(f32[128,128]{1,0:T(8,128)S(1)} %convolution_subtract_fusion.1), custom_call_target="Cholesky" | custom-call | tf_op jit(solution)/shard_map/jit(cholesky)/cholesky | solution.py:481
  191.0 5.0 %while.1 = (s32[]{:T(128)}, f32[256,256]{1,0:T(8,128)S(1)}, s32[2,2]{1,0:T(2,128)S(1)}, f32[2,128,128]{2,1,0:T(8,128)}, s32[]{:T(128)}) while((s32[]{:T(128)}, f32[256,256]{1,0:T(8,128)S(1)}, s32[2,2]{1,0:T(2,128)S(1)}, f32[2,128,128]{2,1,0:T(8,128)}, s32[]{:T(128)}) %tuple.24), condition=%wide.while_cond, body=%wide.while_body.sunk | while | flops 2 | bytes 132705 | solution.py:483
  191.6 1.9 bitcast_dynamic-update-slice_fusion.2
  194.1 1.9 bitcast_dynamic-update-slice_fusion.2
  196.0 20.5 %custom-call.15 = f32[2,128,128]{1,2,0:T(8,128)S(1)} custom-call(f32[2,128,128]{2,1,0:T(8,128)} %get-tuple-element.62), custom_call_target="InvertDiagBlocksLowerTriangular" | custom-call | tf_op jit(solution)/shard_map/triangular_solve | solution.py:483
  218.8 2.7 %convolution_multiply_fusion = f32[2912,256]{1,0:T(8,128)S(1)} fusion(f32[2912,256]{1,0:T(8,128)S(1)} %bitcast.53, f32[128,256]{1,0:T(8,128)S(1)} %fusion.7, f32[128,256]{1,0:T(8,128)S(1)} %fusion.4), kind=kOutput, calls=%fused_computation.2 | convolution fusion | flops 2290900992 | bytes 6225920 | tf_op jit(solution)/shard_map/rb,cb->rc/dot_general | solution.py:484
  221.5 1.9 slice_bitcast_fusion
  (71 shorter events, 15.3 us)
Async XLA Ops:
  0.0 13.7 %copy-start.4 = (s32[2,2,2,512]{3,2,1,0:T(2,128)S(1)}, s32[2,2,2,512]{3,2,1,0:T(2,128)}, u32[]{:S(2)}) copy-start(s32[2,2,2,512]{3,2,1,0:T(2,128)} %conn_ref.1) | copy-start | bytes 49156
  2.0 21.6 %collective-permute-start = (bf16[13,14,256]{2,0,1:T(8,128)(2,1)S(1)}, bf16[13,14,256]{2,0,1:T(8,128)(2,1)S(1)}, u32[]{:S(2)}, u32[]{:S(2)}) collective-permute-start(bf16[13,14,256]{2,0,1:T(8,128)(2,1)S(1)} %slice_bitcast_fusion.2), channel_id=1, source_target_pairs={{0,8},{1,9},{2,10},{3,11},{4,12},{5,13},{6,14},{7,15},{8,16},{9,17... | collective-permute-start | bytes 279560 | tf_op jit(solution)/shard_map/ppermute | solution.py:44
  6.9 16.7 %collective-permute-start.1 = (bf16[14,13,256]{2,1,0:T(8,128)(2,1)S(1)}, bf16[14,13,256]{2,1,0:T(8,128)(2,1)S(1)}, u32[]{:S(2)}, u32[]{:S(2)}) collective-permute-start(bf16[14,13,256]{2,1,0:T(8,128)(2,1)S(1)} %slice_bitcast_fusion.1), channel_id=1, source_target_pairs={{0,1},{1,2},{2,3},{3,4},{4,5},{5,6},{6,7},{8,9},{9,10},{10,11},{11... | collective-permute-start | bytes 279560 | tf_op jit(solution)/shard_map/ppermute | solution.py:44
  8.4 15.2 %copy-start.2 = (bf16[14,14,13,256]{3,1,2,0:T(8,128)(2,1)S(1)}, bf16[14,14,13,256]{3,1,2,0:T(8,128)(2,1)}, u32[]{:S(2)}) copy-start(bf16[14,14,13,256]{3,1,2,0:T(8,128)(2,1)} %param.3) | copy-start | bytes 3913732
  8.4 15.2 %collective-permute-start.2 = (bf16[13,256]{1,0:T(8,128)(2,1)S(1)}, bf16[13,256]{1,0:T(8,128)(2,1)S(1)}, u32[]{:S(2)}, u32[]{:S(2)}) collective-permute-start(bf16[13,256]{1,0:T(8,128)(2,1)S(1)} %slice_bitcast_fusion.7), channel_id=1, source_target_pairs={{0,9},{1,10},{2,11},{3,12},{4,13},{5,14},{6,15},{8,17},{9,18},{10,... | collective-permute-start | bytes 19976 | tf_op jit(solution)/shard_map/ppermute | solution.py:44
  21.6 2.0 copy-start
  30.2 21.4 %collective-permute-start.5 = (f32[4,64,256]{2,1,0:T(8,128)S(1)}, f32[4,64,256]{2,1,0:T(8,128)S(1)}, u32[]{:S(2)}, u32[]{:S(2)}) collective-permute-start(f32[4,64,256]{2,1,0:T(8,128)S(1)} %get-tuple-element.33), channel_id=1, source_target_pairs={{0,1},{1,0},{2,3},{3,2},{4,5},{5,4},{6,7},{7,6},{8,9},{9,8},{10,11... | collective-permute-start | bytes 786440 | tf_op jit(solution)/shard_map/ppermute | solution.py:33
  30.2 21.4 %collective-permute-start.6 = (f32[4,64,256]{2,1,0:T(8,128)S(1)}, f32[4,64,256]{2,1,0:T(8,128)S(1)}, u32[]{:S(2)}, u32[]{:S(2)}) collective-permute-start(f32[4,64,256]{2,1,0:T(8,128)S(1)} %get-tuple-element.34), channel_id=1, source_target_pairs={{0,0},{1,2},{2,1},{3,4},{4,3},{5,6},{6,5},{7,7},{8,8},{9,10},{10,9... | collective-permute-start | bytes 786440 | tf_op jit(solution)/shard_map/ppermute | solution.py:33
  30.9 20.8 %collective-permute-start.3 = (f32[13,16,256]{2,1,0:T(8,128)S(1)}, f32[13,16,256]{2,1,0:T(8,128)S(1)}, u32[]{:S(2)}, u32[]{:S(2)}) collective-permute-start(f32[13,16,256]{2,1,0:T(8,128)S(1)} %get-tuple-element.31), channel_id=1, source_target_pairs={{0,8},{1,9},{2,10},{3,11},{4,12},{5,13},{6,14},{7,15},{8,0},{9,1},... | collective-permute-start | bytes 638984 | tf_op jit(solution)/shard_map/ppermute | solution.py:33
  32.6 19.1 %collective-permute-start.4 = (f32[13,16,256]{2,1,0:T(8,128)S(1)}, f32[13,16,256]{2,1,0:T(8,128)S(1)}, u32[]{:S(2)}, u32[]{:S(2)}) collective-permute-start(f32[13,16,256]{2,1,0:T(8,128)S(1)} %get-tuple-element.32), channel_id=1, source_target_pairs={{0,0},{1,1},{2,2},{3,3},{4,4},{5,5},{6,6},{7,7},{8,16},{9,17},{10,... | collective-permute-start | bytes 638984 | tf_op jit(solution)/shard_map/ppermute | solution.py:33
  33.2 0.7 collective-permute-start.10
  33.9 12.8 %collective-permute-start.7 = (f32[16,256]{1,0:T(8,128)S(1)}, f32[16,256]{1,0:T(8,128)S(1)}, u32[]{:S(2)}, u32[]{:S(2)}) collective-permute-start(f32[16,256]{1,0:T(8,128)S(1)} %get-tuple-element.35), channel_id=1, source_target_pairs={{0,9},{1,8},{2,11},{3,10},{4,13},{5,12},{6,15},{7,14},{8,1},{9,0},... | collective-permute-start | bytes 49160 | tf_op jit(solution)/shard_map/ppermute | solution.py:33
  46.7 3.7 %collective-permute-start.8 = (f32[16,256]{1,0:T(8,128)S(1)}, f32[16,256]{1,0:T(8,128)S(1)}, u32[]{:S(2)}, u32[]{:S(2)}) collective-permute-start(f32[16,256]{1,0:T(8,128)S(1)} %get-tuple-element.36), channel_id=1, source_target_pairs={{0,8},{1,10},{2,9},{3,12},{4,11},{5,14},{6,13},{7,15},{8,0},{9,2},... | collective-permute-start | bytes 49160 | tf_op jit(solution)/shard_map/ppermute | solution.py:33
  50.5 1.2 collective-permute-start.9
  60.3 2.0 copy-start.1
  62.3 19.0 %collective-permute-start.13 = (f32[4,64,256]{2,1,0:T(8,128)S(1)}, f32[4,64,256]{2,1,0:T(8,128)S(1)}, u32[]{:S(2)}, u32[]{:S(2)}) collective-permute-start(f32[4,64,256]{2,1,0:T(8,128)S(1)} %get-tuple-element.43), channel_id=1, source_target_pairs={{0,1},{1,0},{2,3},{3,2},{4,5},{5,4},{6,7},{7,6},{8,9},{9,8},{10,11... | collective-permute-start | bytes 786440 | tf_op jit(solution)/shard_map/ppermute | solution.py:33
  62.5 18.8 %collective-permute-start.14 = (f32[4,64,256]{2,1,0:T(8,128)S(1)}, f32[4,64,256]{2,1,0:T(8,128)S(1)}, u32[]{:S(2)}, u32[]{:S(2)}) collective-permute-start(f32[4,64,256]{2,1,0:T(8,128)S(1)} %get-tuple-element.44), channel_id=1, source_target_pairs={{0,0},{1,2},{2,1},{3,4},{4,3},{5,6},{6,5},{7,7},{8,8},{9,10},{10,9... | collective-permute-start | bytes 786440 | tf_op jit(solution)/shard_map/ppermute | solution.py:33
  63.2 18.1 %collective-permute-start.11 = (f32[13,16,256]{2,1,0:T(8,128)S(1)}, f32[13,16,256]{2,1,0:T(8,128)S(1)}, u32[]{:S(2)}, u32[]{:S(2)}) collective-permute-start(f32[13,16,256]{2,1,0:T(8,128)S(1)} %get-tuple-element.41), channel_id=1, source_target_pairs={{0,8},{1,9},{2,10},{3,11},{4,12},{5,13},{6,14},{7,15},{8,0},{9,1},... | collective-permute-start | bytes 638984 | tf_op jit(solution)/shard_map/ppermute | solution.py:33
  67.5 13.8 %collective-permute-start.12 = (f32[13,16,256]{2,1,0:T(8,128)S(1)}, f32[13,16,256]{2,1,0:T(8,128)S(1)}, u32[]{:S(2)}, u32[]{:S(2)}) collective-permute-start(f32[13,16,256]{2,1,0:T(8,128)S(1)} %get-tuple-element.42), channel_id=1, source_target_pairs={{0,0},{1,1},{2,2},{3,3},{4,4},{5,5},{6,6},{7,7},{8,16},{9,17},{10,... | collective-permute-start | bytes 638984 | tf_op jit(solution)/shard_map/ppermute | solution.py:33
  68.2 6.2 %collective-permute-start.15 = (f32[16,256]{1,0:T(8,128)S(1)}, f32[16,256]{1,0:T(8,128)S(1)}, u32[]{:S(2)}, u32[]{:S(2)}) collective-permute-start(f32[16,256]{1,0:T(8,128)S(1)} %get-tuple-element.45), channel_id=1, source_target_pairs={{0,9},{1,8},{2,11},{3,10},{4,13},{5,12},{6,15},{7,14},{8,1},{9,0},... | collective-permute-start | bytes 49160 | tf_op jit(solution)/shard_map/ppermute | solution.py:33
  74.4 3.7 %collective-permute-start.16 = (f32[16,256]{1,0:T(8,128)S(1)}, f32[16,256]{1,0:T(8,128)S(1)}, u32[]{:S(2)}, u32[]{:S(2)}) collective-permute-start(f32[16,256]{1,0:T(8,128)S(1)} %get-tuple-element.46), channel_id=1, source_target_pairs={{0,8},{1,10},{2,9},{3,12},{4,11},{5,14},{6,13},{7,15},{8,0},{9,2},... | collective-permute-start | bytes 49160 | tf_op jit(solution)/shard_map/ppermute | solution.py:33
  78.1 2.5 %collective-permute-start.17 = (f32[16,256]{1,0:T(8,128)S(1)}, f32[16,256]{1,0:T(8,128)S(1)}, u32[]{:S(2)}, u32[]{:S(2)}) collective-permute-start(f32[16,256]{1,0:T(8,128)S(1)} %get-tuple-element.47), channel_id=1, source_target_pairs={{0,1},{1,0},{2,3},{3,2},{4,5},{5,4},{6,7},{7,6},{8,17},{9,16},{10,... | collective-permute-start | bytes 49160 | tf_op jit(solution)/shard_map/ppermute | solution.py:33
  80.6 0.7 collective-permute-start.18
  91.5 2.0 copy-start.3
  93.4 16.5 %collective-permute-start.20 = (f32[4,64,256]{2,1,0:T(8,128)S(1)}, f32[4,64,256]{2,1,0:T(8,128)S(1)}, u32[]{:S(2)}, u32[]{:S(2)}) collective-permute-start(f32[4,64,256]{2,1,0:T(8,128)S(1)} %get-tuple-element.52), channel_id=1, source_target_pairs={{1,0},{2,1},{3,2},{4,3},{5,4},{6,5},{7,6},{9,8},{10,9},{11,10},{12... | collective-permute-start | bytes 786440 | tf_op jit(solution)/shard_map/ppermute | solution.py:44
  94.7 15.2 %collective-permute-start.19 = (f32[13,16,256]{2,1,0:T(8,128)S(1)}, f32[13,16,256]{2,1,0:T(8,128)S(1)}, u32[]{:S(2)}, u32[]{:S(2)}) collective-permute-start(f32[13,16,256]{2,1,0:T(8,128)S(1)} %get-tuple-element.51), channel_id=1, source_target_pairs={{8,0},{9,1},{10,2},{11,3},{12,4},{13,5},{14,6},{15,7},{16,8},{17,9... | collective-permute-start | bytes 638984 | tf_op jit(solution)/shard_map/ppermute | solution.py:44
  96.0 13.9 %collective-permute-start.21 = (f32[16,256]{1,0:T(8,128)S(1)}, f32[16,256]{1,0:T(8,128)S(1)}, u32[]{:S(2)}, u32[]{:S(2)}) collective-permute-start(f32[16,256]{1,0:T(8,128)S(1)} %get-tuple-element.53), channel_id=1, source_target_pairs={{9,0},{10,1},{11,2},{12,3},{13,4},{14,5},{15,6},{17,8},{18,9},{19,... | collective-permute-start | bytes 49160 | tf_op jit(solution)/shard_map/ppermute | solution.py:44
  120.6 3.4 %collective-permute-start.22 = (f32[128,256]{0,1:T(8,128)S(1)}, f32[128,256]{0,1:T(8,128)S(1)}, u32[]{:S(2)}, u32[]{:S(2)}) collective-permute-start(f32[128,256]{0,1:T(8,128)S(1)} %constant_dynamic-slice_fusion.1), channel_id=1, source_target_pairs={{0,1},{1,0},{2,3},{3,2},{4,5},{5,4},{6,7},{7,6},{8,9},{9,8},{10,11... | collective-permute-start | bytes 393224 | tf_op jit(solution)/shard_map/ppermute | solution.py:48
  124.1 8.4 %collective-permute-start.23 = (f32[128,256]{0,1:T(8,128)S(1)}, f32[128,256]{0,1:T(8,128)S(1)}, u32[]{:S(2)}, u32[]{:S(2)}) collective-permute-start(f32[128,256]{0,1:T(8,128)S(1)} %dynamic-slice_add_fusion), channel_id=1, source_target_pairs={{0,8},{8,0},{16,24},{24,16},{1,9},{9,1},{17,25},{25,17},{2,10},{10... | collective-permute-start | bytes 393224 | tf_op jit(solution)/shard_map/ppermute | solution.py:48
  126.5 12.9 %collective-permute-start.24 = (f32[128,256]{0,1:T(8,128)S(1)}, f32[128,256]{0,1:T(8,128)S(1)}, u32[]{:S(2)}, u32[]{:S(2)}) collective-permute-start(f32[128,256]{0,1:T(8,128)S(1)} %dynamic-slice_add_fusion), channel_id=1, source_target_pairs={{0,16},{8,24},{16,0},{24,8},{1,17},{9,25},{17,1},{25,9},{2,18},{10... | collective-permute-start | bytes 393224 | tf_op jit(solution)/shard_map/ppermute | solution.py:48
  127.4 12.0 %collective-permute-start.25 = (f32[128,256]{0,1:T(8,128)S(1)}, f32[128,256]{0,1:T(8,128)S(1)}, u32[]{:S(2)}, u32[]{:S(2)}) collective-permute-start(f32[128,256]{0,1:T(8,128)S(1)} %dynamic-slice_add_fusion), channel_id=1, source_target_pairs={{0,24},{8,16},{16,8},{24,0},{1,25},{9,17},{17,9},{25,1},{2,26},{10... | collective-permute-start | bytes 393224 | tf_op jit(solution)/shard_map/ppermute | solution.py:48
  139.4 7.5 %collective-permute-start.26 = (f32[128,256]{0,1:T(8,128)S(1)}, f32[128,256]{0,1:T(8,128)S(1)}, u32[]{:S(2)}, u32[]{:S(2)}) collective-permute-start(f32[128,256]{0,1:T(8,128)S(1)} %add_add_fusion.1), channel_id=1, source_target_pairs={{0,2},{1,3},{2,0},{3,1},{4,6},{5,7},{6,4},{7,5},{8,10},{9,11},{10,... | collective-permute-start | bytes 393224 | tf_op jit(solution)/shard_map/ppermute | solution.py:48
  142.9 6.4 %collective-permute-start.27 = (f32[128,256]{0,1:T(8,128)S(1)}, f32[128,256]{0,1:T(8,128)S(1)}, u32[]{:S(2)}, u32[]{:S(2)}) collective-permute-start(f32[128,256]{0,1:T(8,128)S(1)} %add_add_fusion.1), channel_id=1, source_target_pairs={{0,4},{1,5},{2,6},{3,7},{4,0},{5,1},{6,2},{7,3},{8,12},{9,13},{10,... | collective-permute-start | bytes 393224 | tf_op jit(solution)/shard_map/ppermute | solution.py:48
  142.9 6.4 %collective-permute-start.28 = (f32[128,256]{0,1:T(8,128)S(1)}, f32[128,256]{0,1:T(8,128)S(1)}, u32[]{:S(2)}, u32[]{:S(2)}) collective-permute-start(f32[128,256]{0,1:T(8,128)S(1)} %add_add_fusion.1), channel_id=1, source_target_pairs={{0,6},{1,7},{2,4},{3,5},{4,2},{5,3},{6,0},{7,1},{8,14},{9,15},{10,... | collective-permute-start | bytes 393224 | tf_op jit(solution)/shard_map/ppermute | solution.py:48
  149.3 1.4 collective-permute-start.29
  152.6 0.7 copy-start.5

commit v2 on v1

--- a/solution.py
+++ b/solution.py
@@ -10,10 +10,13 @@
 
 filter_center = 1.5
 filter_half = 4.0
+FIRST = 1.0 / filter_half
+LATER = 2.0 / filter_half
 AXES = ("dx", "dy")
 VMEM = pl.BlockSpec(memory_space=pltpu.VMEM)
-LIMIT = 48 * 1024 * 1024
+LIMIT = 12 * 1024 * 1024
 LANES = 128
+ROWS = 8
 
 
 def partner(index, size, pairing):
@@ -33,13 +36,12 @@
     return lax.ppermute(value, AXES, route)
 
 
-def offset(value, step_x, step_y):
+def ring(value, step_x, step_y):
     size_x, size_y = lax.axis_size("dx"), lax.axis_size("dy")
     route = [
-        (p * size_y + q, (p + step_x) * size_y + q + step_y)
+        (p * size_y + q, (p + step_x) % size_x * size_y + (q + step_y) % size_y)
         for p in range(size_x)
         for q in range(size_y)
-        if 0 <= p + step_x < size_x and 0 <= q + step_y < size_y
     ]
     return lax.ppermute(value, AXES, route)
 
@@ -312,7 +314,7 @@
 
 
 def first_kernel(*refs, g):
-    orb_ref, below_x, below_y, below_xy, mats_ref, y_ref, w_ref, *sends = refs
+    orb_ref, below_x, below_y, below_xy, mats_ref, y_ref, next_ref, *sends = refs
     side = g.side
     halves = range(y_ref.shape[1])
     sub = lax.broadcasted_iota(jnp.int32, (side, LANES), 0)
@@ -345,27 +347,36 @@
         place(0, k, below_x[k], below_xy[k : k + 1])
         for i in range(orb_ref.shape[0]):
             place(i + 1, k, orb_ref[i, k], below_y[i, k : k + 1])
-    multiply(g, mats_ref, functools.partial(field_of, y_ref), w_ref)
-    send_all(g, w_ref, sends)
-
-
-def middle_kernel(*refs, g, first):
-    w_old, *refs = refs
+    multiply(g, mats_ref, functools.partial(field_of, y_ref), next_ref)
+    send_all(g, next_ref, sends)
+    advance(next_ref, y_ref, None, FIRST)
+
+
+def advance(next_ref, now_ref, older_ref, gain):
+    for e in range(next_ref.shape[0]):
+        for h in range(next_ref.shape[1]):
+            value = gain * (next_ref[e, h] - filter_center * now_ref[e, h])
+            next_ref[e, h] = value if older_ref is None else value - older_ref[e, h]
+
+
+def middle_kernel(*refs, g):
+    part_ref, *refs = refs
     received, refs = refs[:8], refs[8:]
-    if first:
-        now_ref, mats_ref, y_ref, w_ref, *sends = refs
-    else:
-        now_ref, older_ref, mats_ref, y_ref, w_ref, *sends = refs
-    gain = (1.0 if first else 2.0) / filter_half
-    for e in range(g.elements):
-        for h in range(y_ref.shape[1]):
-            value = gain * (w_old[e, h] - filter_center * now_ref[e, h])
-            y_ref[e, h] = value if first else value - older_ref[e, h]
-    add_all(g, y_ref, received, gain)
-    multiply(g, mats_ref, functools.partial(field_of, y_ref), w_ref)
-    if first:
-        send_all(g, w_ref, sends)
-        return
+    older_ref, mats_ref, y_ref, next_ref, *sends = refs
+    y_ref[...] = part_ref[...]
+    add_all(g, y_ref, received, FIRST)
+    multiply(g, mats_ref, functools.partial(field_of, y_ref), next_ref)
+    send_all(g, next_ref, sends)
+    advance(next_ref, y_ref, older_ref, LATER)
+
+
+def late_kernel(*refs, g):
+    part_ref, *refs = refs
+    received, refs = refs[:8], refs[8:]
+    older_ref, mats_ref, next_ref, *sends, y_ref = refs
+    y_ref[...] = part_ref[...]
+    add_all(g, y_ref, received, LATER)
+    multiply(g, mats_ref, functools.partial(field_of, y_ref), next_ref)
 
     def put_low(ref):
         def put(where, low, high):
@@ -373,26 +384,23 @@
 
         return put
 
-    put_x_face(g, w_ref, put_low(sends[0]))
-    put_y_face(g, w_ref, put_low(sends[1]))
-    for h in range(w_ref.shape[1]):
+    put_x_face(g, next_ref, put_low(sends[0]))
+    put_y_face(g, next_ref, put_low(sends[1]))
+    for h in range(next_ref.shape[1]):
         for e3 in range(g.ez):
             rows = slice(e3 * g.side, (e3 + 1) * g.side)
-            sends[2][rows, lanes(h)] = line(g, w_ref, 0, 0, e3, h)
-
-
-def last_kernel(w_old, from_x, from_y, from_xy, now_ref, older_ref, out_ref, y_ref, *, g):
+            sends[2][rows, lanes(h)] = line(g, next_ref, 0, 0, e3, h)
+    advance(next_ref, y_ref, older_ref, LATER)
+
+
+def last_kernel(part_ref, from_x, from_y, from_xy, out_ref, y_ref, *, g):
     side = g.side
-    gain = 2.0 / filter_half
-    for e in range(g.elements):
-        for h in range(y_ref.shape[1]):
-            value = gain * (w_old[e, h] - filter_center * now_ref[e, h])
-            y_ref[e, h] = value - older_ref[e, h]
+    y_ref[...] = part_ref[...]
     p, q = lax.axis_index("dx"), lax.axis_index("dy")
     has_x, has_y = p < lax.axis_size("dx") - 1, q < lax.axis_size("dy") - 1
-    add_x_face(g, y_ref, True, lambda w: jnp.where(has_x, from_x[w], 0.0), gain)
-    add_y_face(g, y_ref, True, lambda w: jnp.where(has_y, from_y[w], 0.0), gain)
-    add_line(g, y_ref, 1, 1, lambda w: jnp.where(has_x & has_y, from_xy[w], 0.0), gain)
+    add_x_face(g, y_ref, True, lambda w: jnp.where(has_x, from_x[w], 0.0), LATER)
+    add_y_face(g, y_ref, True, lambda w: jnp.where(has_y, from_y[w], 0.0), LATER)
+    add_line(g, y_ref, 1, 1, lambda w: jnp.where(has_x & has_y, from_xy[w], 0.0), LATER)
     sub = lax.broadcasted_iota(jnp.int32, (side, LANES), 0)
     rest = 2 * g.deg - side
     for i in range(g.ex * g.deg):
@@ -408,6 +416,98 @@
                 out_ref[i, k, side:, lanes(h)] = jnp.where(sub < rest, d1, 0.0)
 
 
+def invert_block(block):
+    size = block.shape[0]
+    groups = size // ROWS
+    sub = lax.broadcasted_iota(jnp.int32, (ROWS, size), 0)
+    lane = lax.broadcasted_iota(jnp.int32, (ROWS, size), 1)
+    left = [block[ROWS * j : ROWS * (j + 1)] for j in range(groups)]
+    right = [jnp.where(lane == sub + ROWS * j, 1.0, 0.0) for j in range(groups)]
+    spread = lambda row: jnp.broadcast_to(row, (ROWS, size))
+    result = []
+    for k in range(groups):
+        tile = left[k]
+        cols = [spread(tile[:, ROWS * k + c : ROWS * k + c + 1]) for c in range(ROWS)]
+        s = [[spread(cols[c][r : r + 1]) if c <= r else None for c in range(ROWS)] for r in range(ROWS)]
+        inv, mult = [], [[None] * ROWS for _ in range(ROWS)]
+        root = []
+        for j in range(ROWS):
+            inv.append(1.0 / s[j][j])
+            root.append(lax.rsqrt(s[j][j]))
+            for r in range(j + 1, ROWS):
+                mult[r][j] = s[r][j] * inv[j]
+            for r in range(j + 1, ROWS):
+                for c in range(j + 1, r + 1):
+                    s[r][c] = s[r][c] - mult[r][j] * s[c][j]
+        last = k == groups - 1
+        solved = []
+        for source, wanted in ((right[k], True), (tile, False)):
+            if last and not wanted:
+                continue
+            rows = [spread(source[r : r + 1]) for r in range(ROWS)]
+            for j in range(ROWS):
+                for r in range(j + 1, ROWS):
+                    rows[r] = rows[r] - mult[r][j] * rows[j]
+            if wanted:
+                done = rows[0] * root[0]
+                for r in range(1, ROWS):
+                    done = jnp.where(sub == r, rows[r] * root[r], done)
+                result.append(done)
+            if last:
+                continue
+            rows = [row * d for row, d in zip(rows, inv)]
+            for j in reversed(range(ROWS)):
+                for r in range(j):
+                    rows[r] = rows[r] - mult[j][r] * rows[j]
+            solved.append(rows)
+        for j in range(k + 1, groups):
+            cols = [spread(left[j][:, ROWS * k + c : ROWS * k + c + 1]) for c in range(ROWS)]
+            for c in range(ROWS):
+                right[j] = right[j] - cols[c] * solved[0][c]
+                left[j] = left[j] - cols[c] * solved[1][c]
+    return jnp.concatenate(result, axis=0)
+
+
+def dot(one, two, axis_one=1, axis_two=0):
+    return lax.dot_general(
+        one,
+        two,
+        (((axis_one,), (axis_two,)), ((), ())),
+        precision=lax.Precision.HIGHEST,
+        preferred_element_type=jnp.float32,
+    )
+
+
+def inverse_factor(block_of, count):
+    low, inv = {}, {}
+    for i in range(count):
+        diag = block_of(i, i)
+        for j in range(i):
+            part = block_of(i, j)
+            for k in range(j):
+                part = part - dot(low[i, k], low[j, k], 1, 1)
+            low[i, j] = dot(part, inv[j, j], 1, 1)
+            diag = diag - dot(low[i, j], low[i, j], 1, 1)
+        sums = []
+        for j in range(i):
+            part = dot(low[i, j], inv[j, j])
+            for k in range(j + 1, i):
+                part = part + dot(low[i, k], inv[k, j])
+            sums.append(part)
+        inv[i, i] = invert_block(diag)
+        for j in range(i):
+            inv[i, j] = -dot(inv[i, i], sums[j])
+    return inv
+
+def factor_kernel(gram_ref, out_ref):
+    count = gram_ref.shape[0] // LANES
+    inverse = inverse_factor(lambda i, j: gram_ref[lanes(i), lanes(j)], count)
+    for i in range(count):
+        for j in range(count):
+            block = inverse[i, j] if j <= i else jnp.zeros((LANES, LANES), jnp.float32)
+            out_ref[lanes(i), lanes(j)] = block
+
+
 def call(kernel, outs, scratch, operands, flops):
     size = sum(x.size * x.dtype.itemsize for x in (*operands, *outs))
     return pl.pallas_call(
@@ -427,9 +527,9 @@
     g = Grid(elem_mats, side)
     f32 = jnp.float32
     orb = jnp.transpose(orbitals, (0, 2, 1, 3))
-    below_x = offset(orb[-1], 1, 0)
-    below_y = offset(orb[:, :, -1], 0, 1)
-    below_xy = offset(orb[-1, :, -1], 1, 1)
+    below_x = ring(orb[-1], 1, 0)
+    below_y = ring(orb[:, :, -1], 0, 1)
+    below_xy = ring(orb[-1, :, -1], 1, 1)
     mats = renumber(conn, elem_mats, side, ny + 1, nz + 2)
     mats = mats.reshape(g.elements, g.count, g.count)
 
@@ -443,7 +543,7 @@
     pairings += [("A", "A"), ("A", "B"), ("B", "A"), ("B", "B")]
     flops = 2 * g.elements * g.count**2 * bands
 
-    y0, w1, *sends = call(
+    y0, part, *sends = call(
         functools.partial(first_kernel, g=g),
         [shape(nodes, f32), shape(nodes, f32), *send_shapes],
         [],
@@ -451,36 +551,36 @@
         flops,
     )
     received = [pair_swap(s, *pair) for s, pair in zip(sends, pairings)]
-    y1, w2, *sends = call(
-        functools.partial(middle_kernel, g=g, first=True),
+    y1, part, *sends = call(
+        functools.partial(middle_kernel, g=g),
         [shape(nodes, f32), shape(nodes, f32), *send_shapes],
         [],
-        (w1, *received, y0, mats),
+        (part, *received, y0, mats),
         flops,
     )
     received = [pair_swap(s, *pair) for s, pair in zip(sends, pairings)]
-    y2, w3, *sends = call(
-        functools.partial(middle_kernel, g=g, first=False),
-        [shape(nodes, f32), shape(nodes, f32), x_shape, y_shape, line_shape],
-        [],
-        (w2, *received, y1, y0, mats),
+    part, *sends = call(
+        functools.partial(late_kernel, g=g),
+        [shape(nodes, f32), x_shape, y_shape, line_shape],
+        [pltpu.VMEM(nodes, f32)],
+        (part, *received, y1, mats),
         flops,
     )
-    received = [offset(s, *step) for s, step in zip(sends, ((-1, 0), (0, -1), (-1, -1)))]
+    received = [ring(s, *step) for s, step in zip(sends, ((-1, 0), (0, -1), (-1, -1)))]
     (y3,) = call(
         functools.partial(last_kernel, g=g),
         [shape((nx, nz, 2 * side, bands), f32)],
         [pltpu.VMEM(nodes, f32)],
-        (w3, *received, y2, y1),
+        (part, *received),
         flops // 100,
     )
 
     columns = y3.reshape(-1, bands)
     gram = jnp.einsum("rb,rc->bc", columns, columns, precision=lax.Precision.HIGHEST)
     gram = total(gram)
-    lower = jnp.linalg.cholesky(gram)
-    identity = jnp.eye(bands, dtype=f32)
-    inverse_lower = lax.linalg.triangular_solve(lower, identity, left_side=True, lower=True)
+    (inverse_lower,) = call(
+        factor_kernel, [shape((bands, bands), f32)], [], (gram,), 2 * bands**3
+    )
     basis = jnp.einsum("rb,cb->rc", columns, inverse_lower, precision=lax.Precision.HIGHEST)
     scale = math.sqrt(nx * ny * nz * lax.axis_size(AXES))
     basis = (basis * scale).reshape(nx, nz, 2 * side, bands)[:, :, :ny]

time: 225 us -> 132 us (0.59)
  other arithmetic: 56.1 us -> 0.12 us
  Pallas kernels: 39 us -> 24.1 us
  waiting for transfers between devices: 40.4 us -> 30.8 us
  local copies, waits for them, and re-layouts: 16.8 us -> 10.3 us
  matrix products: 12 us -> 7.59 us
    another operation x9 -> x0, other arithmetic: 54.6 us -> none  [the longest x6 34.1 us: shards(): lower = jnp.linalg.cholesky(gram)]
    pallas_call x4 -> x5, Pallas kernels: 31.1 us -> 18.4 us  [call(): pl.pallas_call(kernel, out_shape=outs, in_specs=[VMEM] * len(operands), o...]
    ppermute x6, waiting for transfers between devices: 12.4 us -> 2.41 us  [ring(): return lax.ppermute(value, AXES, route)]
    another operation x9 -> x0, local copies, waits for them, and re-layouts: 5.1 us -> none
    another operation x5 -> x0, matrix products: 4.49 us -> none  [the longest x3 2.33 us: shards(): lax.linalg.triangular_solve(lower, identity, left_side=True, lower=True)]
    unnamed x13 -> x11, local copies, waits for them, and re-layouts: 8.6 us -> 8.31 us
where the time goes in v2:
time: 132 us
  starting transfers between devices  58.3 us (44%)
  waiting for transfers between devices  30.8 us (23%)
  Pallas kernels  24.1 us (18%)
  local copies, waits for them, and re-layouts  10.3 us (8%)
  matrix products  7.59 us (6%)
    ppermute x16, starting transfers between devices, pair_swap(): return lax.ppermute(value, AXES, route)  30.3 us
    pallas_call x5, Pallas kernels, call(): pl.pallas_call(kernel, out_shape=outs, in_specs=[VMEM] * len(operands), o...  18.4 us
    ppermute x8, waiting for transfers between devices, xor_swap(): lax.ppermute(value, axis, [(i, i ^ bits) for i in range(lax.axis_size(axi...  17.6 us
    ppermute x6, starting transfers between devices, ring(): return lax.ppermute(value, AXES, route)  17.4 us
    ppermute x16, waiting for transfers between devices, pair_swap(): return lax.ppermute(value, AXES, route)  10.8 us
    ppermute x8, starting transfers between devices, xor_swap(): lax.ppermute(value, axis, [(i, i ^ bits) for i in range(lax.axis_size(axi...  10.5 us
    unnamed x11, local copies, waits for them, and re-layouts  8.31 us
    pallas_call x1, Pallas kernels, renumber(): pl.pallas_call(functools.partial(renumber_kernel, side=side, width=width,...  5.73 us
  transfers between devices with their start and end apart: 30, of which 13 were waited for; matrix products, arithmetic and copies ran while one was open for 0% of the time, Pallas kernels for 4%

profile of v2, /device:TPU:0, one launch (start us, length us, event | category | flops | bytes accessed | tf_op | source)
XLA Modules:
  0.0 131.5 jit_solution(13079057487900384552)
XLA Ops:
  0.0 2.0 %copy.10 = bf16[14,14,13,256]{3,2,1,0:T(8,128)(2,1)S(1)} copy(bf16[14,14,13,256]{3,1,2,0:T(8,128)(2,1)} %param.3) | data formatting | bytes 2609152 | tf_op args[0]
  2.0 3.1 %collective-permute-start = (bf16[13,14,256]{2,0,1:T(8,128)(2,1)S(1)}, bf16[13,14,256]{2,0,1:T(8,128)(2,1)S(1)}, u32[]{:S(2)}, u32[]{:S(2)}) collective-permute-start(bf16[13,14,256]{2,0,1:T(8,128)(2,1)S(1)} %slice_bitcast_fusion.2), channel_id=1, source_target_pairs={{0,8},{1,9},{2,10},{3,11},{4,12},{5,13},{6,14},{7,15},{8,16},{9,17... | collective-permute-start | bytes 279560 | tf_op jit(solution)/shard_map/ppermute | solution.py:46
  5.2 2.8 %collective-permute-start.2 = (bf16[13,256]{1,0:T(8,128)(2,1)S(1)}, bf16[13,256]{1,0:T(8,128)(2,1)S(1)}, u32[]{:S(2)}, u32[]{:S(2)}) collective-permute-start(bf16[13,256]{1,0:T(8,128)(2,1)S(1)} %slice_bitcast_fusion.3), channel_id=1, source_target_pairs={{0,9},{1,10},{2,11},{3,12},{4,13},{5,14},{6,15},{7,8},{8,17},{9,18... | collective-permute-start | bytes 19976 | tf_op jit(solution)/shard_map/ppermute | solution.py:46
  7.9 2.2 %copy-done.3 = bf16[2,2,2,512,512]{4,3,2,1,0:T(8,128)(2,1)S(1)} copy-done((bf16[2,2,2,512,512]{4,3,2,1,0:T(8,128)(2,1)S(1)}, bf16[2,2,2,512,512]{4,3,2,1,0:T(8,128)(2,1)}, u32[]{:S(2)}) %copy-start.3) | copy-done | bytes 4194328
  10.1 5.7 %renumber.1 = bf16[2,2,2,512,512]{4,3,2,1,0:T(8,128)(2,1)S(1)} custom-call(s32[2,2,2,512]{3,2,1,0:T(2,128)S(1)} %copy-done.4, bf16[2,2,2,512,512]{4,3,2,1,0:T(8,128)(2,1)S(1)} %copy-done.3), custom_call_target="tpu_custom_call" | custom-call | flops 4294967296 | bytes 8388608 | tf_op jit(solution)/shard_map/renumber/pallas_call | solution.py:114
  15.9 2.1 %shard_map.37 = (f32[8,2,512,128]{3,2,1,0:T(8,128)S(1)}, f32[8,2,512,128]{3,2,1,0:T(8,128)S(1)}, f32[13,16,256]{2,1,0:T(8,128)S(1)}, f32[13,16,256]{2,1,0:T(8,12...) custom-call(bf16[14,13,14,256]{3,2,1,0:T(8,128)(2,1)S(1)} %bitcast.2, ...), custom_call_target="tpu_custom_call" | custom-call | flops 1073741824 | bytes 15096320 | tf_op jit(solution)/shard_map/pallas_call | solution.py:513
  18.1 0.7 collective-permute-start.6
  18.8 1.6 %collective-permute-start.3 = (f32[13,16,256]{2,1,0:T(8,128)S(1)}, f32[13,16,256]{2,1,0:T(8,128)S(1)}, u32[]{:S(2)}, u32[]{:S(2)}) collective-permute-start(f32[13,16,256]{2,1,0:T(8,128)S(1)} %get-tuple-element.30), channel_id=1, source_target_pairs={{0,8},{1,9},{2,10},{3,11},{4,12},{5,13},{6,14},{7,15},{8,0},{9,1},... | collective-permute-start | bytes 638984 | tf_op jit(solution)/shard_map/ppermute | solution.py:36
  20.4 0.7 collective-permute-start.4
  21.1 0.7 collective-permute-start.10
  21.8 11.2 %collective-permute-start.7 = (f32[16,256]{1,0:T(8,128)S(1)}, f32[16,256]{1,0:T(8,128)S(1)}, u32[]{:S(2)}, u32[]{:S(2)}) collective-permute-start(f32[16,256]{1,0:T(8,128)S(1)} %get-tuple-element.34), channel_id=1, source_target_pairs={{0,9},{1,8},{2,11},{3,10},{4,13},{5,12},{6,15},{7,14},{8,1},{9,0},... | collective-permute-start | bytes 49160 | tf_op jit(solution)/shard_map/ppermute | solution.py:36
  33.0 1.4 %collective-permute-done.7.refs_5_ = f32[16,256]{1,0:T(8,128)S(1)} collective-permute-done((f32[16,256]{1,0:T(8,128)S(1)}, f32[16,256]{1,0:T(8,128)S(1)}, u32[]{:S(2)}, u32[]{:S(2)}) %collective-permute-start.7) | collective-permute-done | bytes 16416 | tf_op jit(solution)/shard_map/ppermute | solution.py:36
  34.5 3.7 %collective-permute-done.8.refs_6_ = f32[16,256]{1,0:T(8,128)S(1)} collective-permute-done((f32[16,256]{1,0:T(8,128)S(1)}, f32[16,256]{1,0:T(8,128)S(1)}, u32[]{:S(2)}, u32[]{:S(2)}) %collective-permute-start.8) | collective-permute-done | bytes 16416 | tf_op jit(solution)/shard_map/ppermute | solution.py:36
  38.2 1.2 collective-permute-done.9.refs_7_
  39.4 2.4 %shard_map.38 = (f32[8,2,512,128]{3,2,1,0:T(8,128)S(1)}, f32[8,2,512,128]{3,2,1,0:T(8,128)S(1)}, f32[13,16,256]{2,1,0:T(8,128)S(1)}, f32[13,16,256]{2,1,0:T(8,12...) custom-call(f32[8,2,512,128]{3,2,1,0:T(8,128)S(1)} %get-tuple-elemen, ...), custom_call_target="tpu_custom_call" | custom-call | flops 1073741824 | bytes 23003136 | tf_op jit(solution)/shard_map/pallas_call | solution.py:513
  42.1 0.7 collective-permute-start.14
  42.8 4.3 %collective-permute-start.11 = (f32[13,16,256]{2,1,0:T(8,128)S(1)}, f32[13,16,256]{2,1,0:T(8,128)S(1)}, u32[]{:S(2)}, u32[]{:S(2)}) collective-permute-start(f32[13,16,256]{2,1,0:T(8,128)S(1)} %get-tuple-element.40), channel_id=1, source_target_pairs={{0,8},{1,9},{2,10},{3,11},{4,12},{5,13},{6,14},{7,15},{8,0},{9,1},... | collective-permute-start | bytes 638984 | tf_op jit(solution)/shard_map/ppermute | solution.py:36
  47.1 0.7 collective-permute-start.12
  47.8 4.9 %collective-permute-start.15 = (f32[16,256]{1,0:T(8,128)S(1)}, f32[16,256]{1,0:T(8,128)S(1)}, u32[]{:S(2)}, u32[]{:S(2)}) collective-permute-start(f32[16,256]{1,0:T(8,128)S(1)} %get-tuple-element.44), channel_id=1, source_target_pairs={{0,9},{1,8},{2,11},{3,10},{4,13},{5,12},{6,15},{7,14},{8,1},{9,0},... | collective-permute-start | bytes 49160 | tf_op jit(solution)/shard_map/ppermute | solution.py:36
  52.7 1.4 %collective-permute-done.15.refs_5_ = f32[16,256]{1,0:T(8,128)S(1)} collective-permute-done((f32[16,256]{1,0:T(8,128)S(1)}, f32[16,256]{1,0:T(8,128)S(1)}, u32[]{:S(2)}, u32[]{:S(2)}) %collective-permute-start.15) | collective-permute-done | bytes 16416 | tf_op jit(solution)/shard_map/ppermute | solution.py:36
  54.1 1.6 %collective-permute-start.16 = (f32[16,256]{1,0:T(8,128)S(1)}, f32[16,256]{1,0:T(8,128)S(1)}, u32[]{:S(2)}, u32[]{:S(2)}) collective-permute-start(f32[16,256]{1,0:T(8,128)S(1)} %get-tuple-element.45), channel_id=1, source_target_pairs={{0,8},{1,10},{2,9},{3,12},{4,11},{5,14},{6,13},{7,15},{8,0},{9,2},... | collective-permute-start | bytes 49160 | tf_op jit(solution)/shard_map/ppermute | solution.py:36
  55.7 2.1 %collective-permute-done.16.refs_6_ = f32[16,256]{1,0:T(8,128)S(1)} collective-permute-done((f32[16,256]{1,0:T(8,128)S(1)}, f32[16,256]{1,0:T(8,128)S(1)}, u32[]{:S(2)}, u32[]{:S(2)}) %collective-permute-start.16) | collective-permute-done | bytes 16416 | tf_op jit(solution)/shard_map/ppermute | solution.py:36
  57.9 2.3 %collective-permute-start.17 = (f32[16,256]{1,0:T(8,128)S(1)}, f32[16,256]{1,0:T(8,128)S(1)}, u32[]{:S(2)}, u32[]{:S(2)}) collective-permute-start(f32[16,256]{1,0:T(8,128)S(1)} %get-tuple-element.46), channel_id=1, source_target_pairs={{0,1},{1,0},{2,3},{3,2},{4,5},{5,4},{6,7},{7,6},{8,17},{9,16},{10,... | collective-permute-start | bytes 49160 | tf_op jit(solution)/shard_map/ppermute | solution.py:36
  60.2 0.8 collective-permute-done.17.refs_7_
  61.0 0.7 collective-permute-start.18
  61.7 2.4 %shard_map.39 = (f32[8,2,512,128]{3,2,1,0:T(8,128)S(1)}, f32[13,16,256]{2,1,0:T(8,128)S(1)}, f32[4,64,256]{2,1,0:T(8,128)S(1)}, f32[16,256]{1,0:T(8,128)S(1)}) custom-call(f32[8,2,512,128]{3,2,1,0:T(8,128)S(1)} %get-tuple-element.39.refs_0_, f32[13,16,256]{2,1,0:T(8,128)S(1)} %collective-permute-done.11.refs_1_, ...), custom_call_target="tpu_custom_call" | custom-call | flops 1073741824 | bytes 18284544 | tf_op jit(solution)/shard_map/pallas_call | solution.py:513
  64.1 2.0 %copy-done.1 = f32[8,2,512,128]{3,2,1,0:T(8,128)} copy-done((f32[8,2,512,128]{3,2,1,0:T(8,128)}, f32[8,2,512,128]{3,2,1,0:T(8,128)S(1)}, u32[]{:S(2)}) %copy-start.1) | copy-done | bytes 4194328
  66.0 1.1 collective-permute-start.20
  67.2 1.9 %collective-permute-start.19 = (f32[13,16,256]{2,1,0:T(8,128)S(1)}, f32[13,16,256]{2,1,0:T(8,128)S(1)}, u32[]{:S(2)}, u32[]{:S(2)}) collective-permute-start(f32[13,16,256]{2,1,0:T(8,128)S(1)} %get-tuple-element.50), channel_id=1, source_target_pairs={{0,24},{1,25},{2,26},{3,27},{4,28},{5,29},{6,30},{7,31},{8,0},{9,1... | collective-permute-start | bytes 638984 | tf_op jit(solution)/shard_map/ppermute | solution.py:46
  69.1 8.5 %collective-permute-start.21 = (f32[16,256]{1,0:T(8,128)S(1)}, f32[16,256]{1,0:T(8,128)S(1)}, u32[]{:S(2)}, u32[]{:S(2)}) collective-permute-start(f32[16,256]{1,0:T(8,128)S(1)} %get-tuple-element.52), channel_id=1, source_target_pairs={{0,31},{1,24},{2,25},{3,26},{4,27},{5,28},{6,29},{7,30},{8,7},{9,0... | collective-permute-start | bytes 49160 | tf_op jit(solution)/shard_map/ppermute | solution.py:46
  77.6 2.3 %collective-permute-done.21.from_xy = f32[16,256]{1,0:T(8,128)S(1)} collective-permute-done((f32[16,256]{1,0:T(8,128)S(1)}, f32[16,256]{1,0:T(8,128)S(1)}, u32[]{:S(2)}, u32[]{:S(2)}) %collective-permute-start.21) | collective-permute-done | bytes 16416 | tf_op jit(solution)/shard_map/ppermute | solution.py:46
  80.0 2.2 %copy-done.2 = f32[8,2,512,128]{3,2,1,0:T(8,128)S(1)} copy-done((f32[8,2,512,128]{3,2,1,0:T(8,128)S(1)}, f32[8,2,512,128]{3,2,1,0:T(8,128)}, u32[]{:S(2)}) %copy-start.2) | copy-done | bytes 4194328
  82.7 4.9 %convolution_bitcast_fusion = f32[256,256]{1,0:T(8,128)S(1)} fusion(f32[14,13,16,256]{3,2,1,0:T(8,128)S(1)} %shard_map.40), kind=kOutput, calls=%fused_computation.3 | convolution fusion | flops 2290089984 | bytes 3244032 | tf_op jit(solution)/shard_map/rb,rc->bc/dot_general | solution.py:579
  87.7 1.2 collective-permute-start.22
  88.9 1.0 collective-permute-done.22
  89.9 2.4 %collective-permute-start.23 = (f32[128,256]{1,0:T(8,128)S(1)}, f32[128,256]{1,0:T(8,128)S(1)}, u32[]{:S(2)}, u32[]{:S(2)}) collective-permute-start(f32[128,256]{1,0:T(8,128)S(1)} %dynamic-slice_add_fusion), channel_id=1, source_target_pairs={{0,8},{8,0},{16,24},{24,16},{1,9},{9,1},{17,25},{25,17},{2,10},{10... | collective-permute-start | bytes 393224 | tf_op jit(solution)/shard_map/ppermute | solution.py:50
  92.4 0.6 collective-permute-start.24
  92.9 1.9 %collective-permute-start.25 = (f32[128,256]{1,0:T(8,128)S(1)}, f32[128,256]{1,0:T(8,128)S(1)}, u32[]{:S(2)}, u32[]{:S(2)}) collective-permute-start(f32[128,256]{1,0:T(8,128)S(1)} %dynamic-slice_add_fusion), channel_id=1, source_target_pairs={{0,24},{8,16},{16,8},{24,0},{1,25},{9,17},{17,9},{25,1},{2,26},{10... | collective-permute-start | bytes 393224 | tf_op jit(solution)/shard_map/ppermute | solution.py:50
  94.8 3.2 %collective-permute-done.23 = f32[128,256]{1,0:T(8,128)S(1)} collective-permute-done((f32[128,256]{1,0:T(8,128)S(1)}, f32[128,256]{1,0:T(8,128)S(1)}, u32[]{:S(2)}, u32[]{:S(2)}) %collective-permute-start.23) | collective-permute-done | bytes 131104 | tf_op jit(solution)/shard_map/ppermute | solution.py:50
  98.0 7.3 %collective-permute-done.24 = f32[128,256]{1,0:T(8,128)S(1)} collective-permute-done((f32[128,256]{1,0:T(8,128)S(1)}, f32[128,256]{1,0:T(8,128)S(1)}, u32[]{:S(2)}, u32[]{:S(2)}) %collective-permute-start.24) | collective-permute-done | bytes 131104 | tf_op jit(solution)/shard_map/ppermute | solution.py:50
  105.3 2.9 %collective-permute-start.26 = (f32[128,256]{1,0:T(8,128)S(1)}, f32[128,256]{1,0:T(8,128)S(1)}, u32[]{:S(2)}, u32[]{:S(2)}) collective-permute-start(f32[128,256]{1,0:T(8,128)S(1)} %add_add_fusion.1), channel_id=1, source_target_pairs={{0,2},{1,3},{2,0},{3,1},{4,6},{5,7},{6,4},{7,5},{8,10},{9,11},{10,... | collective-permute-start | bytes 393224 | tf_op jit(solution)/shard_map/ppermute | solution.py:50
  108.2 1.5 %collective-permute-start.28 = (f32[128,256]{1,0:T(8,128)S(1)}, f32[128,256]{1,0:T(8,128)S(1)}, u32[]{:S(2)}, u32[]{:S(2)}) collective-permute-start(f32[128,256]{1,0:T(8,128)S(1)} %add_add_fusion.1), channel_id=1, source_target_pairs={{0,6},{1,7},{2,4},{3,5},{4,2},{5,3},{6,0},{7,1},{8,14},{9,15},{10,... | collective-permute-start | bytes 393224 | tf_op jit(solution)/shard_map/ppermute | solution.py:50
  109.7 2.6 %collective-permute-done.26 = f32[128,256]{1,0:T(8,128)S(1)} collective-permute-done((f32[128,256]{1,0:T(8,128)S(1)}, f32[128,256]{1,0:T(8,128)S(1)}, u32[]{:S(2)}, u32[]{:S(2)}) %collective-permute-start.26) | collective-permute-done | bytes 131104 | tf_op jit(solution)/shard_map/ppermute | solution.py:50
  112.4 2.2 %collective-permute-done.27 = f32[128,256]{1,0:T(8,128)S(1)} collective-permute-done((f32[128,256]{1,0:T(8,128)S(1)}, f32[128,256]{1,0:T(8,128)S(1)}, u32[]{:S(2)}, u32[]{:S(2)}) %collective-permute-start.27) | collective-permute-done | bytes 131104 | tf_op jit(solution)/shard_map/ppermute | solution.py:50
  114.7 1.3 %collective-permute-done.29 = f32[128,256]{1,0:T(8,128)S(1)} collective-permute-done((f32[128,256]{1,0:T(8,128)S(1)}, f32[128,256]{1,0:T(8,128)S(1)}, u32[]{:S(2)}, u32[]{:S(2)}) %collective-permute-start.29) | collective-permute-done | bytes 131104 | tf_op jit(solution)/shard_map/ppermute | solution.py:50
  116.1 10.9 %shard_map.41 = f32[256,256]{1,0:T(8,128)S(1)} custom-call(f32[256,256]{1,0:T(8,128)S(1)} %pad_maximum_fusion.gram_ref), custom_call_target="tpu_custom_call" | custom-call | flops 33554432 | bytes 524288 | tf_op jit(solution)/shard_map/pallas_call | solution.py:513
  127.0 2.7 %convolution_multiply_fusion = f32[2912,256]{1,0:T(8,128)S(1)} fusion(f32[2912,256]{1,0:T(8,128)S(1)} %bitcast.26, f32[256,256]{1,0:T(8,128)S(1)} %shard_map.41), kind=kOutput, calls=%fused_computation | convolution fusion | flops 2290835456 | bytes 6225920 | tf_op jit(solution)/shard_map/rb,cb->rc/dot_general | solution.py:584
  129.6 1.9 %slice_bitcast_fusion = f32[14,14,13,256]{3,1,2,0:T(8,128)} fusion(f32[14,13,16,256]{3,2,1,0:T(8,128)S(1)} %bitcast.28), kind=kLoop, calls=%fused_computation.1 | loop fusion | bytes 5218304 | tf_op jit(solution)/shard_map/transpose | solution.py:587
  (42 shorter events, 1.3 us)
Async XLA Ops:
  0.0 7.9 %copy-start.4 = (s32[2,2,2,512]{3,2,1,0:T(2,128)S(1)}, s32[2,2,2,512]{3,2,1,0:T(2,128)}, u32[]{:S(2)}) copy-start(s32[2,2,2,512]{3,2,1,0:T(2,128)} %conn_ref.1) | copy-start | bytes 49156
  2.0 13.9 %collective-permute-start = (bf16[13,14,256]{2,0,1:T(8,128)(2,1)S(1)}, bf16[13,14,256]{2,0,1:T(8,128)(2,1)S(1)}, u32[]{:S(2)}, u32[]{:S(2)}) collective-permute-start(bf16[13,14,256]{2,0,1:T(8,128)(2,1)S(1)} %slice_bitcast_fusion.2), channel_id=1, source_target_pairs={{0,8},{1,9},{2,10},{3,11},{4,12},{5,13},{6,14},{7,15},{8,16},{9,17... | collective-permute-start | bytes 279560 | tf_op jit(solution)/shard_map/ppermute | solution.py:46
  5.1 10.8 %collective-permute-start.1 = (bf16[14,13,256]{2,1,0:T(8,128)(2,1)S(1)}, bf16[14,13,256]{2,1,0:T(8,128)(2,1)S(1)}, u32[]{:S(2)}, u32[]{:S(2)}) collective-permute-start(bf16[14,13,256]{2,1,0:T(8,128)(2,1)S(1)} %slice_bitcast_fusion.1), channel_id=1, source_target_pairs={{0,1},{1,2},{2,3},{3,4},{4,5},{5,6},{6,7},{7,0},{8,9},{9,10},{10,1... | collective-permute-start | bytes 279560 | tf_op jit(solution)/shard_map/ppermute | solution.py:46
  5.1 10.8 %copy-start = (bf16[14,14,13,256]{3,1,2,0:T(8,128)(2,1)S(1)}, bf16[14,14,13,256]{3,1,2,0:T(8,128)(2,1)}, u32[]{:S(2)}) copy-start(bf16[14,14,13,256]{3,1,2,0:T(8,128)(2,1)} %param.3) | copy-start | bytes 3913732
  5.2 10.7 %collective-permute-start.2 = (bf16[13,256]{1,0:T(8,128)(2,1)S(1)}, bf16[13,256]{1,0:T(8,128)(2,1)S(1)}, u32[]{:S(2)}, u32[]{:S(2)}) collective-permute-start(bf16[13,256]{1,0:T(8,128)(2,1)S(1)} %slice_bitcast_fusion.3), channel_id=1, source_target_pairs={{0,9},{1,10},{2,11},{3,12},{4,13},{5,14},{6,15},{7,8},{8,17},{9,18... | collective-permute-start | bytes 19976 | tf_op jit(solution)/shard_map/ppermute | solution.py:46
  7.9 2.2 %copy-start.3 = (bf16[2,2,2,512,512]{4,3,2,1,0:T(8,128)(2,1)S(1)}, bf16[2,2,2,512,512]{4,3,2,1,0:T(8,128)(2,1)}, u32[]{:S(2)}) copy-start(bf16[2,2,2,512,512]{4,3,2,1,0:T(8,128)(2,1)} %mats_ref.1) | copy-start | bytes 12582916
  18.0 21.4 %collective-permute-start.5 = (f32[4,64,256]{2,1,0:T(8,128)S(1)}, f32[4,64,256]{2,1,0:T(8,128)S(1)}, u32[]{:S(2)}, u32[]{:S(2)}) collective-permute-start(f32[4,64,256]{2,1,0:T(8,128)S(1)} %get-tuple-element.32), channel_id=1, source_target_pairs={{0,1},{1,0},{2,3},{3,2},{4,5},{5,4},{6,7},{7,6},{8,9},{9,8},{10,11... | collective-permute-start | bytes 786440 | tf_op jit(solution)/shard_map/ppermute | solution.py:36
  18.1 21.3 %collective-permute-start.6 = (f32[4,64,256]{2,1,0:T(8,128)S(1)}, f32[4,64,256]{2,1,0:T(8,128)S(1)}, u32[]{:S(2)}, u32[]{:S(2)}) collective-permute-start(f32[4,64,256]{2,1,0:T(8,128)S(1)} %get-tuple-element.33), channel_id=1, source_target_pairs={{0,0},{1,2},{2,1},{3,4},{4,3},{5,6},{6,5},{7,7},{8,8},{9,10},{10,9... | collective-permute-start | bytes 786440 | tf_op jit(solution)/shard_map/ppermute | solution.py:36
  18.8 20.6 %collective-permute-start.3 = (f32[13,16,256]{2,1,0:T(8,128)S(1)}, f32[13,16,256]{2,1,0:T(8,128)S(1)}, u32[]{:S(2)}, u32[]{:S(2)}) collective-permute-start(f32[13,16,256]{2,1,0:T(8,128)S(1)} %get-tuple-element.30), channel_id=1, source_target_pairs={{0,8},{1,9},{2,10},{3,11},{4,12},{5,13},{6,14},{7,15},{8,0},{9,1},... | collective-permute-start | bytes 638984 | tf_op jit(solution)/shard_map/ppermute | solution.py:36
  20.4 19.0 %collective-permute-start.4 = (f32[13,16,256]{2,1,0:T(8,128)S(1)}, f32[13,16,256]{2,1,0:T(8,128)S(1)}, u32[]{:S(2)}, u32[]{:S(2)}) collective-permute-start(f32[13,16,256]{2,1,0:T(8,128)S(1)} %get-tuple-element.31), channel_id=1, source_target_pairs={{0,0},{1,1},{2,2},{3,3},{4,4},{5,5},{6,6},{7,7},{8,16},{9,17},{10,... | collective-permute-start | bytes 638984 | tf_op jit(solution)/shard_map/ppermute | solution.py:36
  21.1 0.7 collective-permute-start.10
  21.8 12.7 %collective-permute-start.7 = (f32[16,256]{1,0:T(8,128)S(1)}, f32[16,256]{1,0:T(8,128)S(1)}, u32[]{:S(2)}, u32[]{:S(2)}) collective-permute-start(f32[16,256]{1,0:T(8,128)S(1)} %get-tuple-element.34), channel_id=1, source_target_pairs={{0,9},{1,8},{2,11},{3,10},{4,13},{5,12},{6,15},{7,14},{8,1},{9,0},... | collective-permute-start | bytes 49160 | tf_op jit(solution)/shard_map/ppermute | solution.py:36
  34.5 3.7 %collective-permute-start.8 = (f32[16,256]{1,0:T(8,128)S(1)}, f32[16,256]{1,0:T(8,128)S(1)}, u32[]{:S(2)}, u32[]{:S(2)}) collective-permute-start(f32[16,256]{1,0:T(8,128)S(1)} %get-tuple-element.35), channel_id=1, source_target_pairs={{0,8},{1,10},{2,9},{3,12},{4,11},{5,14},{6,13},{7,15},{8,0},{9,2},... | collective-permute-start | bytes 49160 | tf_op jit(solution)/shard_map/ppermute | solution.py:36
  38.2 1.2 collective-permute-start.9
  41.9 19.8 %collective-permute-start.13 = (f32[4,64,256]{2,1,0:T(8,128)S(1)}, f32[4,64,256]{2,1,0:T(8,128)S(1)}, u32[]{:S(2)}, u32[]{:S(2)}) collective-permute-start(f32[4,64,256]{2,1,0:T(8,128)S(1)} %get-tuple-element.42), channel_id=1, source_target_pairs={{0,1},{1,0},{2,3},{3,2},{4,5},{5,4},{6,7},{7,6},{8,9},{9,8},{10,11... | collective-permute-start | bytes 786440 | tf_op jit(solution)/shard_map/ppermute | solution.py:36
  42.1 19.6 %collective-permute-start.14 = (f32[4,64,256]{2,1,0:T(8,128)S(1)}, f32[4,64,256]{2,1,0:T(8,128)S(1)}, u32[]{:S(2)}, u32[]{:S(2)}) collective-permute-start(f32[4,64,256]{2,1,0:T(8,128)S(1)} %get-tuple-element.43), channel_id=1, source_target_pairs={{0,0},{1,2},{2,1},{3,4},{4,3},{5,6},{6,5},{7,7},{8,8},{9,10},{10,9... | collective-permute-start | bytes 786440 | tf_op jit(solution)/shard_map/ppermute | solution.py:36
  42.8 18.9 %collective-permute-start.11 = (f32[13,16,256]{2,1,0:T(8,128)S(1)}, f32[13,16,256]{2,1,0:T(8,128)S(1)}, u32[]{:S(2)}, u32[]{:S(2)}) collective-permute-start(f32[13,16,256]{2,1,0:T(8,128)S(1)} %get-tuple-element.40), channel_id=1, source_target_pairs={{0,8},{1,9},{2,10},{3,11},{4,12},{5,13},{6,14},{7,15},{8,0},{9,1},... | collective-permute-start | bytes 638984 | tf_op jit(solution)/shard_map/ppermute | solution.py:36
  47.1 14.6 %collective-permute-start.12 = (f32[13,16,256]{2,1,0:T(8,128)S(1)}, f32[13,16,256]{2,1,0:T(8,128)S(1)}, u32[]{:S(2)}, u32[]{:S(2)}) collective-permute-start(f32[13,16,256]{2,1,0:T(8,128)S(1)} %get-tuple-element.41), channel_id=1, source_target_pairs={{0,0},{1,1},{2,2},{3,3},{4,4},{5,5},{6,6},{7,7},{8,16},{9,17},{10,... | collective-permute-start | bytes 638984 | tf_op jit(solution)/shard_map/ppermute | solution.py:36
  47.8 6.4 %collective-permute-start.15 = (f32[16,256]{1,0:T(8,128)S(1)}, f32[16,256]{1,0:T(8,128)S(1)}, u32[]{:S(2)}, u32[]{:S(2)}) collective-permute-start(f32[16,256]{1,0:T(8,128)S(1)} %get-tuple-element.44), channel_id=1, source_target_pairs={{0,9},{1,8},{2,11},{3,10},{4,13},{5,12},{6,15},{7,14},{8,1},{9,0},... | collective-permute-start | bytes 49160 | tf_op jit(solution)/shard_map/ppermute | solution.py:36
  54.1 3.7 %collective-permute-start.16 = (f32[16,256]{1,0:T(8,128)S(1)}, f32[16,256]{1,0:T(8,128)S(1)}, u32[]{:S(2)}, u32[]{:S(2)}) collective-permute-start(f32[16,256]{1,0:T(8,128)S(1)} %get-tuple-element.45), channel_id=1, source_target_pairs={{0,8},{1,10},{2,9},{3,12},{4,11},{5,14},{6,13},{7,15},{8,0},{9,2},... | collective-permute-start | bytes 49160 | tf_op jit(solution)/shard_map/ppermute | solution.py:36
  57.9 3.1 %collective-permute-start.17 = (f32[16,256]{1,0:T(8,128)S(1)}, f32[16,256]{1,0:T(8,128)S(1)}, u32[]{:S(2)}, u32[]{:S(2)}) collective-permute-start(f32[16,256]{1,0:T(8,128)S(1)} %get-tuple-element.46), channel_id=1, source_target_pairs={{0,1},{1,0},{2,3},{3,2},{4,5},{5,4},{6,7},{7,6},{8,17},{9,16},{10,... | collective-permute-start | bytes 49160 | tf_op jit(solution)/shard_map/ppermute | solution.py:36
  61.0 0.7 collective-permute-start.18
  64.1 2.0 %copy-start.1 = (f32[8,2,512,128]{3,2,1,0:T(8,128)}, f32[8,2,512,128]{3,2,1,0:T(8,128)S(1)}, u32[]{:S(2)}) copy-start(f32[8,2,512,128]{3,2,1,0:T(8,128)S(1)} %get-tuple-element.49.part_ref) | copy-start | bytes 12582916
  66.0 13.9 %collective-permute-start.20 = (f32[4,64,256]{2,1,0:T(8,128)S(1)}, f32[4,64,256]{2,1,0:T(8,128)S(1)}, u32[]{:S(2)}, u32[]{:S(2)}) collective-permute-start(f32[4,64,256]{2,1,0:T(8,128)S(1)} %get-tuple-element.51), channel_id=1, source_target_pairs={{0,7},{1,0},{2,1},{3,2},{4,3},{5,4},{6,5},{7,6},{8,15},{9,8},{10,9... | collective-permute-start | bytes 786440 | tf_op jit(solution)/shard_map/ppermute | solution.py:46
  67.2 12.8 %collective-permute-start.19 = (f32[13,16,256]{2,1,0:T(8,128)S(1)}, f32[13,16,256]{2,1,0:T(8,128)S(1)}, u32[]{:S(2)}, u32[]{:S(2)}) collective-permute-start(f32[13,16,256]{2,1,0:T(8,128)S(1)} %get-tuple-element.50), channel_id=1, source_target_pairs={{0,24},{1,25},{2,26},{3,27},{4,28},{5,29},{6,30},{7,31},{8,0},{9,1... | collective-permute-start | bytes 638984 | tf_op jit(solution)/shard_map/ppermute | solution.py:46
  69.1 10.8 %collective-permute-start.21 = (f32[16,256]{1,0:T(8,128)S(1)}, f32[16,256]{1,0:T(8,128)S(1)}, u32[]{:S(2)}, u32[]{:S(2)}) collective-permute-start(f32[16,256]{1,0:T(8,128)S(1)} %get-tuple-element.52), channel_id=1, source_target_pairs={{0,31},{1,24},{2,25},{3,26},{4,27},{5,28},{6,29},{7,30},{8,7},{9,0... | collective-permute-start | bytes 49160 | tf_op jit(solution)/shard_map/ppermute | solution.py:46
  80.0 2.2 %copy-start.2 = (f32[8,2,512,128]{3,2,1,0:T(8,128)S(1)}, f32[8,2,512,128]{3,2,1,0:T(8,128)}, u32[]{:S(2)}) copy-start(f32[8,2,512,128]{3,2,1,0:T(8,128)} %copy-done.1) | copy-start | bytes 12582916
  87.7 2.2 %collective-permute-start.22 = (f32[128,256]{1,0:T(8,128)S(1)}, f32[128,256]{1,0:T(8,128)S(1)}, u32[]{:S(2)}, u32[]{:S(2)}) collective-permute-start(f32[128,256]{1,0:T(8,128)S(1)} %constant_dynamic-slice_fusion), channel_id=1, source_target_pairs={{0,1},{1,0},{2,3},{3,2},{4,5},{5,4},{6,7},{7,6},{8,9},{9,8},{10,11... | collective-permute-start | bytes 393224 | tf_op jit(solution)/shard_map/ppermute | solution.py:50
  89.9 8.0 %collective-permute-start.23 = (f32[128,256]{1,0:T(8,128)S(1)}, f32[128,256]{1,0:T(8,128)S(1)}, u32[]{:S(2)}, u32[]{:S(2)}) collective-permute-start(f32[128,256]{1,0:T(8,128)S(1)} %dynamic-slice_add_fusion), channel_id=1, source_target_pairs={{0,8},{8,0},{16,24},{24,16},{1,9},{9,1},{17,25},{25,17},{2,10},{10... | collective-permute-start | bytes 393224 | tf_op jit(solution)/shard_map/ppermute | solution.py:50
  92.4 12.9 %collective-permute-start.24 = (f32[128,256]{1,0:T(8,128)S(1)}, f32[128,256]{1,0:T(8,128)S(1)}, u32[]{:S(2)}, u32[]{:S(2)}) collective-permute-start(f32[128,256]{1,0:T(8,128)S(1)} %dynamic-slice_add_fusion), channel_id=1, source_target_pairs={{0,16},{8,24},{16,0},{24,8},{1,17},{9,25},{17,1},{25,9},{2,18},{10... | collective-permute-start | bytes 393224 | tf_op jit(solution)/shard_map/ppermute | solution.py:50
  92.9 12.3 %collective-permute-start.25 = (f32[128,256]{1,0:T(8,128)S(1)}, f32[128,256]{1,0:T(8,128)S(1)}, u32[]{:S(2)}, u32[]{:S(2)}) collective-permute-start(f32[128,256]{1,0:T(8,128)S(1)} %dynamic-slice_add_fusion), channel_id=1, source_target_pairs={{0,24},{8,16},{16,8},{24,0},{1,25},{9,17},{17,9},{25,1},{2,26},{10... | collective-permute-start | bytes 393224 | tf_op jit(solution)/shard_map/ppermute | solution.py:50
  105.3 7.1 %collective-permute-start.26 = (f32[128,256]{1,0:T(8,128)S(1)}, f32[128,256]{1,0:T(8,128)S(1)}, u32[]{:S(2)}, u32[]{:S(2)}) collective-permute-start(f32[128,256]{1,0:T(8,128)S(1)} %add_add_fusion.1), channel_id=1, source_target_pairs={{0,2},{1,3},{2,0},{3,1},{4,6},{5,7},{6,4},{7,5},{8,10},{9,11},{10,... | collective-permute-start | bytes 393224 | tf_op jit(solution)/shard_map/ppermute | solution.py:50
  108.2 6.4 %collective-permute-start.27 = (f32[128,256]{1,0:T(8,128)S(1)}, f32[128,256]{1,0:T(8,128)S(1)}, u32[]{:S(2)}, u32[]{:S(2)}) collective-permute-start(f32[128,256]{1,0:T(8,128)S(1)} %add_add_fusion.1), channel_id=1, source_target_pairs={{0,4},{1,5},{2,6},{3,7},{4,0},{5,1},{6,2},{7,3},{8,12},{9,13},{10,... | collective-permute-start | bytes 393224 | tf_op jit(solution)/shard_map/ppermute | solution.py:50
  108.2 6.4 %collective-permute-start.28 = (f32[128,256]{1,0:T(8,128)S(1)}, f32[128,256]{1,0:T(8,128)S(1)}, u32[]{:S(2)}, u32[]{:S(2)}) collective-permute-start(f32[128,256]{1,0:T(8,128)S(1)} %add_add_fusion.1), channel_id=1, source_target_pairs={{0,6},{1,7},{2,4},{3,5},{4,2},{5,3},{6,0},{7,1},{8,14},{9,15},{10,... | collective-permute-start | bytes 393224 | tf_op jit(solution)/shard_map/ppermute | solution.py:50
  114.6 1.4 %collective-permute-start.29 = (f32[128,256]{1,0:T(8,128)S(1)}, f32[128,256]{1,0:T(8,128)S(1)}, u32[]{:S(2)}, u32[]{:S(2)}) collective-permute-start(f32[128,256]{1,0:T(8,128)S(1)} %add_add_fusion), channel_id=1, source_target_pairs={{0,1},{1,0},{2,3},{3,2},{4,5},{5,4},{6,7},{7,6},{8,9},{9,8},{10,11... | collective-permute-start | bytes 393224 | tf_op jit(solution)/shard_map/ppermute | solution.py:50

commit v3 on v2

--- a/solution.py
+++ b/solution.py
@@ -14,22 +14,27 @@
 LATER = 2.0 / filter_half
 AXES = ("dx", "dy")
 VMEM = pl.BlockSpec(memory_space=pltpu.VMEM)
-LIMIT = 12 * 1024 * 1024
+LIMIT = 16 * 1024 * 1024
 LANES = 128
 ROWS = 8
 
 
-def partner(index, size, pairing):
+def partner(index, size, pairing, closed):
     if pairing == "-":
         return index
     other = index ^ 1 if pairing == "A" else index - 1 if index % 2 == 0 else index + 1
-    return other if 0 <= other < size else index
+    if 0 <= other < size:
+        return other
+    return size - 1 - index if closed and pairing == "B" and size % 2 == 0 else index
 
 
 def pair_swap(value, along_x, along_y):
     size_x, size_y = lax.axis_size("dx"), lax.axis_size("dy")
     route = [
-        (p * size_y + q, partner(p, size_x, along_x) * size_y + partner(q, size_y, along_y))
+        (
+            p * size_y + q,
+            partner(p, size_x, along_x, False) * size_y + partner(q, size_y, along_y, True),
+        )
         for p in range(size_x)
         for q in range(size_y)
     ]
@@ -50,17 +55,9 @@
     return lax.ppermute(value, axis, [(i, i ^ bits) for i in range(lax.axis_size(axis))])
 
 
-def total(gram):
-    sizes = [lax.axis_size(axis) for axis in AXES]
-    if any(size & (size - 1) or size < 2 for size in sizes):
-        return lax.psum(gram, AXES)
-    half = gram.shape[0] // 2
-    odd = lax.axis_index("dy") % 2
-    kept = lax.dynamic_slice_in_dim(gram, odd * half, half, 0)
-    sent = lax.dynamic_slice_in_dim(gram, (1 - odd) * half, half, 0)
+def halved_total(kept, sent):
     part = kept + xor_swap(sent, "dy", 1)
-    for axis, first in (("dx", 1), ("dy", 2)):
-        bit = first
+    for axis, bit in (("dx", 1), ("dy", 2)):
         while bit < lax.axis_size(axis):
             if 2 * bit < lax.axis_size(axis):
                 one, two, three = [xor_swap(part, axis, bit * k) for k in (1, 2, 3)]
@@ -69,10 +66,7 @@
             else:
                 part = part + xor_swap(part, axis, bit)
                 bit *= 2
-    other = xor_swap(part, "dy", 1)
-    low = jnp.where(odd == 0, part, other)
-    high = jnp.where(odd == 0, other, part)
-    return jnp.concatenate([low, high], axis=0)
+    return part, xor_swap(part, "dy", 1)
 
 
 def renumber_kernel(conn_ref, mats_ref, out_ref, *, side, width, depth, layers):
@@ -268,13 +262,25 @@
 
     put_x_face(g, w_ref, by_pair(even_x, sends[0], sends[1]))
     put_y_face(g, w_ref, by_pair(even_y, sends[2], sends[3]))
-    for h in range(w_ref.shape[1]):
+
+
+def corner_kernel(from_a, from_b, to_a, to_b, *, g):
+    even = lax.axis_index("dy") % 2 == 0
+    last = from_a.shape[1] - 1
+    bands = from_a.shape[2]
+    for k, source in enumerate((from_a, from_b)):
         for e3 in range(g.ez):
-            where = (slice(e3 * g.side, (e3 + 1) * g.side), lanes(h))
-            at_x = [[line(g, w_ref, hx, hy, e3, h) for hy in (0, 1)] for hx in (0, 1)]
-            for my in (0, 1):
-                low, high = [jnp.where(even_y, at_x[hx][1 - my], at_x[hx][my]) for hx in (0, 1)]
-                by_pair(even_x, sends[4 + my], sends[6 + my])(where, low, high)
+            low, number, start = g.layers(e3)
+            for c in range(g.side):
+                row = slice(e3 * g.side + c, e3 * g.side + c + 1)
+                if low <= c < low + number:
+                    z = start + c - low
+                    bottom, top = source[z, 0:1], source[z, last : last + 1]
+                    to_a[k, row] = jnp.where(even, top, bottom)
+                    to_b[k, row] = jnp.where(even, bottom, top)
+                else:
+                    to_a[k, row] = jnp.zeros((1, bands), jnp.float32)
+                    to_b[k, row] = jnp.zeros((1, bands), jnp.float32)
 
 
 def add_all(g, out_ref, received, factor):
@@ -301,8 +307,10 @@
         for hy in (0, 1):
 
             def diagonal(where):
-                one = from_pair(even_y, hy, received[4][where], received[5][where], has_y[hy])
-                two = from_pair(even_y, hy, received[6][where], received[7][where], has_y[hy])
+                one, two = [
+                    from_pair(even_y, hy, received[4][k, *where], received[5][k, *where], has_y[hy])
+                    for k in (0, 1)
+                ]
                 return from_pair(even_x, hx, one, two, has_x[hx])
 
             add_line(g, out_ref, hx, hy, diagonal, factor)
@@ -361,7 +369,7 @@
 
 def middle_kernel(*refs, g):
     part_ref, *refs = refs
-    received, refs = refs[:8], refs[8:]
+    received, refs = refs[:6], refs[6:]
     older_ref, mats_ref, y_ref, next_ref, *sends = refs
     y_ref[...] = part_ref[...]
     add_all(g, y_ref, received, FIRST)
@@ -372,7 +380,7 @@
 
 def late_kernel(*refs, g):
     part_ref, *refs = refs
-    received, refs = refs[:8], refs[8:]
+    received, refs = refs[:6], refs[6:]
     older_ref, mats_ref, next_ref, *sends, y_ref = refs
     y_ref[...] = part_ref[...]
     add_all(g, y_ref, received, LATER)
@@ -393,7 +401,52 @@
     advance(next_ref, y_ref, older_ref, LATER)
 
 
-def last_kernel(part_ref, from_x, from_y, from_xy, out_ref, y_ref, *, g):
+def split(value):
+    high = value.astype(jnp.bfloat16)
+    return high, (value - high.astype(jnp.float32)).astype(jnp.bfloat16)
+
+
+def packed_rows(bands):
+    count = bands // LANES
+    return count * bands if count != 2 else bands + 2 * ROWS
+
+
+def pack(gram, put):
+    count = gram.shape[0] // LANES
+    block = lambda i, j: gram[lanes(i), lanes(j)]
+    if count != 2:
+        for i in range(count):
+            for j in range(count):
+                put((i * count + j) * LANES, block(i, j))
+        return
+    row = lax.broadcasted_iota(jnp.int32, (LANES, LANES), 0)
+    lane = lax.broadcasted_iota(jnp.int32, (LANES, LANES), 1)
+    put(0, jnp.where(row >= lane, block(0, 0), block(1, 1)))
+    put(LANES, block(1, 0))
+    diagonal = jnp.sum(jnp.where(row == lane, block(1, 1), 0.0), axis=0, keepdims=True)
+    put(2 * LANES, jnp.broadcast_to(diagonal, (2 * ROWS, LANES)))
+
+
+def unpack(packed, count):
+    block = lambda k: packed[k * LANES : (k + 1) * LANES]
+    if count != 2:
+        return lambda i, j: block(i * count + j)
+    row = lax.broadcasted_iota(jnp.int32, (LANES, LANES), 0)
+    lane = lax.broadcasted_iota(jnp.int32, (LANES, LANES), 1)
+    both = block(0)
+    first = jnp.where(row > lane, both, 0.0)
+    second = jnp.where(row < lane, both, 0.0)
+    diagonal = jnp.broadcast_to(packed[2 * LANES : 2 * LANES + 1], (LANES, LANES))
+    blocks = {
+        (0, 0): first + first.T + jnp.where(row == lane, both, 0.0),
+        (1, 0): block(1),
+        (1, 1): second + second.T + jnp.where(row == lane, diagonal, 0.0),
+    }
+    return lambda i, j: blocks[i, j]
+
+
+def last_kernel(part_ref, from_x, from_y, from_xy, *refs, g):
+    high_ref, low_ref, kept_ref, sent_ref, y_ref, out_ref, packed_ref = refs
     side = g.side
     y_ref[...] = part_ref[...]
     p, q = lax.axis_index("dx"), lax.axis_index("dy")
@@ -412,8 +465,30 @@
             for h in range(y_ref.shape[1]):
                 d0 = pltpu.roll(y_ref[g.at(e1, 0, e3), h, rows], side - 1, 0)
                 d1 = pltpu.roll(y_ref[g.at(e1, 1, e3), h, rows], side - 2, 0)
-                out_ref[i, k, :side, lanes(h)] = jnp.where(sub < g.deg, d0, d1)
-                out_ref[i, k, side:, lanes(h)] = jnp.where(sub < rest, d1, 0.0)
+                start = (i * g.nz + k) * 2 * side
+                out_ref[start : start + side, lanes(h)] = jnp.where(sub < g.deg, d0, d1)
+                bottom = slice(start + side, start + 2 * side)
+                out_ref[bottom, lanes(h)] = jnp.where(sub < rest, d1, 0.0)
+    high, low = split(out_ref[...])
+    high_ref[...] = high
+    low_ref[...] = low
+    inner = functools.partial(
+        lax.dot_general,
+        dimension_numbers=(((0,), (0,)), ((), ())),
+        preferred_element_type=jnp.float32,
+    )
+    mixed = inner(high, low)
+    gram = inner(high, high) + (mixed + mixed.T) + inner(low, low)
+
+    def put(start, rows):
+        packed_ref[start : start + rows.shape[0]] = rows
+
+    pack(gram, put)
+    half = kept_ref.shape[0]
+    odd = lax.axis_index("dy") % 2 == 1
+    first, second = packed_ref[:half], packed_ref[half:]
+    kept_ref[...] = jnp.where(odd, second, first)
+    sent_ref[...] = jnp.where(odd, first, second)
 
 
 def invert_block(block):
@@ -499,13 +574,35 @@
             inv[i, j] = -dot(inv[i, i], sums[j])
     return inv
 
-def factor_kernel(gram_ref, out_ref):
-    count = gram_ref.shape[0] // LANES
-    inverse = inverse_factor(lambda i, j: gram_ref[lanes(i), lanes(j)], count)
-    for i in range(count):
-        for j in range(count):
-            block = inverse[i, j] if j <= i else jnp.zeros((LANES, LANES), jnp.float32)
-            out_ref[lanes(i), lanes(j)] = block
+def basis_kernel(mine_ref, other_ref, high_ref, low_ref, out_ref, factor_ref, *, scale):
+    @pl.when(pl.program_id(0) == 0)
+    def _():
+        count = high_ref.shape[1] // LANES
+        odd = lax.axis_index("dy") % 2 == 1
+        mine, other = mine_ref[...], other_ref[...]
+        packed = jnp.concatenate(
+            [jnp.where(odd, other, mine), jnp.where(odd, mine, other)], axis=0
+        )
+        inverse = inverse_factor(unpack(packed, count), count)
+        for i in range(count):
+            for j in range(count):
+                block = inverse[i, j] * scale if j <= i else jnp.zeros((LANES, LANES), jnp.float32)
+                high, low = split(block)
+                factor_ref[0, lanes(i), lanes(j)] = high
+                factor_ref[1, lanes(i), lanes(j)] = low
+
+    slab, nz, ny, bands = out_ref.shape
+    rows = high_ref.shape[0] // pl.num_programs(0)
+    here = pl.ds(pl.multiple_of(pl.program_id(0) * rows, rows), rows)
+    times = functools.partial(
+        lax.dot_general,
+        dimension_numbers=(((1,), (1,)), ((), ())),
+        preferred_element_type=jnp.float32,
+    )
+    high, low = high_ref[here], low_ref[here]
+    result = times(high, factor_ref[0]) + (times(high, factor_ref[1]) + times(low, factor_ref[0]))
+    result = result.reshape(slab, nz, rows // (slab * nz), bands)
+    out_ref[...] = result[:, :, :ny]
 
 
 def call(kernel, outs, scratch, operands, flops):
@@ -538,10 +635,16 @@
     x_shape = shape((nz, g.ey * side, bands), f32)
     y_shape = shape((g.ex * g.ez, side * side, bands), f32)
     line_shape = shape((g.ez * side, bands), f32)
-    send_shapes = [x_shape] * 2 + [y_shape] * 2 + [line_shape] * 4
+    corner_shape = shape((2, *line_shape.shape), f32)
+    send_shapes = [x_shape] * 2 + [y_shape] * 2
     pairings = [("A", "-"), ("B", "-"), ("-", "A"), ("-", "B")]
-    pairings += [("A", "A"), ("A", "B"), ("B", "A"), ("B", "B")]
     flops = 2 * g.elements * g.count**2 * bands
+
+    def swap(sends):
+        faces = [pair_swap(s, *pair) for s, pair in zip(sends, pairings)]
+        kernel = functools.partial(corner_kernel, g=g)
+        lines = call(kernel, [corner_shape] * 2, [], tuple(faces[:2]), 0)
+        return *faces, *[pair_swap(s, *pair) for s, pair in zip(lines, pairings[2:])]
 
     y0, part, *sends = call(
         functools.partial(first_kernel, g=g),
@@ -550,7 +653,7 @@
         (orb, below_x, below_y, below_xy, mats),
         flops,
     )
-    received = [pair_swap(s, *pair) for s, pair in zip(sends, pairings)]
+    received = swap(sends)
     y1, part, *sends = call(
         functools.partial(middle_kernel, g=g),
         [shape(nodes, f32), shape(nodes, f32), *send_shapes],
@@ -558,7 +661,7 @@
         (part, *received, y0, mats),
         flops,
     )
-    received = [pair_swap(s, *pair) for s, pair in zip(sends, pairings)]
+    received = swap(sends)
     part, *sends = call(
         functools.partial(late_kernel, g=g),
         [shape(nodes, f32), x_shape, y_shape, line_shape],
@@ -567,23 +670,29 @@
         flops,
     )
     received = [ring(s, *step) for s, step in zip(sends, ((-1, 0), (0, -1), (-1, -1)))]
-    (y3,) = call(
+    rows = nx * nz * 2 * side
+    packed = packed_rows(bands)
+    half_shape = shape((packed // 2, LANES), f32)
+    high, low, kept, sent = call(
         functools.partial(last_kernel, g=g),
-        [shape((nx, nz, 2 * side, bands), f32)],
-        [pltpu.VMEM(nodes, f32)],
+        [shape((rows, bands), jnp.bfloat16)] * 2 + [half_shape] * 2,
+        [pltpu.VMEM(nodes, f32), pltpu.VMEM((rows, bands), f32), pltpu.VMEM((packed, LANES), f32)],
         (part, *received),
-        flops // 100,
-    )
-
-    columns = y3.reshape(-1, bands)
-    gram = jnp.einsum("rb,rc->bc", columns, columns, precision=lax.Precision.HIGHEST)
-    gram = total(gram)
-    (inverse_lower,) = call(
-        factor_kernel, [shape((bands, bands), f32)], [], (gram,), 2 * bands**3
-    )
-    basis = jnp.einsum("rb,cb->rc", columns, inverse_lower, precision=lax.Precision.HIGHEST)
-    scale = math.sqrt(nx * ny * nz * lax.axis_size(AXES))
-    basis = (basis * scale).reshape(nx, nz, 2 * side, bands)[:, :, :ny]
+        8 * rows * bands**2,
+    )
+    mine, other = halved_total(kept, sent)
+    slabs = g.ex * g.deg // 2
+    spot = pl.BlockSpec((nx // slabs, nz, ny, bands), lambda i: (i, 0, 0, 0))
+    basis = pl.pallas_call(
+        functools.partial(basis_kernel, scale=math.sqrt(nx * ny * nz * lax.axis_size(AXES))),
+        out_shape=shape((nx, nz, ny, bands), f32),
+        grid=(slabs,),
+        in_specs=[VMEM] * 4,
+        out_specs=spot,
+        scratch_shapes=[pltpu.VMEM((2, bands, bands), jnp.bfloat16)],
+        compiler_params=pltpu.CompilerParams(vmem_limit_bytes=LIMIT),
+        name="basis",
+    )(mine, other, high, low)
     return jnp.transpose(basis, (0, 2, 1, 3))
 
 

time: 132 us -> 98.9 us (0.75)
  starting transfers between devices: 58.3 us -> 32.1 us
  matrix products: 7.59 us -> 0 us
  Pallas kernels: 24.1 us -> 30.2 us
  local copies, waits for them, and re-layouts: 10.3 us -> 4.21 us
    ppermute x16 -> x12, starting transfers between devices: 30.3 us -> 12.3 us  [pair_swap(): return lax.ppermute(value, AXES, route)]
    pallas_call x0 -> x1, Pallas kernels: none -> 15.4 us  [shards(): pl.pallas_call(functools.partial(basis_kernel, scale=math.sqrt(nx * ny *...]
    pallas_call x5 -> x6, Pallas kernels: 18.4 us -> 9.1 us  [call(): pl.pallas_call(kernel, out_shape=outs, in_specs=[VMEM] * len(operands), o...]
    dot_general x2 -> x0, matrix products: 7.59 us -> none  [the longest x1 4.94 us: shards(): jnp.einsum('rb,rc->bc', columns, columns, precision=lax.Precision.HIGHEST)]
    ppermute x8, waiting for transfers between devices: 17.6 us -> 11.5 us  [xor_swap(): lax.ppermute(value, axis, [(i, i ^ bits) for i in range(lax.axis_size(axi...]
    ppermute x16 -> x12, waiting for transfers between devices: 10.8 us -> 16.8 us  [pair_swap(): return lax.ppermute(value, AXES, route)]
    ppermute x6, starting transfers between devices: 17.4 us -> 11.6 us  [ring(): return lax.ppermute(value, AXES, route)]
    unnamed x11 -> x7, local copies, waits for them, and re-layouts: 8.31 us -> 4.16 us
  transfers between devices with their start and end apart: 30 -> 26, of which waited for: 13 -> 14; matrix products, arithmetic and copies ran while one was open for 0% -> 0% of each run, Pallas kernels for 4% -> 6%
where the time goes in v3:
time: 98.9 us; the launch traced here: 98.8 us
  starting transfers between devices  32.1 us (32%)
  waiting for transfers between devices  32 us (32%)
  Pallas kernels  30.2 us (31%)
  local copies, waits for them, and re-layouts  4.21 us (4%)
    ppermute x12, waiting for transfers between devices, pair_swap(): return lax.ppermute(value, AXES, route)  16.8 us
    pallas_call x1, Pallas kernels, shards(): pl.pallas_call(functools.partial(basis_kernel, scale=math.sqrt(nx * ny *...  15.4 us
    ppermute x12, starting transfers between devices, pair_swap(): return lax.ppermute(value, AXES, route)  12.3 us
    ppermute x6, starting transfers between devices, ring(): return lax.ppermute(value, AXES, route)  11.6 us
    ppermute x8, waiting for transfers between devices, xor_swap(): lax.ppermute(value, axis, [(i, i ^ bits) for i in range(lax.axis_size(axi...  11.5 us
    pallas_call x6, Pallas kernels, call(): pl.pallas_call(kernel, out_shape=outs, in_specs=[VMEM] * len(operands), o...  9.1 us
    ppermute x8, starting transfers between devices, xor_swap(): lax.ppermute(value, axis, [(i, i ^ bits) for i in range(lax.axis_size(axi...  8.15 us
    pallas_call x1, Pallas kernels, renumber(): pl.pallas_call(functools.partial(renumber_kernel, side=side, width=width,...  5.73 us
  transfers between devices with their start and end apart: 26, of which 14 were waited for; matrix products, arithmetic and copies ran while one was open for 0% of the time, Pallas kernels for 6%

profile of v3, /device:TPU:0, one launch (start us, length us, event | category | flops | bytes accessed | tf_op | source)
XLA Modules:
  0.0 98.8 jit_solution(7727415364728560366)
XLA Ops:
  0.0 2.0 %copy.9 = bf16[14,14,13,256]{3,2,1,0:T(8,128)(2,1)S(1)} copy(bf16[14,14,13,256]{3,1,2,0:T(8,128)(2,1)} %param.3) | data formatting | bytes 2609152 | tf_op args[0]
  2.0 2.5 %collective-permute-start.2 = (bf16[13,256]{1,0:T(8,128)(2,1)S(1)}, bf16[13,256]{1,0:T(8,128)(2,1)S(1)}, u32[]{:S(2)}, u32[]{:S(2)}) collective-permute-start(bf16[13,256]{1,0:T(8,128)(2,1)S(1)} %slice_bitcast_fusion.2), channel_id=1, source_target_pairs={{0,9},{1,10},{2,11},{3,12},{4,13},{5,14},{6,15},{7,8},{8,17},{9,18... | collective-permute-start | bytes 19976 | tf_op jit(solution)/shard_map/ppermute | solution.py:51
  4.5 1.6 %collective-permute-start = (bf16[13,14,256]{2,0,1:T(8,128)(2,1)S(1)}, bf16[13,14,256]{2,0,1:T(8,128)(2,1)S(1)}, u32[]{:S(2)}, u32[]{:S(2)}) collective-permute-start(bf16[13,14,256]{2,0,1:T(8,128)(2,1)S(1)} %slice_bitcast_fusion.1), channel_id=1, source_target_pairs={{0,8},{1,9},{2,10},{3,11},{4,12},{5,13},{6,14},{7,15},{8,16},{9,17... | collective-permute-start | bytes 279560 | tf_op jit(solution)/shard_map/ppermute | solution.py:51
  6.2 1.4 %collective-permute-start.1 = (bf16[14,13,256]{2,1,0:T(8,128)(2,1)S(1)}, bf16[14,13,256]{2,1,0:T(8,128)(2,1)S(1)}, u32[]{:S(2)}, u32[]{:S(2)}) collective-permute-start(bf16[14,13,256]{2,1,0:T(8,128)(2,1)S(1)} %slice_bitcast_fusion), channel_id=1, source_target_pairs={{0,1},{1,2},{2,3},{3,4},{4,5},{5,6},{6,7},{7,0},{8,9},{9,10},{10,1... | collective-permute-start | bytes 279560 | tf_op jit(solution)/shard_map/ppermute | solution.py:51
  7.5 2.2 %copy-done.1 = bf16[2,2,2,512,512]{4,3,2,1,0:T(8,128)(2,1)S(1)} copy-done((bf16[2,2,2,512,512]{4,3,2,1,0:T(8,128)(2,1)S(1)}, bf16[2,2,2,512,512]{4,3,2,1,0:T(8,128)(2,1)}, u32[]{:S(2)}) %copy-start.1) | copy-done | bytes 4194328
  9.7 5.7 %renumber.1 = bf16[2,2,2,512,512]{4,3,2,1,0:T(8,128)(2,1)S(1)} custom-call(s32[2,2,2,512]{3,2,1,0:T(2,128)S(1)} %copy-done.2, bf16[2,2,2,512,512]{4,3,2,1,0:T(8,128)(2,1)S(1)} %copy-done.1), custom_call_target="tpu_custom_call" | custom-call | flops 4294967296 | bytes 8388608 | tf_op jit(solution)/shard_map/renumber/pallas_call | solution.py:108
  15.5 2.1 %shard_map.37 = (f32[8,2,512,128]{3,2,1,0:T(8,128)S(1)}, f32[8,2,512,128]{3,2,1,0:T(8,128)S(1)}, f32[13,16,256]{2,1,0:T(8,128)S(1)}, f32[13,16,256]{2,1,0:T(8,12...) custom-call(bf16[14,13,14,256]{3,2,1,0:T(8,128)(2,1)S(1)} %bitcast.15, ...), custom_call_target="tpu_custom_call" | custom-call | flops 1073741824 | bytes 15030784 | tf_op jit(solution)/shard_map/pallas_call | solution.py:610
  17.7 0.4 collective-permute-start.5
  18.1 1.2 %collective-permute-start.6 = (f32[4,64,256]{2,1,0:T(8,128)S(1)}, f32[4,64,256]{2,1,0:T(8,128)S(1)}, u32[]{:S(2)}, u32[]{:S(2)}) collective-permute-start(f32[4,64,256]{2,1,0:T(8,128)S(1)} %get-tuple-element.33), channel_id=1, source_target_pairs={{0,7},{1,2},{2,1},{3,4},{4,3},{5,6},{6,5},{7,0},{8,15},{9,10},{10,... | collective-permute-start | bytes 786440 | tf_op jit(solution)/shard_map/ppermute | solution.py:41
  19.3 1.6 %collective-permute-start.3 = (f32[13,16,256]{2,1,0:T(8,128)S(1)}, f32[13,16,256]{2,1,0:T(8,128)S(1)}, u32[]{:S(2)}, u32[]{:S(2)}) collective-permute-start(f32[13,16,256]{2,1,0:T(8,128)S(1)} %get-tuple-element.30), channel_id=1, source_target_pairs={{0,8},{1,9},{2,10},{3,11},{4,12},{5,13},{6,14},{7,15},{8,0},{9,1},... | collective-permute-start | bytes 638984 | tf_op jit(solution)/shard_map/ppermute | solution.py:41
  20.9 0.7 collective-permute-start.4
  21.6 5.3 %collective-permute-done.3.from_a.refs_1_ = f32[13,16,256]{2,1,0:T(8,128)S(1)} collective-permute-done((f32[13,16,256]{2,1,0:T(8,128)S(1)}, f32[13,16,256]{2,1,0:T(8,128)S(1)}, u32[]{:S(2)}, u32[]{:S(2)}) %collective-permute-start.3) | collective-permute-done | bytes 213024 | tf_op jit(solution)/shard_map/ppermute | solution.py:41
  26.9 0.1 collective-permute-start.7
  27.0 1.5 %collective-permute-start.8 = (f32[2,16,256]{2,1,0:T(8,128)S(1)}, f32[2,16,256]{2,1,0:T(8,128)S(1)}, u32[]{:S(2)}, u32[]{:S(2)}) collective-permute-start(f32[2,16,256]{2,1,0:T(8,128)S(1)} %get-tuple-element.35), channel_id=1, source_target_pairs={{0,7},{1,2},{2,1},{3,4},{4,3},{5,6},{6,5},{7,0},{8,15},{9,10},{10,... | collective-permute-start | bytes 98312 | tf_op jit(solution)/shard_map/ppermute | solution.py:41
  28.5 2.8 %collective-permute-done.8.refs_6_ = f32[2,16,256]{2,1,0:T(8,128)S(1)} collective-permute-done((f32[2,16,256]{2,1,0:T(8,128)S(1)}, f32[2,16,256]{2,1,0:T(8,128)S(1)}, u32[]{:S(2)}, u32[]{:S(2)}) %collective-permute-start.8) | collective-permute-done | bytes 32800 | tf_op jit(solution)/shard_map/ppermute | solution.py:41
  31.3 2.4 %shard_map.39 = (f32[8,2,512,128]{3,2,1,0:T(8,128)S(1)}, f32[8,2,512,128]{3,2,1,0:T(8,128)S(1)}, f32[13,16,256]{2,1,0:T(8,128)S(1)}, f32[13,16,256]{2,1,0:T(8,12...) custom-call(f32[8,2,512,128]{3,2,1,0:T(8,128)S(1)} %get-tuple-element.29.refs_0_, ...), custom_call_target="tpu_custom_call" | custom-call | flops 1073741824 | bytes 22937600 | tf_op jit(solution)/shard_map/pallas_call | solution.py:610
  33.8 0.1 collective-permute-start.11
  33.8 1.5 %collective-permute-start.12 = (f32[4,64,256]{2,1,0:T(8,128)S(1)}, f32[4,64,256]{2,1,0:T(8,128)S(1)}, u32[]{:S(2)}, u32[]{:S(2)}) collective-permute-start(f32[4,64,256]{2,1,0:T(8,128)S(1)} %get-tuple-element.41), channel_id=1, source_target_pairs={{0,7},{1,2},{2,1},{3,4},{4,3},{5,6},{6,5},{7,0},{8,15},{9,10},{10,... | collective-permute-start | bytes 786440 | tf_op jit(solution)/shard_map/ppermute | solution.py:41
  35.4 3.6 %collective-permute-start.9 = (f32[13,16,256]{2,1,0:T(8,128)S(1)}, f32[13,16,256]{2,1,0:T(8,128)S(1)}, u32[]{:S(2)}, u32[]{:S(2)}) collective-permute-start(f32[13,16,256]{2,1,0:T(8,128)S(1)} %get-tuple-element.38), channel_id=1, source_target_pairs={{0,8},{1,9},{2,10},{3,11},{4,12},{5,13},{6,14},{7,15},{8,0},{9,1},... | collective-permute-start | bytes 638984 | tf_op jit(solution)/shard_map/ppermute | solution.py:41
  39.0 0.7 collective-permute-start.10
  39.7 5.1 %collective-permute-done.9.from_a.refs_1_ = f32[13,16,256]{2,1,0:T(8,128)S(1)} collective-permute-done((f32[13,16,256]{2,1,0:T(8,128)S(1)}, f32[13,16,256]{2,1,0:T(8,128)S(1)}, u32[]{:S(2)}, u32[]{:S(2)}) %collective-permute-start.9) | collective-permute-done | bytes 213024 | tf_op jit(solution)/shard_map/ppermute | solution.py:41
  44.8 0.1 collective-permute-start.13
  44.8 0.8 collective-permute-start.14
  45.6 0.4 collective-permute-done.13.refs_5_
  46.0 3.3 %collective-permute-done.14.refs_6_ = f32[2,16,256]{2,1,0:T(8,128)S(1)} collective-permute-done((f32[2,16,256]{2,1,0:T(8,128)S(1)}, f32[2,16,256]{2,1,0:T(8,128)S(1)}, u32[]{:S(2)}, u32[]{:S(2)}) %collective-permute-start.14) | collective-permute-done | bytes 32800 | tf_op jit(solution)/shard_map/ppermute | solution.py:41
  49.3 2.5 %shard_map.41 = (f32[8,2,512,128]{3,2,1,0:T(8,128)S(1)}, f32[13,16,256]{2,1,0:T(8,128)S(1)}, f32[4,64,256]{2,1,0:T(8,128)S(1)}, f32[16,256]{1,0:T(8,128)S(1)}) custom-call(f32[8,2,512,128]{3,2,1,0:T(8,128)S(1)} %get-tuple-element.37.refs_0_, f32[13,16,256]{2,1,0:T(8,128)S(1)} %collective-permute-done.9.from_a.refs_1_, ...), custom_call_target="tpu_custom_call" | custom-call | flops 1073741824 | bytes 18284544 | tf_op jit(solution)/shard_map/pallas_call | solution.py:610
  51.8 0.6 collective-permute-start.16
  52.3 2.3 %collective-permute-start.15 = (f32[13,16,256]{2,1,0:T(8,128)S(1)}, f32[13,16,256]{2,1,0:T(8,128)S(1)}, u32[]{:S(2)}, u32[]{:S(2)}) collective-permute-start(f32[13,16,256]{2,1,0:T(8,128)S(1)} %get-tuple-element.46), channel_id=1, source_target_pairs={{0,24},{1,25},{2,26},{3,27},{4,28},{5,29},{6,30},{7,31},{8,0},{9,1... | collective-permute-start | bytes 638984 | tf_op jit(solution)/shard_map/ppermute | solution.py:51
  54.6 3.3 %collective-permute-start.17 = (f32[16,256]{1,0:T(8,128)S(1)}, f32[16,256]{1,0:T(8,128)S(1)}, u32[]{:S(2)}, u32[]{:S(2)}) collective-permute-start(f32[16,256]{1,0:T(8,128)S(1)} %get-tuple-element.48), channel_id=1, source_target_pairs={{0,31},{1,24},{2,25},{3,26},{4,27},{5,28},{6,29},{7,30},{8,7},{9,0... | collective-permute-start | bytes 49160 | tf_op jit(solution)/shard_map/ppermute | solution.py:51
  57.9 2.6 %collective-permute-done.17.from_xy = f32[16,256]{1,0:T(8,128)S(1)} collective-permute-done((f32[16,256]{1,0:T(8,128)S(1)}, f32[16,256]{1,0:T(8,128)S(1)}, u32[]{:S(2)}, u32[]{:S(2)}) %collective-permute-start.17) | collective-permute-done | bytes 16416 | tf_op jit(solution)/shard_map/ppermute | solution.py:51
  60.6 1.0 %collective-permute-done.15.from_x = f32[13,16,256]{2,1,0:T(8,128)S(1)} collective-permute-done((f32[13,16,256]{2,1,0:T(8,128)S(1)}, f32[13,16,256]{2,1,0:T(8,128)S(1)}, u32[]{:S(2)}, u32[]{:S(2)}) %collective-permute-start.15) | collective-permute-done | bytes 213024 | tf_op jit(solution)/shard_map/ppermute | solution.py:51
  61.6 2.0 %shard_map.42 = (bf16[2912,256]{1,0:T(8,128)(2,1)S(1)}, bf16[2912,256]{1,0:T(8,128)(2,1)S(1)}, f32[136,128]{1,0:T(8,128)S(1)}, f32[136,128]{1,0:T(8,128)S(1)}) custom-call(f32[8,2,512,128]{3,2,1,0:T(8,128)S(1)} %get-tuple-element.45.part_ref, f32[13,16,256]{2,1,0:T(8,128)S(1)} %collective-permute-done.15.from_x, ...), custom_call_target="tpu_custom_call" | custom-call | flops 1526726656 | bytes 7806976 | tf_op jit(solution)/shard_map/pallas_call | solution.py:610
  63.6 0.1 collective-permute-start.18
  63.7 1.2 %collective-permute-done.18 = f32[136,128]{1,0:T(8,128)S(1)} collective-permute-done((f32[136,128]{1,0:T(8,128)S(1)}, f32[136,128]{1,0:T(8,128)S(1)}, u32[]{:S(2)}, u32[]{:S(2)}) %collective-permute-start.18) | collective-permute-done | bytes 69664 | tf_op jit(solution)/shard_map/ppermute | solution.py:55
  65.0 2.4 %collective-permute-start.21 = (f32[136,128]{1,0:T(8,128)S(1)}, f32[136,128]{1,0:T(8,128)S(1)}, u32[]{:S(2)}, u32[]{:S(2)}) collective-permute-start(f32[136,128]{1,0:T(8,128)S(1)} %add.21), channel_id=1, source_target_pairs={{0,24},{8,16},{16,8},{24,0},{1,25},{9,17},{17,9},{25,1},{2,26},{10... | collective-permute-start | bytes 208904 | tf_op jit(solution)/shard_map/ppermute | solution.py:55
  67.4 0.9 collective-permute-start.20
  68.2 1.2 %collective-permute-start.19 = (f32[136,128]{1,0:T(8,128)S(1)}, f32[136,128]{1,0:T(8,128)S(1)}, u32[]{:S(2)}, u32[]{:S(2)}) collective-permute-start(f32[136,128]{1,0:T(8,128)S(1)} %add.21), channel_id=1, source_target_pairs={{0,8},{8,0},{16,24},{24,16},{1,9},{9,1},{17,25},{25,17},{2,10},{10... | collective-permute-start | bytes 208904 | tf_op jit(solution)/shard_map/ppermute | solution.py:55
  69.4 2.0 %collective-permute-done.21 = f32[136,128]{1,0:T(8,128)S(1)} collective-permute-done((f32[136,128]{1,0:T(8,128)S(1)}, f32[136,128]{1,0:T(8,128)S(1)}, u32[]{:S(2)}, u32[]{:S(2)}) %collective-permute-start.21) | collective-permute-done | bytes 69664 | tf_op jit(solution)/shard_map/ppermute | solution.py:55
  71.4 3.5 %collective-permute-done.20 = f32[136,128]{1,0:T(8,128)S(1)} collective-permute-done((f32[136,128]{1,0:T(8,128)S(1)}, f32[136,128]{1,0:T(8,128)S(1)}, u32[]{:S(2)}, u32[]{:S(2)}) %collective-permute-start.20) | collective-permute-done | bytes 69664 | tf_op jit(solution)/shard_map/ppermute | solution.py:55
  74.9 2.3 %collective-permute-start.24 = (f32[136,128]{1,0:T(8,128)S(1)}, f32[136,128]{1,0:T(8,128)S(1)}, u32[]{:S(2)}, u32[]{:S(2)}) collective-permute-start(f32[136,128]{1,0:T(8,128)S(1)} %add_add_fusion.1), channel_id=1, source_target_pairs={{0,6},{1,7},{2,4},{3,5},{4,2},{5,3},{6,0},{7,1},{8,14},{9,15},{10,... | collective-permute-start | bytes 208904 | tf_op jit(solution)/shard_map/ppermute | solution.py:55
  77.2 0.5 collective-permute-start.23
  77.7 0.8 collective-permute-start.22
  78.5 1.8 %collective-permute-done.24 = f32[136,128]{1,0:T(8,128)S(1)} collective-permute-done((f32[136,128]{1,0:T(8,128)S(1)}, f32[136,128]{1,0:T(8,128)S(1)}, u32[]{:S(2)}, u32[]{:S(2)}) %collective-permute-start.24) | collective-permute-done | bytes 69664 | tf_op jit(solution)/shard_map/ppermute | solution.py:55
  80.3 1.2 %collective-permute-done.23 = f32[136,128]{1,0:T(8,128)S(1)} collective-permute-done((f32[136,128]{1,0:T(8,128)S(1)}, f32[136,128]{1,0:T(8,128)S(1)}, u32[]{:S(2)}, u32[]{:S(2)}) %collective-permute-start.23) | collective-permute-done | bytes 69664 | tf_op jit(solution)/shard_map/ppermute | solution.py:55
  81.5 0.5 collective-permute-done.22
  82.0 0.1 collective-permute-start.25
  82.1 1.2 %collective-permute-done.25.other_ref = f32[136,128]{1,0:T(8,128)S(1)} collective-permute-done((f32[136,128]{1,0:T(8,128)S(1)}, f32[136,128]{1,0:T(8,128)S(1)}, u32[]{:S(2)}, u32[]{:S(2)}) %collective-permute-start.25) | collective-permute-done | bytes 69664 | tf_op jit(solution)/shard_map/ppermute | solution.py:55
  83.4 15.4 %basis.1 = f32[14,13,14,256]{3,2,1,0:T(8,128)} custom-call(f32[136,128]{1,0:T(8,128)S(1)} %add_add_fusion.mine_ref, f32[136,128]{1,0:T(8,128)S(1)} %collective-permute-done.25.other_ref, bf16[2912,256]{1,0:T(8,128)(2,1)S(1)} %get-tuple-element.51.high_ref, bf16[2912,256]{1,0:T(8,128)(2,1)S(1)} %get-tuple-element.52.low_ref), custom_call_target="tpu_custom_call" | custom-call | tf_op jit(solution)/shard_map/basis/pallas_call | solution.py:686
  (26 shorter events, 0.2 us)
Async XLA Ops:
  0.0 7.5 %copy-start.2 = (s32[2,2,2,512]{3,2,1,0:T(2,128)S(1)}, s32[2,2,2,512]{3,2,1,0:T(2,128)}, u32[]{:S(2)}) copy-start(s32[2,2,2,512]{3,2,1,0:T(2,128)} %conn_ref.1) | copy-start | bytes 49156
  2.0 13.5 %collective-permute-start.2 = (bf16[13,256]{1,0:T(8,128)(2,1)S(1)}, bf16[13,256]{1,0:T(8,128)(2,1)S(1)}, u32[]{:S(2)}, u32[]{:S(2)}) collective-permute-start(bf16[13,256]{1,0:T(8,128)(2,1)S(1)} %slice_bitcast_fusion.2), channel_id=1, source_target_pairs={{0,9},{1,10},{2,11},{3,12},{4,13},{5,14},{6,15},{7,8},{8,17},{9,18... | collective-permute-start | bytes 19976 | tf_op jit(solution)/shard_map/ppermute | solution.py:51
  4.5 11.0 %collective-permute-start = (bf16[13,14,256]{2,0,1:T(8,128)(2,1)S(1)}, bf16[13,14,256]{2,0,1:T(8,128)(2,1)S(1)}, u32[]{:S(2)}, u32[]{:S(2)}) collective-permute-start(bf16[13,14,256]{2,0,1:T(8,128)(2,1)S(1)} %slice_bitcast_fusion.1), channel_id=1, source_target_pairs={{0,8},{1,9},{2,10},{3,11},{4,12},{5,13},{6,14},{7,15},{8,16},{9,17... | collective-permute-start | bytes 279560 | tf_op jit(solution)/shard_map/ppermute | solution.py:51
  6.1 9.4 %copy-start = (bf16[14,14,13,256]{3,1,2,0:T(8,128)(2,1)S(1)}, bf16[14,14,13,256]{3,1,2,0:T(8,128)(2,1)}, u32[]{:S(2)}) copy-start(bf16[14,14,13,256]{3,1,2,0:T(8,128)(2,1)} %param.3) | copy-start | bytes 3913732
  6.2 9.4 %collective-permute-start.1 = (bf16[14,13,256]{2,1,0:T(8,128)(2,1)S(1)}, bf16[14,13,256]{2,1,0:T(8,128)(2,1)S(1)}, u32[]{:S(2)}, u32[]{:S(2)}) collective-permute-start(bf16[14,13,256]{2,1,0:T(8,128)(2,1)S(1)} %slice_bitcast_fusion), channel_id=1, source_target_pairs={{0,1},{1,2},{2,3},{3,4},{4,5},{5,6},{6,7},{7,0},{8,9},{9,10},{10,1... | collective-permute-start | bytes 279560 | tf_op jit(solution)/shard_map/ppermute | solution.py:51
  7.5 2.2 %copy-start.1 = (bf16[2,2,2,512,512]{4,3,2,1,0:T(8,128)(2,1)S(1)}, bf16[2,2,2,512,512]{4,3,2,1,0:T(8,128)(2,1)}, u32[]{:S(2)}) copy-start(bf16[2,2,2,512,512]{4,3,2,1,0:T(8,128)(2,1)} %mats_ref.1) | copy-start | bytes 12582916
  17.7 13.6 %collective-permute-start.5 = (f32[4,64,256]{2,1,0:T(8,128)S(1)}, f32[4,64,256]{2,1,0:T(8,128)S(1)}, u32[]{:S(2)}, u32[]{:S(2)}) collective-permute-start(f32[4,64,256]{2,1,0:T(8,128)S(1)} %get-tuple-element.32), channel_id=1, source_target_pairs={{0,1},{1,0},{2,3},{3,2},{4,5},{5,4},{6,7},{7,6},{8,9},{9,8},{10,11... | collective-permute-start | bytes 786440 | tf_op jit(solution)/shard_map/ppermute | solution.py:41
  18.1 13.2 %collective-permute-start.6 = (f32[4,64,256]{2,1,0:T(8,128)S(1)}, f32[4,64,256]{2,1,0:T(8,128)S(1)}, u32[]{:S(2)}, u32[]{:S(2)}) collective-permute-start(f32[4,64,256]{2,1,0:T(8,128)S(1)} %get-tuple-element.33), channel_id=1, source_target_pairs={{0,7},{1,2},{2,1},{3,4},{4,3},{5,6},{6,5},{7,0},{8,15},{9,10},{10,... | collective-permute-start | bytes 786440 | tf_op jit(solution)/shard_map/ppermute | solution.py:41
  19.3 7.5 %collective-permute-start.3 = (f32[13,16,256]{2,1,0:T(8,128)S(1)}, f32[13,16,256]{2,1,0:T(8,128)S(1)}, u32[]{:S(2)}, u32[]{:S(2)}) collective-permute-start(f32[13,16,256]{2,1,0:T(8,128)S(1)} %get-tuple-element.30), channel_id=1, source_target_pairs={{0,8},{1,9},{2,10},{3,11},{4,12},{5,13},{6,14},{7,15},{8,0},{9,1},... | collective-permute-start | bytes 638984 | tf_op jit(solution)/shard_map/ppermute | solution.py:41
  20.9 5.9 %collective-permute-start.4 = (f32[13,16,256]{2,1,0:T(8,128)S(1)}, f32[13,16,256]{2,1,0:T(8,128)S(1)}, u32[]{:S(2)}, u32[]{:S(2)}) collective-permute-start(f32[13,16,256]{2,1,0:T(8,128)S(1)} %get-tuple-element.31), channel_id=1, source_target_pairs={{0,0},{1,1},{2,2},{3,3},{4,4},{5,5},{6,6},{7,7},{8,16},{9,17},{10,... | collective-permute-start | bytes 638984 | tf_op jit(solution)/shard_map/ppermute | solution.py:41
  26.9 1.6 %collective-permute-start.7 = (f32[2,16,256]{2,1,0:T(8,128)S(1)}, f32[2,16,256]{2,1,0:T(8,128)S(1)}, u32[]{:S(2)}, u32[]{:S(2)}) collective-permute-start(f32[2,16,256]{2,1,0:T(8,128)S(1)} %get-tuple-element.34), channel_id=1, source_target_pairs={{0,1},{1,0},{2,3},{3,2},{4,5},{5,4},{6,7},{7,6},{8,9},{9,8},{10,11... | collective-permute-start | bytes 98312 | tf_op jit(solution)/shard_map/ppermute | solution.py:41
  27.0 4.3 %collective-permute-start.8 = (f32[2,16,256]{2,1,0:T(8,128)S(1)}, f32[2,16,256]{2,1,0:T(8,128)S(1)}, u32[]{:S(2)}, u32[]{:S(2)}) collective-permute-start(f32[2,16,256]{2,1,0:T(8,128)S(1)} %get-tuple-element.35), channel_id=1, source_target_pairs={{0,7},{1,2},{2,1},{3,4},{4,3},{5,6},{6,5},{7,0},{8,15},{9,10},{10,... | collective-permute-start | bytes 98312 | tf_op jit(solution)/shard_map/ppermute | solution.py:41
  33.8 15.6 %collective-permute-start.11 = (f32[4,64,256]{2,1,0:T(8,128)S(1)}, f32[4,64,256]{2,1,0:T(8,128)S(1)}, u32[]{:S(2)}, u32[]{:S(2)}) collective-permute-start(f32[4,64,256]{2,1,0:T(8,128)S(1)} %get-tuple-element.40), channel_id=1, source_target_pairs={{0,1},{1,0},{2,3},{3,2},{4,5},{5,4},{6,7},{7,6},{8,9},{9,8},{10,11... | collective-permute-start | bytes 786440 | tf_op jit(solution)/shard_map/ppermute | solution.py:41
  33.8 15.5 %collective-permute-start.12 = (f32[4,64,256]{2,1,0:T(8,128)S(1)}, f32[4,64,256]{2,1,0:T(8,128)S(1)}, u32[]{:S(2)}, u32[]{:S(2)}) collective-permute-start(f32[4,64,256]{2,1,0:T(8,128)S(1)} %get-tuple-element.41), channel_id=1, source_target_pairs={{0,7},{1,2},{2,1},{3,4},{4,3},{5,6},{6,5},{7,0},{8,15},{9,10},{10,... | collective-permute-start | bytes 786440 | tf_op jit(solution)/shard_map/ppermute | solution.py:41
  35.4 9.3 %collective-permute-start.9 = (f32[13,16,256]{2,1,0:T(8,128)S(1)}, f32[13,16,256]{2,1,0:T(8,128)S(1)}, u32[]{:S(2)}, u32[]{:S(2)}) collective-permute-start(f32[13,16,256]{2,1,0:T(8,128)S(1)} %get-tuple-element.38), channel_id=1, source_target_pairs={{0,8},{1,9},{2,10},{3,11},{4,12},{5,13},{6,14},{7,15},{8,0},{9,1},... | collective-permute-start | bytes 638984 | tf_op jit(solution)/shard_map/ppermute | solution.py:41
  39.0 5.7 %collective-permute-start.10 = (f32[13,16,256]{2,1,0:T(8,128)S(1)}, f32[13,16,256]{2,1,0:T(8,128)S(1)}, u32[]{:S(2)}, u32[]{:S(2)}) collective-permute-start(f32[13,16,256]{2,1,0:T(8,128)S(1)} %get-tuple-element.39), channel_id=1, source_target_pairs={{0,0},{1,1},{2,2},{3,3},{4,4},{5,5},{6,6},{7,7},{8,16},{9,17},{10,... | collective-permute-start | bytes 638984 | tf_op jit(solution)/shard_map/ppermute | solution.py:41
  44.8 1.3 %collective-permute-start.13 = (f32[2,16,256]{2,1,0:T(8,128)S(1)}, f32[2,16,256]{2,1,0:T(8,128)S(1)}, u32[]{:S(2)}, u32[]{:S(2)}) collective-permute-start(f32[2,16,256]{2,1,0:T(8,128)S(1)} %get-tuple-element.42), channel_id=1, source_target_pairs={{0,1},{1,0},{2,3},{3,2},{4,5},{5,4},{6,7},{7,6},{8,9},{9,8},{10,11... | collective-permute-start | bytes 98312 | tf_op jit(solution)/shard_map/ppermute | solution.py:41
  44.8 4.5 %collective-permute-start.14 = (f32[2,16,256]{2,1,0:T(8,128)S(1)}, f32[2,16,256]{2,1,0:T(8,128)S(1)}, u32[]{:S(2)}, u32[]{:S(2)}) collective-permute-start(f32[2,16,256]{2,1,0:T(8,128)S(1)} %get-tuple-element.43), channel_id=1, source_target_pairs={{0,7},{1,2},{2,1},{3,4},{4,3},{5,6},{6,5},{7,0},{8,15},{9,10},{10,... | collective-permute-start | bytes 98312 | tf_op jit(solution)/shard_map/ppermute | solution.py:41
  51.8 9.8 %collective-permute-start.16 = (f32[4,64,256]{2,1,0:T(8,128)S(1)}, f32[4,64,256]{2,1,0:T(8,128)S(1)}, u32[]{:S(2)}, u32[]{:S(2)}) collective-permute-start(f32[4,64,256]{2,1,0:T(8,128)S(1)} %get-tuple-element.47), channel_id=1, source_target_pairs={{0,7},{1,0},{2,1},{3,2},{4,3},{5,4},{6,5},{7,6},{8,15},{9,8},{10,9... | collective-permute-start | bytes 786440 | tf_op jit(solution)/shard_map/ppermute | solution.py:51
  52.3 9.2 %collective-permute-start.15 = (f32[13,16,256]{2,1,0:T(8,128)S(1)}, f32[13,16,256]{2,1,0:T(8,128)S(1)}, u32[]{:S(2)}, u32[]{:S(2)}) collective-permute-start(f32[13,16,256]{2,1,0:T(8,128)S(1)} %get-tuple-element.46), channel_id=1, source_target_pairs={{0,24},{1,25},{2,26},{3,27},{4,28},{5,29},{6,30},{7,31},{8,0},{9,1... | collective-permute-start | bytes 638984 | tf_op jit(solution)/shard_map/ppermute | solution.py:51
  54.6 6.0 %collective-permute-start.17 = (f32[16,256]{1,0:T(8,128)S(1)}, f32[16,256]{1,0:T(8,128)S(1)}, u32[]{:S(2)}, u32[]{:S(2)}) collective-permute-start(f32[16,256]{1,0:T(8,128)S(1)} %get-tuple-element.48), channel_id=1, source_target_pairs={{0,31},{1,24},{2,25},{3,26},{4,27},{5,28},{6,29},{7,30},{8,7},{9,0... | collective-permute-start | bytes 49160 | tf_op jit(solution)/shard_map/ppermute | solution.py:51
  63.6 1.3 %collective-permute-start.18 = (f32[136,128]{1,0:T(8,128)S(1)}, f32[136,128]{1,0:T(8,128)S(1)}, u32[]{:S(2)}, u32[]{:S(2)}) collective-permute-start(f32[136,128]{1,0:T(8,128)S(1)} %get-tuple-element.50), channel_id=1, source_target_pairs={{0,1},{1,0},{2,3},{3,2},{4,5},{5,4},{6,7},{7,6},{8,9},{9,8},{10,11... | collective-permute-start | bytes 208904 | tf_op jit(solution)/shard_map/ppermute | solution.py:55
  65.0 6.5 %collective-permute-start.21 = (f32[136,128]{1,0:T(8,128)S(1)}, f32[136,128]{1,0:T(8,128)S(1)}, u32[]{:S(2)}, u32[]{:S(2)}) collective-permute-start(f32[136,128]{1,0:T(8,128)S(1)} %add.21), channel_id=1, source_target_pairs={{0,24},{8,16},{16,8},{24,0},{1,25},{9,17},{17,9},{25,1},{2,26},{10... | collective-permute-start | bytes 208904 | tf_op jit(solution)/shard_map/ppermute | solution.py:55
  67.4 7.6 %collective-permute-start.20 = (f32[136,128]{1,0:T(8,128)S(1)}, f32[136,128]{1,0:T(8,128)S(1)}, u32[]{:S(2)}, u32[]{:S(2)}) collective-permute-start(f32[136,128]{1,0:T(8,128)S(1)} %add.21), channel_id=1, source_target_pairs={{0,16},{8,24},{16,0},{24,8},{1,17},{9,25},{17,1},{25,9},{2,18},{10... | collective-permute-start | bytes 208904 | tf_op jit(solution)/shard_map/ppermute | solution.py:55
  68.2 6.7 %collective-permute-start.19 = (f32[136,128]{1,0:T(8,128)S(1)}, f32[136,128]{1,0:T(8,128)S(1)}, u32[]{:S(2)}, u32[]{:S(2)}) collective-permute-start(f32[136,128]{1,0:T(8,128)S(1)} %add.21), channel_id=1, source_target_pairs={{0,8},{8,0},{16,24},{24,16},{1,9},{9,1},{17,25},{25,17},{2,10},{10... | collective-permute-start | bytes 208904 | tf_op jit(solution)/shard_map/ppermute | solution.py:55
  74.9 5.4 %collective-permute-start.24 = (f32[136,128]{1,0:T(8,128)S(1)}, f32[136,128]{1,0:T(8,128)S(1)}, u32[]{:S(2)}, u32[]{:S(2)}) collective-permute-start(f32[136,128]{1,0:T(8,128)S(1)} %add_add_fusion.1), channel_id=1, source_target_pairs={{0,6},{1,7},{2,4},{3,5},{4,2},{5,3},{6,0},{7,1},{8,14},{9,15},{10,... | collective-permute-start | bytes 208904 | tf_op jit(solution)/shard_map/ppermute | solution.py:55
  77.2 4.3 %collective-permute-start.23 = (f32[136,128]{1,0:T(8,128)S(1)}, f32[136,128]{1,0:T(8,128)S(1)}, u32[]{:S(2)}, u32[]{:S(2)}) collective-permute-start(f32[136,128]{1,0:T(8,128)S(1)} %add_add_fusion.1), channel_id=1, source_target_pairs={{0,4},{1,5},{2,6},{3,7},{4,0},{5,1},{6,2},{7,3},{8,12},{9,13},{10,... | collective-permute-start | bytes 208904 | tf_op jit(solution)/shard_map/ppermute | solution.py:55
  77.7 4.3 %collective-permute-start.22 = (f32[136,128]{1,0:T(8,128)S(1)}, f32[136,128]{1,0:T(8,128)S(1)}, u32[]{:S(2)}, u32[]{:S(2)}) collective-permute-start(f32[136,128]{1,0:T(8,128)S(1)} %add_add_fusion.1), channel_id=1, source_target_pairs={{0,2},{1,3},{2,0},{3,1},{4,6},{5,7},{6,4},{7,5},{8,10},{9,11},{10,... | collective-permute-start | bytes 208904 | tf_op jit(solution)/shard_map/ppermute | solution.py:55
  82.0 1.3 %collective-permute-start.25 = (f32[136,128]{1,0:T(8,128)S(1)}, f32[136,128]{1,0:T(8,128)S(1)}, u32[]{:S(2)}, u32[]{:S(2)}) collective-permute-start(f32[136,128]{1,0:T(8,128)S(1)} %add_add_fusion.mine_ref), channel_id=1, source_target_pairs={{0,1},{1,0},{2,3},{3,2},{4,5},{5,4},{6,7},{7,6},{8,9},{9,8},{10,11... | collective-permute-start | bytes 208904 | tf_op jit(solution)/shard_map/ppermute | solution.py:55

commit v4 on v3

--- a/solution.py
+++ b/solution.py
@@ -55,65 +55,83 @@
     return lax.ppermute(value, axis, [(i, i ^ bits) for i in range(lax.axis_size(axis))])
 
 
+def sum_swap(value, stage, bits):
+    size_x, size_y = lax.axis_size("dx"), lax.axis_size("dy")
+    route = []
+    for p in range(size_x):
+        for q in range(size_y):
+            along_x = (q + stage) % 2 == 0
+            to = (p ^ bits, q) if along_x else (p, q ^ 2 * bits)
+            route.append((p * size_y + q, to[0] * size_y + to[1]))
+    return lax.ppermute(value, AXES, route)
+
+
 def halved_total(kept, sent):
     part = kept + xor_swap(sent, "dy", 1)
-    for axis, bit in (("dx", 1), ("dy", 2)):
-        while bit < lax.axis_size(axis):
-            if 2 * bit < lax.axis_size(axis):
-                one, two, three = [xor_swap(part, axis, bit * k) for k in (1, 2, 3)]
+    sizes = lax.axis_size("dx"), lax.axis_size("dy") // 2
+    if sizes[0] == sizes[1]:
+        steps = [functools.partial(sum_swap, stage=stage) for stage in (0, 1)]
+    else:
+        steps = [
+            lambda value, bits: xor_swap(value, "dx", bits),
+            lambda value, bits: xor_swap(value, "dy", 2 * bits),
+        ]
+    for step, size in zip(steps, sizes):
+        bit = 1
+        while bit < size:
+            if 2 * bit < size:
+                one, two, three = [step(part, bits=bit * k) for k in (1, 2, 3)]
                 part = (part + one) + (two + three)
                 bit *= 4
             else:
-                part = part + xor_swap(part, axis, bit)
+                part = part + step(part, bits=bit)
                 bit *= 2
     return part, xor_swap(part, "dy", 1)
 
 
-def renumber_kernel(conn_ref, mats_ref, out_ref, *, side, width, depth, layers):
-    e1, e2, e3 = (pl.program_id(k) for k in range(3))
-    deg = side - 1
-    rows = conn_ref[0, 0]
-    node = rows[0:1]
-    for k in range(1, layers):
-        node = jnp.where(e3 == k, rows[k : k + 1], node)
-    node = node.astype(jnp.float32)
-    plane = jnp.floor((node + 0.5) * (1.0 / depth))
-    first = jnp.floor((plane + 0.5) * (1.0 / width))
-    c = (node - plane * depth).astype(jnp.int32) - deg * e3
-    b = (plane - first * width).astype(jnp.int32) - deg * e2
-    a = first.astype(jnp.int32) - deg * e1
-    place = (a * side + c) * side + b
-    a = jnp.where((e1 == 0) & (lax.axis_index("dx") == 0), a, 1)
-    b = jnp.where((e2 == 0) & (lax.axis_index("dy") == 0), b, 1)
-    c_low = jnp.where(e3 == 0, c, 1)
-    c_high = jnp.where(e3 == layers - 1, c, 1)
-    held = (a == 0) | (b == 0) | (c_low == 0) | (c_high == deg)
-    place = jnp.where(held, -1, place)
-    count = mats_ref.shape[-1]
-    order = lax.broadcasted_iota(jnp.int32, (count, count), 0) == place
-    order = jnp.where(order, 1.0, 0.0).astype(jnp.bfloat16)
-    half = jnp.dot(order, mats_ref[0, 0, 0], preferred_element_type=jnp.float32)
-    whole = lax.dot_general(
-        half.astype(jnp.bfloat16),
-        order,
-        (((1,), (1,)), ((), ())),
-        preferred_element_type=jnp.float32,
-    )
-    out_ref[0, 0, 0] = whole.astype(jnp.bfloat16)
-
-
-def renumber(conn, elem_mats, side, width, depth):
-    ex, ey, layers, count, _ = elem_mats.shape
-    spot = pl.BlockSpec((1, 1, 1, count, count), lambda i, j, k: (i, j, k, 0, 0))
+def renumber_kernel(conn_ref, mats_ref, out_ref, *, g, width, depth):
+    side, deg, layers = g.side, g.deg, g.ez
+    spots = [
+        (e1, e2, e3) for e1 in range(g.ex) for e2 in range(g.ey) for e3 in range(g.ez)
+    ]
+    for e, (e1, e2, e3) in enumerate(spots):
+        node = conn_ref[e1, e2, e3 : e3 + 1].astype(jnp.float32)
+        plane = jnp.floor((node + 0.5) * (1.0 / depth))
+        first = jnp.floor((plane + 0.5) * (1.0 / width))
+        c = (node - plane * depth).astype(jnp.int32) - deg * e3
+        b = (plane - first * width).astype(jnp.int32) - deg * e2
+        a = first.astype(jnp.int32) - deg * e1
+        place = (a * side + c) * side + b
+        if e1 == 0:
+            place = jnp.where((a == 0) & (lax.axis_index("dx") == 0), -1, place)
+        if e2 == 0:
+            place = jnp.where((b == 0) & (lax.axis_index("dy") == 0), -1, place)
+        if e3 == 0:
+            place = jnp.where(c == 0, -1, place)
+        if e3 == layers - 1:
+            place = jnp.where(c == deg, -1, place)
+        order = lax.broadcasted_iota(jnp.int32, (g.count, g.count), 0) == place
+        order = jnp.where(order, 1.0, 0.0).astype(jnp.bfloat16)
+        half = jnp.dot(order, mats_ref[e], preferred_element_type=jnp.float32)
+        whole = lax.dot_general(
+            half.astype(jnp.bfloat16),
+            order,
+            (((1,), (1,)), ((), ())),
+            preferred_element_type=jnp.float32,
+        )
+        out_ref[e] = whole.astype(jnp.bfloat16)
+
+
+def renumber(g, conn, elem_mats, width, depth):
+    shape = (g.elements, g.count, g.count)
     return pl.pallas_call(
-        functools.partial(renumber_kernel, side=side, width=width, depth=depth, layers=layers),
-        out_shape=jax.ShapeDtypeStruct(elem_mats.shape, jnp.bfloat16),
-        grid=(ex, ey, layers),
-        in_specs=[pl.BlockSpec((1, 1, layers, count), lambda i, j, k: (i, j, 0, 0)), spot],
-        out_specs=spot,
+        functools.partial(renumber_kernel, g=g, width=width, depth=depth),
+        out_shape=jax.ShapeDtypeStruct(shape, jnp.bfloat16),
+        in_specs=[VMEM] * 2,
+        out_specs=VMEM,
         compiler_params=pltpu.CompilerParams(vmem_limit_bytes=LIMIT),
         cost_estimate=pl.CostEstimate(
-            flops=4 * ex * ey * layers * count**3,
+            flops=4 * g.elements * g.count**3,
             bytes_accessed=4 * elem_mats.size,
             transcendentals=0,
         ),
@@ -321,6 +339,24 @@
     return jnp.concatenate(parts, axis=-1)
 
 
+def edge_kernel(orb_ref, mats_ref, conn_ref, x_ref, y_ref, line_ref, tiles_ref):
+    del mats_ref, conn_ref
+    nx, nz, ny, bands = orb_ref.shape
+    last = (ny - 1) % ROWS
+    tail = slice(ny - 1 - last, ny)
+    x_ref[...] = orb_ref[nx - 1]
+    for h in range(bands // LANES):
+        for i in range(nx):
+            part = orb_ref[i, :, tail, lanes(h)].astype(jnp.float32)
+            for k in range(nz):
+                start = (i * nz + k) * ROWS
+                tiles_ref[h, start : start + last + 1] = part[k]
+        rows = tiles_ref[h, pl.ds(last, y_ref.shape[0], stride=ROWS)]
+        y_ref[:, lanes(h)] = rows.astype(jnp.bfloat16)
+        line = tiles_ref[h, pl.ds((nx - 1) * nz * ROWS + last, line_ref.shape[0], stride=ROWS)]
+        line_ref[:, lanes(h)] = line.astype(jnp.bfloat16)
+
+
 def first_kernel(*refs, g):
     orb_ref, below_x, below_y, below_xy, mats_ref, y_ref, next_ref, *sends = refs
     side = g.side
@@ -354,7 +390,7 @@
     for k in range(g.nz):
         place(0, k, below_x[k], below_xy[k : k + 1])
         for i in range(orb_ref.shape[0]):
-            place(i + 1, k, orb_ref[i, k], below_y[i, k : k + 1])
+            place(i + 1, k, orb_ref[i, k], below_y[i * g.nz + k : i * g.nz + k + 1])
     multiply(g, mats_ref, functools.partial(field_of, y_ref), next_ref)
     send_all(g, next_ref, sends)
     advance(next_ref, y_ref, None, FIRST)
@@ -504,42 +540,63 @@
         tile = left[k]
         cols = [spread(tile[:, ROWS * k + c : ROWS * k + c + 1]) for c in range(ROWS)]
         s = [[spread(cols[c][r : r + 1]) if c <= r else None for c in range(ROWS)] for r in range(ROWS)]
-        inv, mult = [], [[None] * ROWS for _ in range(ROWS)]
-        root = []
-        for j in range(ROWS):
-            inv.append(1.0 / s[j][j])
-            root.append(lax.rsqrt(s[j][j]))
-            for r in range(j + 1, ROWS):
-                mult[r][j] = s[r][j] * inv[j]
-            for r in range(j + 1, ROWS):
-                for c in range(j + 1, r + 1):
-                    s[r][c] = s[r][c] - mult[r][j] * s[c][j]
+        take = [[None] * ROWS for _ in range(ROWS)]
+        pairs = {}
+        for j in range(0, ROWS, 2):
+            p, q, t = s[j][j], s[j + 1][j], s[j + 1][j + 1]
+            over = 1.0 / (p * t - q * q)
+            across = q * (1.0 / p)
+            pairs[j] = (
+                (t * over, q * over, p * over),
+                across,
+                lax.rsqrt(p),
+                lax.rsqrt(t - across * q),
+            )
+            one, both, two = pairs[j][0]
+            for r in range(j + 2, ROWS):
+                take[r][j] = s[r][j] * one - s[r][j + 1] * both
+                take[r][j + 1] = s[r][j + 1] * two - s[r][j] * both
+                for c in range(j + 2, r + 1):
+                    s[r][c] = s[r][c] - (take[r][j] * s[c][j] + take[r][j + 1] * s[c][j + 1])
         last = k == groups - 1
         solved = []
         for source, wanted in ((right[k], True), (tile, False)):
             if last and not wanted:
                 continue
             rows = [spread(source[r : r + 1]) for r in range(ROWS)]
-            for j in range(ROWS):
-                for r in range(j + 1, ROWS):
-                    rows[r] = rows[r] - mult[r][j] * rows[j]
+            for j in range(0, ROWS, 2):
+                for r in range(j + 2, ROWS):
+                    rows[r] = rows[r] - (take[r][j] * rows[j] + take[r][j + 1] * rows[j + 1])
             if wanted:
-                done = rows[0] * root[0]
-                for r in range(1, ROWS):
-                    done = jnp.where(sub == r, rows[r] * root[r], done)
+                done = jnp.zeros((ROWS, size), jnp.float32)
+                for j in range(0, ROWS, 2):
+                    _, across, scale, scale_next = pairs[j]
+                    done = jnp.where(sub == j, rows[j] * scale, done)
+                    below = (rows[j + 1] - across * rows[j]) * scale_next
+                    done = jnp.where(sub == j + 1, below, done)
                 result.append(done)
             if last:
                 continue
-            rows = [row * d for row, d in zip(rows, inv)]
-            for j in reversed(range(ROWS)):
+            for j in range(0, ROWS, 2):
+                one, both, two = pairs[j][0]
+                rows[j], rows[j + 1] = (
+                    one * rows[j] - both * rows[j + 1],
+                    two * rows[j + 1] - both * rows[j],
+                )
+            for j in reversed(range(0, ROWS, 2)):
                 for r in range(j):
-                    rows[r] = rows[r] - mult[j][r] * rows[j]
+                    rows[r] = rows[r] - (take[j][r] * rows[j] + take[j + 1][r] * rows[j + 1])
             solved.append(rows)
+
+        def tree(terms):
+            while len(terms) > 1:
+                terms = [a + b for a, b in zip(terms[::2], terms[1::2])]
+            return terms[0]
+
         for j in range(k + 1, groups):
             cols = [spread(left[j][:, ROWS * k + c : ROWS * k + c + 1]) for c in range(ROWS)]
-            for c in range(ROWS):
-                right[j] = right[j] - cols[c] * solved[0][c]
-                left[j] = left[j] - cols[c] * solved[1][c]
+            left[j] = left[j] - tree([cols[c] * solved[1][c] for c in range(ROWS)])
+            right[j] = right[j] - tree([cols[c] * solved[0][c] for c in range(ROWS)])
     return jnp.concatenate(result, axis=0)
 
 
@@ -622,16 +679,29 @@
     nx, ny, nz, bands = orbitals.shape
     side = round(elem_mats.shape[-1] ** (1 / 3))
     g = Grid(elem_mats, side)
+    elem_mats = elem_mats.reshape(g.elements, g.count, g.count)
     f32 = jnp.float32
     orb = jnp.transpose(orbitals, (0, 2, 1, 3))
-    below_x = ring(orb[-1], 1, 0)
-    below_y = ring(orb[:, :, -1], 0, 1)
-    below_xy = ring(orb[-1, :, -1], 1, 1)
-    mats = renumber(conn, elem_mats, side, ny + 1, nz + 2)
-    mats = mats.reshape(g.elements, g.count, g.count)
+    shape = jax.ShapeDtypeStruct
+    plane = -(-nx * nz // (2 * ROWS)) * 2 * ROWS
+    tall = (plane + 2 * ROWS) * ROWS
+    edges = call(
+        edge_kernel,
+        [
+            shape((nz, ny, bands), orb.dtype),
+            shape((plane, bands), orb.dtype),
+            shape((2 * ROWS, bands), orb.dtype),
+        ],
+        [pltpu.VMEM((bands // LANES, tall, LANES), f32)],
+        (orb, elem_mats, conn),
+        0,
+    )
+    below_x, below_y, below_xy = [
+        ring(s, *step) for s, step in zip(edges, ((1, 0), (0, 1), (1, 1)))
+    ]
+    mats = renumber(g, conn, elem_mats, ny + 1, nz + 2)
 
     nodes = (g.elements, bands // LANES, g.count, LANES)
-    shape = jax.ShapeDtypeStruct
     x_shape = shape((nz, g.ey * side, bands), f32)
     y_shape = shape((g.ex * g.ez, side * side, bands), f32)
     line_shape = shape((g.ez * side, bands), f32)

time: 98.9 us -> 95.6 us (0.967)
  Pallas kernels: 30.2 us -> 28.4 us
  starting transfers between devices: 32.1 us -> 31 us
    ppermute x8 -> x2, waiting for transfers between devices: 11.5 us -> 2.49 us  [xor_swap(): lax.ppermute(value, axis, [(i, i ^ bits) for i in range(lax.axis_size(axi...]
    ppermute x0 -> x6, starting transfers between devices: none -> 8.01 us  [sum_swap(): return lax.ppermute(value, AXES, route)]
    ppermute x8 -> x2, starting transfers between devices: 8.15 us -> 0.14 us  [xor_swap(): lax.ppermute(value, axis, [(i, i ^ bits) for i in range(lax.axis_size(axi...]
    ppermute x0 -> x6, waiting for transfers between devices: none -> 6.98 us  [sum_swap(): return lax.ppermute(value, AXES, route)]
    pallas_call x1, Pallas kernels: 5.73 us -> 4.52 us  [renumber(): pl.pallas_call(functools.partial(renumber_kernel, g=g, width=width, depth...]
    ppermute x6, waiting for transfers between devices: 3.66 us -> 4.65 us  [ring(): return lax.ppermute(value, AXES, route)]
    pallas_call x6 -> x7, Pallas kernels: 9.1 us -> 9.29 us  [call(): pl.pallas_call(kernel, out_shape=outs, in_specs=[VMEM] * len(operands), o...]
    unnamed x7 -> x10, local copies, waits for them, and re-layouts: 4.16 us -> 4.29 us
  transfers between devices with their start and end apart: 26 -> 26, of which waited for: 14 -> 16; matrix products, arithmetic and copies ran while one was open for 0% -> 0% of each run, Pallas kernels for 6% -> 5%
where the time goes in v4:
time: 95.6 us; the launch traced here: 95.3 us
  waiting for transfers between devices  31.5 us (33%)
  starting transfers between devices  31 us (32%)
  Pallas kernels  28.4 us (30%)
  local copies, waits for them, and re-layouts  4.29 us (4%)
    ppermute x12, waiting for transfers between devices, pair_swap(): return lax.ppermute(value, AXES, route)  17.3 us
    pallas_call x1, Pallas kernels, shards(): pl.pallas_call(functools.partial(basis_kernel, scale=math.sqrt(nx * ny *...  14.6 us
    ppermute x12, starting transfers between devices, pair_swap(): return lax.ppermute(value, AXES, route)  11.4 us
    ppermute x6, starting transfers between devices, ring(): return lax.ppermute(value, AXES, route)  11.4 us
    pallas_call x7, Pallas kernels, call(): pl.pallas_call(kernel, out_shape=outs, in_specs=[VMEM] * len(operands), o...  9.29 us
    ppermute x6, starting transfers between devices, sum_swap(): return lax.ppermute(value, AXES, route)  8.01 us
    ppermute x6, waiting for transfers between devices, sum_swap(): return lax.ppermute(value, AXES, route)  6.98 us
    ppermute x6, waiting for transfers between devices, ring(): return lax.ppermute(value, AXES, route)  4.65 us
  transfers between devices with their start and end apart: 26, of which 16 were waited for; matrix products, arithmetic and copies ran while one was open for 0% of the time, Pallas kernels for 5%

profile of v4, /device:TPU:0, one launch (start us, length us, event | category | flops | bytes accessed | tf_op | source)
XLA Modules:
  0.0 95.3 jit_solution(18199160300858213126)
XLA Ops:
  0.0 1.4 %copy-done = bf16[14,14,13,256]{3,1,2,0:T(8,128)(2,1)S(1)} copy-done((bf16[14,14,13,256]{3,1,2,0:T(8,128)(2,1)S(1)}, bf16[14,14,13,256]{3,1,2,0:T(8,128)(2,1)}, u32[]{:S(2)}) %copy-start) | copy-done | bytes 1304600
  1.4 2.2 %copy-done.2 = bf16[2,2,2,512,512]{4,3,2,1,0:T(8,128)(2,1)S(1)} copy-done((bf16[2,2,2,512,512]{4,3,2,1,0:T(8,128)(2,1)S(1)}, bf16[2,2,2,512,512]{4,3,2,1,0:T(8,128)(2,1)}, u32[]{:S(2)}) %copy-start.2) | copy-done | bytes 4194328
  3.6 0.7 copy-done.4
  4.3 0.2 shard_map.37
  4.5 2.5 %collective-permute-start.2 = (bf16[16,256]{1,0:T(8,128)(2,1)S(1)}, bf16[16,256]{1,0:T(8,128)(2,1)S(1)}, u32[]{:S(2)}, u32[]{:S(2)}) collective-permute-start(bf16[16,256]{1,0:T(8,128)(2,1)S(1)} %get-tuple-element.34), channel_id=1, source_target_pairs={{0,9},{1,10},{2,11},{3,12},{4,13},{5,14},{6,15},{7,8},{8,17},{9,18... | collective-permute-start | bytes 24584 | tf_op jit(solution)/shard_map/ppermute | solution.py:51
  7.0 1.6 %collective-permute-start.1 = (bf16[192,256]{1,0:T(8,128)(2,1)S(1)}, bf16[192,256]{1,0:T(8,128)(2,1)S(1)}, u32[]{:S(2)}, u32[]{:S(2)}) collective-permute-start(bf16[192,256]{1,0:T(8,128)(2,1)S(1)} %get-tuple-element.33), channel_id=1, source_target_pairs={{0,1},{1,2},{2,3},{3,4},{4,5},{5,6},{6,7},{7,0},{8,9},{9,10},{10,1... | collective-permute-start | bytes 294920 | tf_op jit(solution)/shard_map/ppermute | solution.py:51
  8.6 1.6 %collective-permute-start = (bf16[13,14,256]{2,1,0:T(8,128)(2,1)S(1)}, bf16[13,14,256]{2,1,0:T(8,128)(2,1)S(1)}, u32[]{:S(2)}, u32[]{:S(2)}) collective-permute-start(bf16[13,14,256]{2,1,0:T(8,128)(2,1)S(1)} %get-tuple-element.32), channel_id=1, source_target_pairs={{0,8},{1,9},{2,10},{3,11},{4,12},{5,13},{6,14},{7,15},{8,16},{9,17... | collective-permute-start | bytes 279560 | tf_op jit(solution)/shard_map/ppermute | solution.py:51
  10.2 4.5 %renumber.1.refs_4_.refs_8_ = bf16[8,512,512]{2,1,0:T(8,128)(2,1)S(1)} custom-call(s32[2,2,2,512]{3,2,1,0:T(2,128)S(1)} %copy-done.4, bf16[8,512,512]{2,1,0:T(8,128)(2,1)S(1)} %bitcast.6), custom_call_target="tpu_custom_call" | custom-call | flops 4294967296 | bytes 8388608 | tf_op jit(solution)/shard_map/renumber/pallas_call | solution.py:127
  14.7 0.6 collective-permute-done.refs_1_
  15.3 2.1 %shard_map.38 = (f32[8,2,512,128]{3,2,1,0:T(8,128)S(1)}, f32[8,2,512,128]{3,2,1,0:T(8,128)S(1)}, f32[13,16,256]{2,1,0:T(8,128)S(1)}, f32[13,16,256]{2,1,0:T(8,12...) custom-call(bf16[14,13,14,256]{3,2,1,0:T(8,128)(2,1)S(1)} %bitcast.4, ...), custom_call_target="tpu_custom_call" | custom-call | flops 1073741824 | bytes 15037440 | tf_op jit(solution)/shard_map/pallas_call | solution.py:667
  17.4 0.1 collective-permute-start.5
  17.5 1.5 %collective-permute-start.6 = (f32[4,64,256]{2,1,0:T(8,128)S(1)}, f32[4,64,256]{2,1,0:T(8,128)S(1)}, u32[]{:S(2)}, u32[]{:S(2)}) collective-permute-start(f32[4,64,256]{2,1,0:T(8,128)S(1)} %get-tuple-element.39), channel_id=1, source_target_pairs={{0,7},{1,2},{2,1},{3,4},{4,3},{5,6},{6,5},{7,0},{8,15},{9,10},{10,... | collective-permute-start | bytes 786440 | tf_op jit(solution)/shard_map/ppermute | solution.py:41
  19.0 1.0 %collective-permute-start.3 = (f32[13,16,256]{2,1,0:T(8,128)S(1)}, f32[13,16,256]{2,1,0:T(8,128)S(1)}, u32[]{:S(2)}, u32[]{:S(2)}) collective-permute-start(f32[13,16,256]{2,1,0:T(8,128)S(1)} %get-tuple-element.36), channel_id=1, source_target_pairs={{0,8},{1,9},{2,10},{3,11},{4,12},{5,13},{6,14},{7,15},{8,0},{9,1},... | collective-permute-start | bytes 638984 | tf_op jit(solution)/shard_map/ppermute | solution.py:41
  20.1 0.7 collective-permute-start.4
  20.7 5.6 %collective-permute-done.3.from_a.refs_1_ = f32[13,16,256]{2,1,0:T(8,128)S(1)} collective-permute-done((f32[13,16,256]{2,1,0:T(8,128)S(1)}, f32[13,16,256]{2,1,0:T(8,128)S(1)}, u32[]{:S(2)}, u32[]{:S(2)}) %collective-permute-start.3) | collective-permute-done | bytes 213024 | tf_op jit(solution)/shard_map/ppermute | solution.py:41
  26.3 0.1 collective-permute-start.7
  26.4 1.5 %collective-permute-start.8 = (f32[2,16,256]{2,1,0:T(8,128)S(1)}, f32[2,16,256]{2,1,0:T(8,128)S(1)}, u32[]{:S(2)}, u32[]{:S(2)}) collective-permute-start(f32[2,16,256]{2,1,0:T(8,128)S(1)} %get-tuple-element.41), channel_id=1, source_target_pairs={{0,7},{1,2},{2,1},{3,4},{4,3},{5,6},{6,5},{7,0},{8,15},{9,10},{10,... | collective-permute-start | bytes 98312 | tf_op jit(solution)/shard_map/ppermute | solution.py:41
  28.0 2.8 %collective-permute-done.8.refs_6_ = f32[2,16,256]{2,1,0:T(8,128)S(1)} collective-permute-done((f32[2,16,256]{2,1,0:T(8,128)S(1)}, f32[2,16,256]{2,1,0:T(8,128)S(1)}, u32[]{:S(2)}, u32[]{:S(2)}) %collective-permute-start.8) | collective-permute-done | bytes 32800 | tf_op jit(solution)/shard_map/ppermute | solution.py:41
  30.7 2.4 %shard_map.40 = (f32[8,2,512,128]{3,2,1,0:T(8,128)S(1)}, f32[8,2,512,128]{3,2,1,0:T(8,128)S(1)}, f32[13,16,256]{2,1,0:T(8,128)S(1)}, f32[13,16,256]{2,1,0:T(8,12...) custom-call(f32[8,2,512,128]{3,2,1,0:T(8,128)S(1)} %get-tuple-element.35.refs_0_, ...), custom_call_target="tpu_custom_call" | custom-call | flops 1073741824 | bytes 22937600 | tf_op jit(solution)/shard_map/pallas_call | solution.py:667
  33.3 1.5 %collective-permute-start.12 = (f32[4,64,256]{2,1,0:T(8,128)S(1)}, f32[4,64,256]{2,1,0:T(8,128)S(1)}, u32[]{:S(2)}, u32[]{:S(2)}) collective-permute-start(f32[4,64,256]{2,1,0:T(8,128)S(1)} %get-tuple-element.47), channel_id=1, source_target_pairs={{0,7},{1,2},{2,1},{3,4},{4,3},{5,6},{6,5},{7,0},{8,15},{9,10},{10,... | collective-permute-start | bytes 786440 | tf_op jit(solution)/shard_map/ppermute | solution.py:41
  34.8 3.6 %collective-permute-start.9 = (f32[13,16,256]{2,1,0:T(8,128)S(1)}, f32[13,16,256]{2,1,0:T(8,128)S(1)}, u32[]{:S(2)}, u32[]{:S(2)}) collective-permute-start(f32[13,16,256]{2,1,0:T(8,128)S(1)} %get-tuple-element.44), channel_id=1, source_target_pairs={{0,8},{1,9},{2,10},{3,11},{4,12},{5,13},{6,14},{7,15},{8,0},{9,1},... | collective-permute-start | bytes 638984 | tf_op jit(solution)/shard_map/ppermute | solution.py:41
  38.4 0.7 collective-permute-start.10
  39.1 5.2 %collective-permute-done.9.from_a.refs_1_ = f32[13,16,256]{2,1,0:T(8,128)S(1)} collective-permute-done((f32[13,16,256]{2,1,0:T(8,128)S(1)}, f32[13,16,256]{2,1,0:T(8,128)S(1)}, u32[]{:S(2)}, u32[]{:S(2)}) %collective-permute-start.9) | collective-permute-done | bytes 213024 | tf_op jit(solution)/shard_map/ppermute | solution.py:41
  44.4 0.6 collective-permute-start.14
  45.0 0.6 collective-permute-done.13.refs_5_
  45.6 3.1 %collective-permute-done.14.refs_6_ = f32[2,16,256]{2,1,0:T(8,128)S(1)} collective-permute-done((f32[2,16,256]{2,1,0:T(8,128)S(1)}, f32[2,16,256]{2,1,0:T(8,128)S(1)}, u32[]{:S(2)}, u32[]{:S(2)}) %collective-permute-start.14) | collective-permute-done | bytes 32800 | tf_op jit(solution)/shard_map/ppermute | solution.py:41
  48.8 2.4 %shard_map.42 = (f32[8,2,512,128]{3,2,1,0:T(8,128)S(1)}, f32[13,16,256]{2,1,0:T(8,128)S(1)}, f32[4,64,256]{2,1,0:T(8,128)S(1)}, f32[16,256]{1,0:T(8,128)S(1)}) custom-call(f32[8,2,512,128]{3,2,1,0:T(8,128)S(1)} %get-tuple-element.43.refs_0_, f32[13,16,256]{2,1,0:T(8,128)S(1)} %collective-permute-done.9.from_a.refs_1_, ...), custom_call_target="tpu_custom_call" | custom-call | flops 1073741824 | bytes 18284544 | tf_op jit(solution)/shard_map/pallas_call | solution.py:667
  51.2 0.6 collective-permute-start.16
  51.8 1.8 %collective-permute-start.15 = (f32[13,16,256]{2,1,0:T(8,128)S(1)}, f32[13,16,256]{2,1,0:T(8,128)S(1)}, u32[]{:S(2)}, u32[]{:S(2)}) collective-permute-start(f32[13,16,256]{2,1,0:T(8,128)S(1)} %get-tuple-element.52), channel_id=1, source_target_pairs={{0,24},{1,25},{2,26},{3,27},{4,28},{5,29},{6,30},{7,31},{8,0},{9,1... | collective-permute-start | bytes 638984 | tf_op jit(solution)/shard_map/ppermute | solution.py:51
  53.6 3.3 %collective-permute-start.17 = (f32[16,256]{1,0:T(8,128)S(1)}, f32[16,256]{1,0:T(8,128)S(1)}, u32[]{:S(2)}, u32[]{:S(2)}) collective-permute-start(f32[16,256]{1,0:T(8,128)S(1)} %get-tuple-element.54), channel_id=1, source_target_pairs={{0,31},{1,24},{2,25},{3,26},{4,27},{5,28},{6,29},{7,30},{8,7},{9,0... | collective-permute-start | bytes 49160 | tf_op jit(solution)/shard_map/ppermute | solution.py:51
  56.9 3.1 %collective-permute-done.17.from_xy = f32[16,256]{1,0:T(8,128)S(1)} collective-permute-done((f32[16,256]{1,0:T(8,128)S(1)}, f32[16,256]{1,0:T(8,128)S(1)}, u32[]{:S(2)}, u32[]{:S(2)}) %collective-permute-start.17) | collective-permute-done | bytes 16416 | tf_op jit(solution)/shard_map/ppermute | solution.py:51
  60.0 1.0 %collective-permute-done.15.from_x = f32[13,16,256]{2,1,0:T(8,128)S(1)} collective-permute-done((f32[13,16,256]{2,1,0:T(8,128)S(1)}, f32[13,16,256]{2,1,0:T(8,128)S(1)}, u32[]{:S(2)}, u32[]{:S(2)}) %collective-permute-start.15) | collective-permute-done | bytes 213024 | tf_op jit(solution)/shard_map/ppermute | solution.py:51
  61.0 2.0 %shard_map.43 = (bf16[2912,256]{1,0:T(8,128)(2,1)S(1)}, bf16[2912,256]{1,0:T(8,128)(2,1)S(1)}, f32[136,128]{1,0:T(8,128)S(1)}, f32[136,128]{1,0:T(8,128)S(1)}) custom-call(f32[8,2,512,128]{3,2,1,0:T(8,128)S(1)} %get-tuple-element.51.part_ref, f32[13,16,256]{2,1,0:T(8,128)S(1)} %collective-permute-done.15.from_x, ...), custom_call_target="tpu_custom_call" | custom-call | flops 1526726656 | bytes 7806976 | tf_op jit(solution)/shard_map/pallas_call | solution.py:667
  63.1 1.2 %collective-permute-done.18 = f32[136,128]{1,0:T(8,128)S(1)} collective-permute-done((f32[136,128]{1,0:T(8,128)S(1)}, f32[136,128]{1,0:T(8,128)S(1)}, u32[]{:S(2)}, u32[]{:S(2)}) %collective-permute-start.18) | collective-permute-done | bytes 69664 | tf_op jit(solution)/shard_map/ppermute | solution.py:55
  64.4 1.9 %collective-permute-start.21 = (f32[136,128]{1,0:T(8,128)S(1)}, f32[136,128]{1,0:T(8,128)S(1)}, u32[]{:S(2)}, u32[]{:S(2)}) collective-permute-start(f32[136,128]{1,0:T(8,128)S(1)} %add.21), channel_id=1, source_target_pairs={{0,24},{1,7},{2,26},{3,5},{4,28},{5,3},{6,30},{7,1},{8,16},{9,15},... | collective-permute-start | bytes 208904 | tf_op jit(solution)/shard_map/ppermute | solution.py:66
  66.3 1.4 %collective-permute-start.20 = (f32[136,128]{1,0:T(8,128)S(1)}, f32[136,128]{1,0:T(8,128)S(1)}, u32[]{:S(2)}, u32[]{:S(2)}) collective-permute-start(f32[136,128]{1,0:T(8,128)S(1)} %add.21), channel_id=1, source_target_pairs={{0,16},{1,5},{2,18},{3,7},{4,20},{5,1},{6,22},{7,3},{8,24},{9,13},... | collective-permute-start | bytes 208904 | tf_op jit(solution)/shard_map/ppermute | solution.py:66
  67.7 1.2 %collective-permute-start.19 = (f32[136,128]{1,0:T(8,128)S(1)}, f32[136,128]{1,0:T(8,128)S(1)}, u32[]{:S(2)}, u32[]{:S(2)}) collective-permute-start(f32[136,128]{1,0:T(8,128)S(1)} %add.21), channel_id=1, source_target_pairs={{0,8},{1,3},{2,10},{3,1},{4,12},{5,7},{6,14},{7,5},{8,0},{9,11},{1... | collective-permute-start | bytes 208904 | tf_op jit(solution)/shard_map/ppermute | solution.py:66
  68.8 1.8 %collective-permute-done.21 = f32[136,128]{1,0:T(8,128)S(1)} collective-permute-done((f32[136,128]{1,0:T(8,128)S(1)}, f32[136,128]{1,0:T(8,128)S(1)}, u32[]{:S(2)}, u32[]{:S(2)}) %collective-permute-start.21) | collective-permute-done | bytes 69664 | tf_op jit(solution)/shard_map/ppermute | solution.py:66
  70.7 1.7 %collective-permute-done.20 = f32[136,128]{1,0:T(8,128)S(1)} collective-permute-done((f32[136,128]{1,0:T(8,128)S(1)}, f32[136,128]{1,0:T(8,128)S(1)}, u32[]{:S(2)}, u32[]{:S(2)}) %collective-permute-start.20) | collective-permute-done | bytes 69664 | tf_op jit(solution)/shard_map/ppermute | solution.py:66
  72.3 0.2 collective-permute-done.19
  72.5 2.0 %collective-permute-start.24 = (f32[136,128]{1,0:T(8,128)S(1)}, f32[136,128]{1,0:T(8,128)S(1)}, u32[]{:S(2)}, u32[]{:S(2)}) collective-permute-start(f32[136,128]{1,0:T(8,128)S(1)} %add_add_fusion.1), channel_id=1, source_target_pairs={{0,6},{1,25},{2,4},{3,27},{4,2},{5,29},{6,0},{7,31},{8,14},{9,17},... | collective-permute-start | bytes 208904 | tf_op jit(solution)/shard_map/ppermute | solution.py:66
  74.6 0.5 collective-permute-start.23
  75.1 1.0 %collective-permute-start.22 = (f32[136,128]{1,0:T(8,128)S(1)}, f32[136,128]{1,0:T(8,128)S(1)}, u32[]{:S(2)}, u32[]{:S(2)}) collective-permute-start(f32[136,128]{1,0:T(8,128)S(1)} %add_add_fusion.1), channel_id=1, source_target_pairs={{0,2},{1,9},{2,0},{3,11},{4,6},{5,13},{6,4},{7,15},{8,10},{9,1},{1... | collective-permute-start | bytes 208904 | tf_op jit(solution)/shard_map/ppermute | solution.py:66
  76.1 1.7 %collective-permute-done.24 = f32[136,128]{1,0:T(8,128)S(1)} collective-permute-done((f32[136,128]{1,0:T(8,128)S(1)}, f32[136,128]{1,0:T(8,128)S(1)}, u32[]{:S(2)}, u32[]{:S(2)}) %collective-permute-start.24) | collective-permute-done | bytes 69664 | tf_op jit(solution)/shard_map/ppermute | solution.py:66
  77.8 1.1 %collective-permute-done.23 = f32[136,128]{1,0:T(8,128)S(1)} collective-permute-done((f32[136,128]{1,0:T(8,128)S(1)}, f32[136,128]{1,0:T(8,128)S(1)}, u32[]{:S(2)}, u32[]{:S(2)}) %collective-permute-start.23) | collective-permute-done | bytes 69664 | tf_op jit(solution)/shard_map/ppermute | solution.py:66
  78.9 0.5 collective-permute-done.22
  79.5 1.2 %collective-permute-done.25.other_ref = f32[136,128]{1,0:T(8,128)S(1)} collective-permute-done((f32[136,128]{1,0:T(8,128)S(1)}, f32[136,128]{1,0:T(8,128)S(1)}, u32[]{:S(2)}, u32[]{:S(2)}) %collective-permute-start.25) | collective-permute-done | bytes 69664 | tf_op jit(solution)/shard_map/ppermute | solution.py:55
  80.7 14.6 %basis.1 = f32[14,13,14,256]{3,2,1,0:T(8,128)} custom-call(f32[136,128]{1,0:T(8,128)S(1)} %add_add_fusion.mine_ref, f32[136,128]{1,0:T(8,128)S(1)} %collective-permute-done.25.other_ref, bf16[2912,256]{1,0:T(8,128)(2,1)S(1)} %get-tuple-element.57.high_ref, bf16[2912,256]{1,0:T(8,128)(2,1)S(1)} %get-tuple-element.58.low_ref), custom_call_target="tpu_custom_call" | custom-call | tf_op jit(solution)/shard_map/basis/pallas_call | solution.py:756
  (26 shorter events, 0.4 us)
Async XLA Ops:
  0.0 1.4 %copy-start = (bf16[14,14,13,256]{3,1,2,0:T(8,128)(2,1)S(1)}, bf16[14,14,13,256]{3,1,2,0:T(8,128)(2,1)}, u32[]{:S(2)}) copy-start(bf16[14,14,13,256]{3,1,2,0:T(8,128)(2,1)} %param.3) | copy-start | bytes 3913732
  1.4 2.2 %copy-start.2 = (bf16[2,2,2,512,512]{4,3,2,1,0:T(8,128)(2,1)S(1)}, bf16[2,2,2,512,512]{4,3,2,1,0:T(8,128)(2,1)}, u32[]{:S(2)}) copy-start(bf16[2,2,2,512,512]{4,3,2,1,0:T(8,128)(2,1)} %param.4) | copy-start | bytes 12582916
  3.6 0.7 copy-start.4
  4.3 5.9 %copy-start.3 = (bf16[2,2,2,512,512]{4,3,2,1,0:T(8,128)(2,1)S(1)}, bf16[2,2,2,512,512]{4,3,2,1,0:T(8,128)(2,1)}, u32[]{:S(2)}) copy-start(bf16[2,2,2,512,512]{4,3,2,1,0:T(8,128)(2,1)} %param.4) | copy-start | bytes 12582916
  4.5 10.2 %collective-permute-start.2 = (bf16[16,256]{1,0:T(8,128)(2,1)S(1)}, bf16[16,256]{1,0:T(8,128)(2,1)S(1)}, u32[]{:S(2)}, u32[]{:S(2)}) collective-permute-start(bf16[16,256]{1,0:T(8,128)(2,1)S(1)} %get-tuple-element.34), channel_id=1, source_target_pairs={{0,9},{1,10},{2,11},{3,12},{4,13},{5,14},{6,15},{7,8},{8,17},{9,18... | collective-permute-start | bytes 24584 | tf_op jit(solution)/shard_map/ppermute | solution.py:51
  7.0 8.3 %collective-permute-start.1 = (bf16[192,256]{1,0:T(8,128)(2,1)S(1)}, bf16[192,256]{1,0:T(8,128)(2,1)S(1)}, u32[]{:S(2)}, u32[]{:S(2)}) collective-permute-start(bf16[192,256]{1,0:T(8,128)(2,1)S(1)} %get-tuple-element.33), channel_id=1, source_target_pairs={{0,1},{1,2},{2,3},{3,4},{4,5},{5,6},{6,7},{7,0},{8,9},{9,10},{10,1... | collective-permute-start | bytes 294920 | tf_op jit(solution)/shard_map/ppermute | solution.py:51
  8.6 6.7 %copy-start.1 = (bf16[14,14,13,256]{3,1,2,0:T(8,128)(2,1)S(1)}, bf16[14,14,13,256]{3,1,2,0:T(8,128)(2,1)}, u32[]{:S(2)}) copy-start(bf16[14,14,13,256]{3,1,2,0:T(8,128)(2,1)} %param.3) | copy-start | bytes 3913732
  8.6 6.7 %collective-permute-start = (bf16[13,14,256]{2,1,0:T(8,128)(2,1)S(1)}, bf16[13,14,256]{2,1,0:T(8,128)(2,1)S(1)}, u32[]{:S(2)}, u32[]{:S(2)}) collective-permute-start(bf16[13,14,256]{2,1,0:T(8,128)(2,1)S(1)} %get-tuple-element.32), channel_id=1, source_target_pairs={{0,8},{1,9},{2,10},{3,11},{4,12},{5,13},{6,14},{7,15},{8,16},{9,17... | collective-permute-start | bytes 279560 | tf_op jit(solution)/shard_map/ppermute | solution.py:51
  17.4 13.3 %collective-permute-start.5 = (f32[4,64,256]{2,1,0:T(8,128)S(1)}, f32[4,64,256]{2,1,0:T(8,128)S(1)}, u32[]{:S(2)}, u32[]{:S(2)}) collective-permute-start(f32[4,64,256]{2,1,0:T(8,128)S(1)} %get-tuple-element.38), channel_id=1, source_target_pairs={{0,1},{1,0},{2,3},{3,2},{4,5},{5,4},{6,7},{7,6},{8,9},{9,8},{10,11... | collective-permute-start | bytes 786440 | tf_op jit(solution)/shard_map/ppermute | solution.py:41
  17.5 13.3 %collective-permute-start.6 = (f32[4,64,256]{2,1,0:T(8,128)S(1)}, f32[4,64,256]{2,1,0:T(8,128)S(1)}, u32[]{:S(2)}, u32[]{:S(2)}) collective-permute-start(f32[4,64,256]{2,1,0:T(8,128)S(1)} %get-tuple-element.39), channel_id=1, source_target_pairs={{0,7},{1,2},{2,1},{3,4},{4,3},{5,6},{6,5},{7,0},{8,15},{9,10},{10,... | collective-permute-start | bytes 786440 | tf_op jit(solution)/shard_map/ppermute | solution.py:41
  19.0 7.3 %collective-permute-start.3 = (f32[13,16,256]{2,1,0:T(8,128)S(1)}, f32[13,16,256]{2,1,0:T(8,128)S(1)}, u32[]{:S(2)}, u32[]{:S(2)}) collective-permute-start(f32[13,16,256]{2,1,0:T(8,128)S(1)} %get-tuple-element.36), channel_id=1, source_target_pairs={{0,8},{1,9},{2,10},{3,11},{4,12},{5,13},{6,14},{7,15},{8,0},{9,1},... | collective-permute-start | bytes 638984 | tf_op jit(solution)/shard_map/ppermute | solution.py:41
  20.1 6.3 %collective-permute-start.4 = (f32[13,16,256]{2,1,0:T(8,128)S(1)}, f32[13,16,256]{2,1,0:T(8,128)S(1)}, u32[]{:S(2)}, u32[]{:S(2)}) collective-permute-start(f32[13,16,256]{2,1,0:T(8,128)S(1)} %get-tuple-element.37), channel_id=1, source_target_pairs={{0,0},{1,1},{2,2},{3,3},{4,4},{5,5},{6,6},{7,7},{8,16},{9,17},{10,... | collective-permute-start | bytes 638984 | tf_op jit(solution)/shard_map/ppermute | solution.py:41
  26.3 1.6 %collective-permute-start.7 = (f32[2,16,256]{2,1,0:T(8,128)S(1)}, f32[2,16,256]{2,1,0:T(8,128)S(1)}, u32[]{:S(2)}, u32[]{:S(2)}) collective-permute-start(f32[2,16,256]{2,1,0:T(8,128)S(1)} %get-tuple-element.40), channel_id=1, source_target_pairs={{0,1},{1,0},{2,3},{3,2},{4,5},{5,4},{6,7},{7,6},{8,9},{9,8},{10,11... | collective-permute-start | bytes 98312 | tf_op jit(solution)/shard_map/ppermute | solution.py:41
  26.4 4.3 %collective-permute-start.8 = (f32[2,16,256]{2,1,0:T(8,128)S(1)}, f32[2,16,256]{2,1,0:T(8,128)S(1)}, u32[]{:S(2)}, u32[]{:S(2)}) collective-permute-start(f32[2,16,256]{2,1,0:T(8,128)S(1)} %get-tuple-element.41), channel_id=1, source_target_pairs={{0,7},{1,2},{2,1},{3,4},{4,3},{5,6},{6,5},{7,0},{8,15},{9,10},{10,... | collective-permute-start | bytes 98312 | tf_op jit(solution)/shard_map/ppermute | solution.py:41
  33.2 15.6 %collective-permute-start.11 = (f32[4,64,256]{2,1,0:T(8,128)S(1)}, f32[4,64,256]{2,1,0:T(8,128)S(1)}, u32[]{:S(2)}, u32[]{:S(2)}) collective-permute-start(f32[4,64,256]{2,1,0:T(8,128)S(1)} %get-tuple-element.46), channel_id=1, source_target_pairs={{0,1},{1,0},{2,3},{3,2},{4,5},{5,4},{6,7},{7,6},{8,9},{9,8},{10,11... | collective-permute-start | bytes 786440 | tf_op jit(solution)/shard_map/ppermute | solution.py:41
  33.3 15.5 %collective-permute-start.12 = (f32[4,64,256]{2,1,0:T(8,128)S(1)}, f32[4,64,256]{2,1,0:T(8,128)S(1)}, u32[]{:S(2)}, u32[]{:S(2)}) collective-permute-start(f32[4,64,256]{2,1,0:T(8,128)S(1)} %get-tuple-element.47), channel_id=1, source_target_pairs={{0,7},{1,2},{2,1},{3,4},{4,3},{5,6},{6,5},{7,0},{8,15},{9,10},{10,... | collective-permute-start | bytes 786440 | tf_op jit(solution)/shard_map/ppermute | solution.py:41
  34.8 9.5 %collective-permute-start.9 = (f32[13,16,256]{2,1,0:T(8,128)S(1)}, f32[13,16,256]{2,1,0:T(8,128)S(1)}, u32[]{:S(2)}, u32[]{:S(2)}) collective-permute-start(f32[13,16,256]{2,1,0:T(8,128)S(1)} %get-tuple-element.44), channel_id=1, source_target_pairs={{0,8},{1,9},{2,10},{3,11},{4,12},{5,13},{6,14},{7,15},{8,0},{9,1},... | collective-permute-start | bytes 638984 | tf_op jit(solution)/shard_map/ppermute | solution.py:41
  38.4 5.9 %collective-permute-start.10 = (f32[13,16,256]{2,1,0:T(8,128)S(1)}, f32[13,16,256]{2,1,0:T(8,128)S(1)}, u32[]{:S(2)}, u32[]{:S(2)}) collective-permute-start(f32[13,16,256]{2,1,0:T(8,128)S(1)} %get-tuple-element.45), channel_id=1, source_target_pairs={{0,0},{1,1},{2,2},{3,3},{4,4},{5,5},{6,6},{7,7},{8,16},{9,17},{10,... | collective-permute-start | bytes 638984 | tf_op jit(solution)/shard_map/ppermute | solution.py:41
  44.4 1.3 %collective-permute-start.13 = (f32[2,16,256]{2,1,0:T(8,128)S(1)}, f32[2,16,256]{2,1,0:T(8,128)S(1)}, u32[]{:S(2)}, u32[]{:S(2)}) collective-permute-start(f32[2,16,256]{2,1,0:T(8,128)S(1)} %get-tuple-element.48), channel_id=1, source_target_pairs={{0,1},{1,0},{2,3},{3,2},{4,5},{5,4},{6,7},{7,6},{8,9},{9,8},{10,11... | collective-permute-start | bytes 98312 | tf_op jit(solution)/shard_map/ppermute | solution.py:41
  44.4 4.3 %collective-permute-start.14 = (f32[2,16,256]{2,1,0:T(8,128)S(1)}, f32[2,16,256]{2,1,0:T(8,128)S(1)}, u32[]{:S(2)}, u32[]{:S(2)}) collective-permute-start(f32[2,16,256]{2,1,0:T(8,128)S(1)} %get-tuple-element.49), channel_id=1, source_target_pairs={{0,7},{1,2},{2,1},{3,4},{4,3},{5,6},{6,5},{7,0},{8,15},{9,10},{10,... | collective-permute-start | bytes 98312 | tf_op jit(solution)/shard_map/ppermute | solution.py:41
  51.2 9.8 %collective-permute-start.16 = (f32[4,64,256]{2,1,0:T(8,128)S(1)}, f32[4,64,256]{2,1,0:T(8,128)S(1)}, u32[]{:S(2)}, u32[]{:S(2)}) collective-permute-start(f32[4,64,256]{2,1,0:T(8,128)S(1)} %get-tuple-element.53), channel_id=1, source_target_pairs={{0,7},{1,0},{2,1},{3,2},{4,3},{5,4},{6,5},{7,6},{8,15},{9,8},{10,9... | collective-permute-start | bytes 786440 | tf_op jit(solution)/shard_map/ppermute | solution.py:51
  51.8 9.2 %collective-permute-start.15 = (f32[13,16,256]{2,1,0:T(8,128)S(1)}, f32[13,16,256]{2,1,0:T(8,128)S(1)}, u32[]{:S(2)}, u32[]{:S(2)}) collective-permute-start(f32[13,16,256]{2,1,0:T(8,128)S(1)} %get-tuple-element.52), channel_id=1, source_target_pairs={{0,24},{1,25},{2,26},{3,27},{4,28},{5,29},{6,30},{7,31},{8,0},{9,1... | collective-permute-start | bytes 638984 | tf_op jit(solution)/shard_map/ppermute | solution.py:51
  53.6 6.4 %collective-permute-start.17 = (f32[16,256]{1,0:T(8,128)S(1)}, f32[16,256]{1,0:T(8,128)S(1)}, u32[]{:S(2)}, u32[]{:S(2)}) collective-permute-start(f32[16,256]{1,0:T(8,128)S(1)} %get-tuple-element.54), channel_id=1, source_target_pairs={{0,31},{1,24},{2,25},{3,26},{4,27},{5,28},{6,29},{7,30},{8,7},{9,0... | collective-permute-start | bytes 49160 | tf_op jit(solution)/shard_map/ppermute | solution.py:51
  63.0 1.3 %collective-permute-start.18 = (f32[136,128]{1,0:T(8,128)S(1)}, f32[136,128]{1,0:T(8,128)S(1)}, u32[]{:S(2)}, u32[]{:S(2)}) collective-permute-start(f32[136,128]{1,0:T(8,128)S(1)} %get-tuple-element.56), channel_id=1, source_target_pairs={{0,1},{1,0},{2,3},{3,2},{4,5},{5,4},{6,7},{7,6},{8,9},{9,8},{10,11... | collective-permute-start | bytes 208904 | tf_op jit(solution)/shard_map/ppermute | solution.py:55
  64.4 6.3 %collective-permute-start.21 = (f32[136,128]{1,0:T(8,128)S(1)}, f32[136,128]{1,0:T(8,128)S(1)}, u32[]{:S(2)}, u32[]{:S(2)}) collective-permute-start(f32[136,128]{1,0:T(8,128)S(1)} %add.21), channel_id=1, source_target_pairs={{0,24},{1,7},{2,26},{3,5},{4,28},{5,3},{6,30},{7,1},{8,16},{9,15},... | collective-permute-start | bytes 208904 | tf_op jit(solution)/shard_map/ppermute | solution.py:66
  66.3 6.1 %collective-permute-start.20 = (f32[136,128]{1,0:T(8,128)S(1)}, f32[136,128]{1,0:T(8,128)S(1)}, u32[]{:S(2)}, u32[]{:S(2)}) collective-permute-start(f32[136,128]{1,0:T(8,128)S(1)} %add.21), channel_id=1, source_target_pairs={{0,16},{1,5},{2,18},{3,7},{4,20},{5,1},{6,22},{7,3},{8,24},{9,13},... | collective-permute-start | bytes 208904 | tf_op jit(solution)/shard_map/ppermute | solution.py:66
  67.7 4.9 %collective-permute-start.19 = (f32[136,128]{1,0:T(8,128)S(1)}, f32[136,128]{1,0:T(8,128)S(1)}, u32[]{:S(2)}, u32[]{:S(2)}) collective-permute-start(f32[136,128]{1,0:T(8,128)S(1)} %add.21), channel_id=1, source_target_pairs={{0,8},{1,3},{2,10},{3,1},{4,12},{5,7},{6,14},{7,5},{8,0},{9,11},{1... | collective-permute-start | bytes 208904 | tf_op jit(solution)/shard_map/ppermute | solution.py:66
  72.5 5.3 %collective-permute-start.24 = (f32[136,128]{1,0:T(8,128)S(1)}, f32[136,128]{1,0:T(8,128)S(1)}, u32[]{:S(2)}, u32[]{:S(2)}) collective-permute-start(f32[136,128]{1,0:T(8,128)S(1)} %add_add_fusion.1), channel_id=1, source_target_pairs={{0,6},{1,25},{2,4},{3,27},{4,2},{5,29},{6,0},{7,31},{8,14},{9,17},... | collective-permute-start | bytes 208904 | tf_op jit(solution)/shard_map/ppermute | solution.py:66
  74.6 4.3 %collective-permute-start.23 = (f32[136,128]{1,0:T(8,128)S(1)}, f32[136,128]{1,0:T(8,128)S(1)}, u32[]{:S(2)}, u32[]{:S(2)}) collective-permute-start(f32[136,128]{1,0:T(8,128)S(1)} %add_add_fusion.1), channel_id=1, source_target_pairs={{0,4},{1,17},{2,6},{3,19},{4,0},{5,21},{6,2},{7,23},{8,12},{9,25},... | collective-permute-start | bytes 208904 | tf_op jit(solution)/shard_map/ppermute | solution.py:66
  75.1 4.3 %collective-permute-start.22 = (f32[136,128]{1,0:T(8,128)S(1)}, f32[136,128]{1,0:T(8,128)S(1)}, u32[]{:S(2)}, u32[]{:S(2)}) collective-permute-start(f32[136,128]{1,0:T(8,128)S(1)} %add_add_fusion.1), channel_id=1, source_target_pairs={{0,2},{1,9},{2,0},{3,11},{4,6},{5,13},{6,4},{7,15},{8,10},{9,1},{1... | collective-permute-start | bytes 208904 | tf_op jit(solution)/shard_map/ppermute | solution.py:66
  79.4 1.3 %collective-permute-start.25 = (f32[136,128]{1,0:T(8,128)S(1)}, f32[136,128]{1,0:T(8,128)S(1)}, u32[]{:S(2)}, u32[]{:S(2)}) collective-permute-start(f32[136,128]{1,0:T(8,128)S(1)} %add_add_fusion.mine_ref), channel_id=1, source_target_pairs={{0,1},{1,0},{2,3},{3,2},{4,5},{5,4},{6,7},{7,6},{8,9},{9,8},{10,11... | collective-permute-start | bytes 208904 | tf_op jit(solution)/shard_map/ppermute | solution.py:55

commit v5 on v4

--- a/solution.py
+++ b/solution.py
@@ -203,6 +203,10 @@
                 join(one, g.side_rows(deg), two, g.side_rows(0))
 
 
+def rest_of(value):
+    return value - value.astype(jnp.bfloat16).astype(jnp.float32)
+
+
 def put_x_face(g, w_ref, put):
     for h in range(w_ref.shape[1]):
         for e2 in range(g.ey):
@@ -219,6 +223,9 @@
                 )
                 shape = (number, g.side, LANES)
                 put(where, one.reshape(shape), two.reshape(shape))
+                if e3 < g.ez - 1:
+                    one, two = one[-g.side :], two[-g.side :]
+                    put((g.nz + e3, *where[1:]), rest_of(one), rest_of(two))
 
 
 def put_y_face(g, w_ref, put):
@@ -227,6 +234,10 @@
             for e3 in range(g.ez):
                 one = w_ref[g.at(e1, 0, e3), h, g.side_rows(0)]
                 two = w_ref[g.at(e1, g.ey - 1, e3), h, g.side_rows(g.deg)]
+                if e3 > 0:
+                    layer = lax.broadcasted_iota(jnp.int32, one.shape, 0) % g.side
+                    one = jnp.where(layer == 0, rest_of(one), one)
+                    two = jnp.where(layer == 0, rest_of(two), two)
                 put((e1 * g.ez + e3, slice(None), lanes(h)), one, two)
 
 
@@ -246,15 +257,33 @@
                 part = received((slice(start, start + number), columns, lanes(h)))
                 rows = g.rows(a, low, number)
                 part = part.reshape(number * g.side, LANES)
-                out_ref[g.at(e1, e2, e3), h, rows] += factor * part
+                e = g.at(e1, e2, e3)
+                out_ref[e, h, rows] += factor * part
+                if e3 < g.ez - 1:
+                    part = received((g.nz + e3, columns, lanes(h)))
+                    out_ref[e, h, g.rows(a, g.deg, 1)] += factor * part
+                if e3 > 0:
+                    part = received((g.nz + e3 - 1, columns, lanes(h)))
+                    out_ref[e, h, g.rows(a, 0, 1)] += factor * part
 
 
 def add_y_face(g, out_ref, high, received, factor):
     e2, b = (g.ey - 1, g.deg) if high else (0, 0)
     for h in range(out_ref.shape[1]):
         for e1 in range(g.ex):
+            parts = [
+                received((e1 * g.ez + e3, slice(None), lanes(h))) for e3 in range(g.ez)
+            ]
+            count = parts[0].shape[0]
+            layer = lax.broadcasted_iota(jnp.int32, parts[0].shape, 0) % g.side
             for e3 in range(g.ez):
-                part = received((e1 * g.ez + e3, slice(None), lanes(h)))
+                part = parts[e3]
+                if e3 < g.ez - 1:
+                    above = pltpu.roll(parts[e3 + 1], g.deg, 0)
+                    part = part + jnp.where(layer == g.deg, above, 0.0)
+                if e3 > 0:
+                    below = pltpu.roll(parts[e3 - 1], count - g.deg, 0)
+                    part = part + jnp.where(layer == 0, below, 0.0)
                 out_ref[g.at(e1, e2, e3), h, g.side_rows(b)] += factor * part
 
 
@@ -273,8 +302,8 @@
 
     def by_pair(even, one_ref, two_ref):
         def put(where, low, high):
-            one_ref[where] = jnp.where(even, high, low)
-            two_ref[where] = jnp.where(even, low, high)
+            one_ref[where] = jnp.where(even, high, low).astype(one_ref.dtype)
+            two_ref[where] = jnp.where(even, low, high).astype(two_ref.dtype)
 
         return put
 
@@ -293,7 +322,11 @@
                 row = slice(e3 * g.side + c, e3 * g.side + c + 1)
                 if low <= c < low + number:
                     z = start + c - low
-                    bottom, top = source[z, 0:1], source[z, last : last + 1]
+                    both = source[z].astype(jnp.float32)
+                    if (z + 1) % g.deg == 0:
+                        layer = g.nz + (z + 1) // g.deg - 1
+                        both = both + source[layer].astype(jnp.float32)
+                    bottom, top = both[0:1], both[last : last + 1]
                     to_a[k, row] = jnp.where(even, top, bottom)
                     to_b[k, row] = jnp.where(even, bottom, top)
                 else:
@@ -308,6 +341,7 @@
     has_y = (q > 0, q < lax.axis_size("dy") - 1)
 
     def from_pair(even, high, one, two, exists):
+        one, two = one.astype(jnp.float32), two.astype(jnp.float32)
         value = jnp.where(even, one, two) if high else jnp.where(even, two, one)
         return jnp.where(exists, value, 0.0)
 
@@ -424,7 +458,7 @@
 
     def put_low(ref):
         def put(where, low, high):
-            ref[where] = low
+            ref[where] = low.astype(ref.dtype)
 
         return put
 
@@ -487,8 +521,8 @@
     y_ref[...] = part_ref[...]
     p, q = lax.axis_index("dx"), lax.axis_index("dy")
     has_x, has_y = p < lax.axis_size("dx") - 1, q < lax.axis_size("dy") - 1
-    add_x_face(g, y_ref, True, lambda w: jnp.where(has_x, from_x[w], 0.0), LATER)
-    add_y_face(g, y_ref, True, lambda w: jnp.where(has_y, from_y[w], 0.0), LATER)
+    add_x_face(g, y_ref, True, lambda w: jnp.where(has_x, from_x[w].astype(jnp.float32), 0.0), LATER)
+    add_y_face(g, y_ref, True, lambda w: jnp.where(has_y, from_y[w].astype(jnp.float32), 0.0), LATER)
     add_line(g, y_ref, 1, 1, lambda w: jnp.where(has_x & has_y, from_xy[w], 0.0), LATER)
     sub = lax.broadcasted_iota(jnp.int32, (side, LANES), 0)
     rest = 2 * g.deg - side
@@ -702,8 +736,8 @@
     mats = renumber(g, conn, elem_mats, ny + 1, nz + 2)
 
     nodes = (g.elements, bands // LANES, g.count, LANES)
-    x_shape = shape((nz, g.ey * side, bands), f32)
-    y_shape = shape((g.ex * g.ez, side * side, bands), f32)
+    x_shape = shape((nz + g.ez - 1, g.ey * side, bands), jnp.bfloat16)
+    y_shape = shape((g.ex * g.ez, side * side, bands), jnp.bfloat16)
     line_shape = shape((g.ez * side, bands), f32)
     corner_shape = shape((2, *line_shape.shape), f32)
     send_shapes = [x_shape] * 2 + [y_shape] * 2

time: 95.6 us -> 87.8 us (0.918)
  waiting for transfers between devices: 31.5 us -> 21.9 us
  starting transfers between devices: 31 us -> 32.4 us
    ppermute x12, waiting for transfers between devices: 17.3 us -> 9.01 us  [pair_swap(): return lax.ppermute(value, AXES, route)]
    ppermute x6, waiting for transfers between devices: 4.65 us -> 2.39 us  [ring(): return lax.ppermute(value, AXES, route)]
    ppermute x6, waiting for transfers between devices: 6.98 us -> 8.37 us  [sum_swap(): return lax.ppermute(value, AXES, route)]
where the time goes in v5:
time: 87.8 us; the launch traced here: 87.5 us
  starting transfers between devices  32.4 us (37%)
  Pallas kernels  28.7 us (33%)
  waiting for transfers between devices  21.9 us (25%)
  local copies, waits for them, and re-layouts  4.29 us (5%)
    pallas_call x1, Pallas kernels, shards(): pl.pallas_call(functools.partial(basis_kernel, scale=math.sqrt(nx * ny *...  14.6 us
    ppermute x12, starting transfers between devices, pair_swap(): return lax.ppermute(value, AXES, route)  11.9 us
    ppermute x6, starting transfers between devices, ring(): return lax.ppermute(value, AXES, route)  11.8 us
    pallas_call x7, Pallas kernels, call(): pl.pallas_call(kernel, out_shape=outs, in_specs=[VMEM] * len(operands), o...  9.59 us
    ppermute x12, waiting for transfers between devices, pair_swap(): return lax.ppermute(value, AXES, route)  9.01 us
    ppermute x6, waiting for transfers between devices, sum_swap(): return lax.ppermute(value, AXES, route)  8.37 us
    ppermute x6, starting transfers between devices, sum_swap(): return lax.ppermute(value, AXES, route)  8.01 us
    pallas_call x1, Pallas kernels, renumber(): pl.pallas_call(functools.partial(renumber_kernel, g=g, width=width, depth...  4.52 us
  transfers between devices with their start and end apart: 26, of which 16 were waited for; matrix products, arithmetic and copies ran while one was open for 0% of the time, Pallas kernels for 5%

profile of v5, /device:TPU:0, one launch (start us, length us, event | category | flops | bytes accessed | tf_op | source)
XLA Modules:
  0.0 87.5 jit_solution(8328285964267654654)
XLA Ops:
  0.0 1.4 %copy-done = bf16[14,14,13,256]{3,1,2,0:T(8,128)(2,1)S(1)} copy-done((bf16[14,14,13,256]{3,1,2,0:T(8,128)(2,1)S(1)}, bf16[14,14,13,256]{3,1,2,0:T(8,128)(2,1)}, u32[]{:S(2)}) %copy-start) | copy-done | bytes 1304600
  1.4 2.2 %copy-done.2 = bf16[2,2,2,512,512]{4,3,2,1,0:T(8,128)(2,1)S(1)} copy-done((bf16[2,2,2,512,512]{4,3,2,1,0:T(8,128)(2,1)S(1)}, bf16[2,2,2,512,512]{4,3,2,1,0:T(8,128)(2,1)}, u32[]{:S(2)}) %copy-start.2) | copy-done | bytes 4194328
  3.6 0.7 copy-done.4
  4.3 0.2 shard_map.37
  4.5 2.5 %collective-permute-start.2 = (bf16[16,256]{1,0:T(8,128)(2,1)S(1)}, bf16[16,256]{1,0:T(8,128)(2,1)S(1)}, u32[]{:S(2)}, u32[]{:S(2)}) collective-permute-start(bf16[16,256]{1,0:T(8,128)(2,1)S(1)} %get-tuple-element.34), channel_id=1, source_target_pairs={{0,9},{1,10},{2,11},{3,12},{4,13},{5,14},{6,15},{7,8},{8,17},{9,18... | collective-permute-start | bytes 24584 | tf_op jit(solution)/shard_map/ppermute | solution.py:51
  7.0 1.6 %collective-permute-start.1 = (bf16[192,256]{1,0:T(8,128)(2,1)S(1)}, bf16[192,256]{1,0:T(8,128)(2,1)S(1)}, u32[]{:S(2)}, u32[]{:S(2)}) collective-permute-start(bf16[192,256]{1,0:T(8,128)(2,1)S(1)} %get-tuple-element.33), channel_id=1, source_target_pairs={{0,1},{1,2},{2,3},{3,4},{4,5},{5,6},{6,7},{7,0},{8,9},{9,10},{10,1... | collective-permute-start | bytes 294920 | tf_op jit(solution)/shard_map/ppermute | solution.py:51
  8.6 1.6 %collective-permute-start = (bf16[13,14,256]{2,1,0:T(8,128)(2,1)S(1)}, bf16[13,14,256]{2,1,0:T(8,128)(2,1)S(1)}, u32[]{:S(2)}, u32[]{:S(2)}) collective-permute-start(bf16[13,14,256]{2,1,0:T(8,128)(2,1)S(1)} %get-tuple-element.32), channel_id=1, source_target_pairs={{0,8},{1,9},{2,10},{3,11},{4,12},{5,13},{6,14},{7,15},{8,16},{9,17... | collective-permute-start | bytes 279560 | tf_op jit(solution)/shard_map/ppermute | solution.py:51
  10.2 4.5 %renumber.1.refs_4_.refs_8_ = bf16[8,512,512]{2,1,0:T(8,128)(2,1)S(1)} custom-call(s32[2,2,2,512]{3,2,1,0:T(2,128)S(1)} %copy-done.4, bf16[8,512,512]{2,1,0:T(8,128)(2,1)S(1)} %bitcast.6), custom_call_target="tpu_custom_call" | custom-call | flops 4294967296 | bytes 8388608 | tf_op jit(solution)/shard_map/renumber/pallas_call | solution.py:127
  14.7 0.6 collective-permute-done.refs_1_
  15.3 2.1 %shard_map.38 = (f32[8,2,512,128]{3,2,1,0:T(8,128)S(1)}, f32[8,2,512,128]{3,2,1,0:T(8,128)S(1)}, bf16[14,16,256]{2,1,0:T(8,128)(2,1)S(1)}, bf16[14,16,256]{2,1,0...) custom-call(bf16[14,13,14,256]{3,2,1,0:T(8,128)(2,1)S(1)} %bitcast.4, ...), custom_call_target="tpu_custom_call" | custom-call | flops 1073741824 | bytes 14578688 | tf_op jit(solution)/shard_map/pallas_call | solution.py:701
  17.4 1.1 %collective-permute-start.3 = (bf16[14,16,256]{2,1,0:T(8,128)(2,1)S(1)}, bf16[14,16,256]{2,1,0:T(8,128)(2,1)S(1)}, u32[]{:S(2)}, u32[]{:S(2)}) collective-permute-start(bf16[14,16,256]{2,1,0:T(8,128)(2,1)S(1)} %get-tuple-element.36), channel_id=1, source_target_pairs={{0,8},{1,9},{2,10},{3,11},{4,12},{5,13},{6,14},{7,15},{8,0},{9,1},... | collective-permute-start | bytes 344072 | tf_op jit(solution)/shard_map/ppermute | solution.py:41
  18.5 0.7 collective-permute-start.4
  19.3 1.5 %collective-permute-start.6 = (bf16[4,64,256]{2,1,0:T(8,128)(2,1)S(1)}, bf16[4,64,256]{2,1,0:T(8,128)(2,1)S(1)}, u32[]{:S(2)}, u32[]{:S(2)}) collective-permute-start(bf16[4,64,256]{2,1,0:T(8,128)(2,1)S(1)} %get-tuple-element.39), channel_id=1, source_target_pairs={{0,7},{1,2},{2,1},{3,4},{4,3},{5,6},{6,5},{7,0},{8,15},{9,10},{10,... | collective-permute-start | bytes 393224 | tf_op jit(solution)/shard_map/ppermute | solution.py:41
  20.8 1.5 %collective-permute-done.3.from_a.refs_1_ = bf16[14,16,256]{2,1,0:T(8,128)(2,1)S(1)} collective-permute-done((bf16[14,16,256]{2,1,0:T(8,128)(2,1)S(1)}, bf16[14,16,256]{2,1,0:T(8,128)(2,1)S(1)}, u32[]{:S(2)}, u32[]{:S(2)}) %collective-permute-start.3) | collective-permute-done | bytes 114720 | tf_op jit(solution)/shard_map/ppermute | solution.py:41
  22.3 0.1 shard_map.39
  22.5 1.5 %collective-permute-start.8 = (f32[2,16,256]{2,1,0:T(8,128)S(1)}, f32[2,16,256]{2,1,0:T(8,128)S(1)}, u32[]{:S(2)}, u32[]{:S(2)}) collective-permute-start(f32[2,16,256]{2,1,0:T(8,128)S(1)} %get-tuple-element.41), channel_id=1, source_target_pairs={{0,7},{1,2},{2,1},{3,4},{4,3},{5,6},{6,5},{7,0},{8,15},{9,10},{10,... | collective-permute-start | bytes 98312 | tf_op jit(solution)/shard_map/ppermute | solution.py:41
  24.0 1.4 %collective-permute-done.6.refs_4_ = bf16[4,64,256]{2,1,0:T(8,128)(2,1)S(1)} collective-permute-done((bf16[4,64,256]{2,1,0:T(8,128)(2,1)S(1)}, bf16[4,64,256]{2,1,0:T(8,128)(2,1)S(1)}, u32[]{:S(2)}, u32[]{:S(2)}) %collective-permute-start.6) | collective-permute-done | bytes 131104 | tf_op jit(solution)/shard_map/ppermute | solution.py:41
  25.4 1.3 %collective-permute-done.8.refs_6_ = f32[2,16,256]{2,1,0:T(8,128)S(1)} collective-permute-done((f32[2,16,256]{2,1,0:T(8,128)S(1)}, f32[2,16,256]{2,1,0:T(8,128)S(1)}, u32[]{:S(2)}, u32[]{:S(2)}) %collective-permute-start.8) | collective-permute-done | bytes 32800 | tf_op jit(solution)/shard_map/ppermute | solution.py:41
  26.8 2.5 %shard_map.40 = (f32[8,2,512,128]{3,2,1,0:T(8,128)S(1)}, f32[8,2,512,128]{3,2,1,0:T(8,128)S(1)}, bf16[14,16,256]{2,1,0:T(8,128)(2,1)S(1)}, bf16[14,16,256]{2,1,0...) custom-call(f32[8,2,512,128]{3,2,1,0:T(8,128)S(1)} %get-tuple-element.35.refs_0_, ...), custom_call_target="tpu_custom_call" | custom-call | flops 1073741824 | bytes 22020096 | tf_op jit(solution)/shard_map/pallas_call | solution.py:701
  29.3 4.0 %collective-permute-start.9 = (bf16[14,16,256]{2,1,0:T(8,128)(2,1)S(1)}, bf16[14,16,256]{2,1,0:T(8,128)(2,1)S(1)}, u32[]{:S(2)}, u32[]{:S(2)}) collective-permute-start(bf16[14,16,256]{2,1,0:T(8,128)(2,1)S(1)} %get-tuple-element.44), channel_id=1, source_target_pairs={{0,8},{1,9},{2,10},{3,11},{4,12},{5,13},{6,14},{7,15},{8,0},{9,1},... | collective-permute-start | bytes 344072 | tf_op jit(solution)/shard_map/ppermute | solution.py:41
  33.3 0.7 collective-permute-start.10
  34.0 1.3 %collective-permute-start.12 = (bf16[4,64,256]{2,1,0:T(8,128)(2,1)S(1)}, bf16[4,64,256]{2,1,0:T(8,128)(2,1)S(1)}, u32[]{:S(2)}, u32[]{:S(2)}) collective-permute-start(bf16[4,64,256]{2,1,0:T(8,128)(2,1)S(1)} %get-tuple-element.47), channel_id=1, source_target_pairs={{0,7},{1,2},{2,1},{3,4},{4,3},{5,6},{6,5},{7,0},{8,15},{9,10},{10,... | collective-permute-start | bytes 393224 | tf_op jit(solution)/shard_map/ppermute | solution.py:41
  35.3 1.1 %collective-permute-done.9.from_a.refs_1_ = bf16[14,16,256]{2,1,0:T(8,128)(2,1)S(1)} collective-permute-done((bf16[14,16,256]{2,1,0:T(8,128)(2,1)S(1)}, bf16[14,16,256]{2,1,0:T(8,128)(2,1)S(1)}, u32[]{:S(2)}, u32[]{:S(2)}) %collective-permute-start.9) | collective-permute-done | bytes 114720 | tf_op jit(solution)/shard_map/ppermute | solution.py:41
  36.4 0.1 shard_map.41
  36.6 0.9 %collective-permute-start.14 = (f32[2,16,256]{2,1,0:T(8,128)S(1)}, f32[2,16,256]{2,1,0:T(8,128)S(1)}, u32[]{:S(2)}, u32[]{:S(2)}) collective-permute-start(f32[2,16,256]{2,1,0:T(8,128)S(1)} %get-tuple-element.49), channel_id=1, source_target_pairs={{0,7},{1,2},{2,1},{3,4},{4,3},{5,6},{6,5},{7,0},{8,15},{9,10},{10,... | collective-permute-start | bytes 98312 | tf_op jit(solution)/shard_map/ppermute | solution.py:41
  37.5 2.7 %collective-permute-done.12.refs_4_ = bf16[4,64,256]{2,1,0:T(8,128)(2,1)S(1)} collective-permute-done((bf16[4,64,256]{2,1,0:T(8,128)(2,1)S(1)}, bf16[4,64,256]{2,1,0:T(8,128)(2,1)S(1)}, u32[]{:S(2)}, u32[]{:S(2)}) %collective-permute-start.12) | collective-permute-done | bytes 131104 | tf_op jit(solution)/shard_map/ppermute | solution.py:41
  40.1 1.0 %collective-permute-done.14.refs_6_ = f32[2,16,256]{2,1,0:T(8,128)S(1)} collective-permute-done((f32[2,16,256]{2,1,0:T(8,128)S(1)}, f32[2,16,256]{2,1,0:T(8,128)S(1)}, u32[]{:S(2)}, u32[]{:S(2)}) %collective-permute-start.14) | collective-permute-done | bytes 32800 | tf_op jit(solution)/shard_map/ppermute | solution.py:41
  41.1 2.5 %shard_map.42 = (f32[8,2,512,128]{3,2,1,0:T(8,128)S(1)}, bf16[14,16,256]{2,1,0:T(8,128)(2,1)S(1)}, bf16[4,64,256]{2,1,0:T(8,128)(2,1)S(1)}, f32[16,256]{1,0:T(8,128)S(1)}) custom-call(f32[8,2,512,128]{3,2,1,0:T(8,128)S(1)} %get-tuple-element.43.refs_0_, bf16[14,16,256]{2,1,0:T(8,128)(2,1)S(1)} %collective-permute-done.9.from_a.refs_1_, ...), custom_call_target="tpu_custom_call" | custom-call | flops 1073741824 | bytes 17596416 | tf_op jit(solution)/shard_map/pallas_call | solution.py:701
  43.6 1.6 %collective-permute-start.16 = (bf16[4,64,256]{2,1,0:T(8,128)(2,1)S(1)}, bf16[4,64,256]{2,1,0:T(8,128)(2,1)S(1)}, u32[]{:S(2)}, u32[]{:S(2)}) collective-permute-start(bf16[4,64,256]{2,1,0:T(8,128)(2,1)S(1)} %get-tuple-element.53), channel_id=1, source_target_pairs={{0,7},{1,0},{2,1},{3,2},{4,3},{5,4},{6,5},{7,6},{8,15},{9,8},{10,9... | collective-permute-start | bytes 393224 | tf_op jit(solution)/shard_map/ppermute | solution.py:51
  45.2 1.7 %collective-permute-start.15 = (bf16[14,16,256]{2,1,0:T(8,128)(2,1)S(1)}, bf16[14,16,256]{2,1,0:T(8,128)(2,1)S(1)}, u32[]{:S(2)}, u32[]{:S(2)}) collective-permute-start(bf16[14,16,256]{2,1,0:T(8,128)(2,1)S(1)} %get-tuple-element.52), channel_id=1, source_target_pairs={{0,24},{1,25},{2,26},{3,27},{4,28},{5,29},{6,30},{7,31},{8,0},{9,1... | collective-permute-start | bytes 344072 | tf_op jit(solution)/shard_map/ppermute | solution.py:51
  46.9 2.8 %collective-permute-start.17 = (f32[16,256]{1,0:T(8,128)S(1)}, f32[16,256]{1,0:T(8,128)S(1)}, u32[]{:S(2)}, u32[]{:S(2)}) collective-permute-start(f32[16,256]{1,0:T(8,128)S(1)} %get-tuple-element.54), channel_id=1, source_target_pairs={{0,31},{1,24},{2,25},{3,26},{4,27},{5,28},{6,29},{7,30},{8,7},{9,0... | collective-permute-start | bytes 49160 | tf_op jit(solution)/shard_map/ppermute | solution.py:51
  49.7 1.4 %collective-permute-done.17.from_xy = f32[16,256]{1,0:T(8,128)S(1)} collective-permute-done((f32[16,256]{1,0:T(8,128)S(1)}, f32[16,256]{1,0:T(8,128)S(1)}, u32[]{:S(2)}, u32[]{:S(2)}) %collective-permute-start.17) | collective-permute-done | bytes 16416 | tf_op jit(solution)/shard_map/ppermute | solution.py:51
  51.2 0.4 collective-permute-done.15.from_x
  51.5 2.1 %shard_map.43 = (bf16[2912,256]{1,0:T(8,128)(2,1)S(1)}, bf16[2912,256]{1,0:T(8,128)(2,1)S(1)}, f32[136,128]{1,0:T(8,128)S(1)}, f32[136,128]{1,0:T(8,128)S(1)}) custom-call(f32[8,2,512,128]{3,2,1,0:T(8,128)S(1)} %get-tuple-element.51.part_ref, bf16[14,16,256]{2,1,0:T(8,128)(2,1)S(1)} %collective-permute-done.15.from_x, ...), custom_call_target="tpu_custom_call" | custom-call | flops 1526726656 | bytes 7577600 | tf_op jit(solution)/shard_map/pallas_call | solution.py:701
  53.7 0.6 collective-permute-start.18
  54.3 0.9 %collective-permute-done.18 = f32[136,128]{1,0:T(8,128)S(1)} collective-permute-done((f32[136,128]{1,0:T(8,128)S(1)}, f32[136,128]{1,0:T(8,128)S(1)}, u32[]{:S(2)}, u32[]{:S(2)}) %collective-permute-start.18) | collective-permute-done | bytes 69664 | tf_op jit(solution)/shard_map/ppermute | solution.py:55
  55.2 3.8 %collective-permute-start.21 = (f32[136,128]{1,0:T(8,128)S(1)}, f32[136,128]{1,0:T(8,128)S(1)}, u32[]{:S(2)}, u32[]{:S(2)}) collective-permute-start(f32[136,128]{1,0:T(8,128)S(1)} %add.21), channel_id=1, source_target_pairs={{0,24},{1,7},{2,26},{3,5},{4,28},{5,3},{6,30},{7,1},{8,16},{9,15},... | collective-permute-start | bytes 208904 | tf_op jit(solution)/shard_map/ppermute | solution.py:66
  59.0 0.7 collective-permute-start.19
  59.7 1.8 %collective-permute-done.21 = f32[136,128]{1,0:T(8,128)S(1)} collective-permute-done((f32[136,128]{1,0:T(8,128)S(1)}, f32[136,128]{1,0:T(8,128)S(1)}, u32[]{:S(2)}, u32[]{:S(2)}) %collective-permute-start.21) | collective-permute-done | bytes 69664 | tf_op jit(solution)/shard_map/ppermute | solution.py:66
  61.5 2.7 %collective-permute-done.20 = f32[136,128]{1,0:T(8,128)S(1)} collective-permute-done((f32[136,128]{1,0:T(8,128)S(1)}, f32[136,128]{1,0:T(8,128)S(1)}, u32[]{:S(2)}, u32[]{:S(2)}) %collective-permute-start.20) | collective-permute-done | bytes 69664 | tf_op jit(solution)/shard_map/ppermute | solution.py:66
  64.2 1.7 %collective-permute-start.24 = (f32[136,128]{1,0:T(8,128)S(1)}, f32[136,128]{1,0:T(8,128)S(1)}, u32[]{:S(2)}, u32[]{:S(2)}) collective-permute-start(f32[136,128]{1,0:T(8,128)S(1)} %add_add_fusion.1), channel_id=1, source_target_pairs={{0,6},{1,25},{2,4},{3,27},{4,2},{5,29},{6,0},{7,31},{8,14},{9,17},... | collective-permute-start | bytes 208904 | tf_op jit(solution)/shard_map/ppermute | solution.py:66
  65.9 1.4 %collective-permute-start.23 = (f32[136,128]{1,0:T(8,128)S(1)}, f32[136,128]{1,0:T(8,128)S(1)}, u32[]{:S(2)}, u32[]{:S(2)}) collective-permute-start(f32[136,128]{1,0:T(8,128)S(1)} %add_add_fusion.1), channel_id=1, source_target_pairs={{0,4},{1,17},{2,6},{3,19},{4,0},{5,21},{6,2},{7,23},{8,12},{9,25},... | collective-permute-start | bytes 208904 | tf_op jit(solution)/shard_map/ppermute | solution.py:66
  67.3 0.5 collective-permute-start.22
  67.8 1.7 %collective-permute-done.24 = f32[136,128]{1,0:T(8,128)S(1)} collective-permute-done((f32[136,128]{1,0:T(8,128)S(1)}, f32[136,128]{1,0:T(8,128)S(1)}, u32[]{:S(2)}, u32[]{:S(2)}) %collective-permute-start.24) | collective-permute-done | bytes 69664 | tf_op jit(solution)/shard_map/ppermute | solution.py:66
  69.5 0.7 collective-permute-done.23
  70.2 1.4 %collective-permute-done.22 = f32[136,128]{1,0:T(8,128)S(1)} collective-permute-done((f32[136,128]{1,0:T(8,128)S(1)}, f32[136,128]{1,0:T(8,128)S(1)}, u32[]{:S(2)}, u32[]{:S(2)}) %collective-permute-start.22) | collective-permute-done | bytes 69664 | tf_op jit(solution)/shard_map/ppermute | solution.py:66
  71.7 1.2 %collective-permute-done.25.other_ref = f32[136,128]{1,0:T(8,128)S(1)} collective-permute-done((f32[136,128]{1,0:T(8,128)S(1)}, f32[136,128]{1,0:T(8,128)S(1)}, u32[]{:S(2)}, u32[]{:S(2)}) %collective-permute-start.25) | collective-permute-done | bytes 69664 | tf_op jit(solution)/shard_map/ppermute | solution.py:55
  73.0 14.6 %basis.1 = f32[14,13,14,256]{3,2,1,0:T(8,128)} custom-call(f32[136,128]{1,0:T(8,128)S(1)} %add_add_fusion.mine_ref, f32[136,128]{1,0:T(8,128)S(1)} %collective-permute-done.25.other_ref, bf16[2912,256]{1,0:T(8,128)(2,1)S(1)} %get-tuple-element.57.high_ref, bf16[2912,256]{1,0:T(8,128)(2,1)S(1)} %get-tuple-element.58.low_ref), custom_call_target="tpu_custom_call" | custom-call | tf_op jit(solution)/shard_map/basis/pallas_call | solution.py:790
  (26 shorter events, 0.4 us)
Async XLA Ops:
  0.0 1.4 %copy-start = (bf16[14,14,13,256]{3,1,2,0:T(8,128)(2,1)S(1)}, bf16[14,14,13,256]{3,1,2,0:T(8,128)(2,1)}, u32[]{:S(2)}) copy-start(bf16[14,14,13,256]{3,1,2,0:T(8,128)(2,1)} %param.3) | copy-start | bytes 3913732
  1.4 2.2 %copy-start.2 = (bf16[2,2,2,512,512]{4,3,2,1,0:T(8,128)(2,1)S(1)}, bf16[2,2,2,512,512]{4,3,2,1,0:T(8,128)(2,1)}, u32[]{:S(2)}) copy-start(bf16[2,2,2,512,512]{4,3,2,1,0:T(8,128)(2,1)} %param.4) | copy-start | bytes 12582916
  3.6 0.7 copy-start.4
  4.3 5.9 %copy-start.3 = (bf16[2,2,2,512,512]{4,3,2,1,0:T(8,128)(2,1)S(1)}, bf16[2,2,2,512,512]{4,3,2,1,0:T(8,128)(2,1)}, u32[]{:S(2)}) copy-start(bf16[2,2,2,512,512]{4,3,2,1,0:T(8,128)(2,1)} %param.4) | copy-start | bytes 12582916
  4.5 10.2 %collective-permute-start.2 = (bf16[16,256]{1,0:T(8,128)(2,1)S(1)}, bf16[16,256]{1,0:T(8,128)(2,1)S(1)}, u32[]{:S(2)}, u32[]{:S(2)}) collective-permute-start(bf16[16,256]{1,0:T(8,128)(2,1)S(1)} %get-tuple-element.34), channel_id=1, source_target_pairs={{0,9},{1,10},{2,11},{3,12},{4,13},{5,14},{6,15},{7,8},{8,17},{9,18... | collective-permute-start | bytes 24584 | tf_op jit(solution)/shard_map/ppermute | solution.py:51
  7.0 8.3 %collective-permute-start.1 = (bf16[192,256]{1,0:T(8,128)(2,1)S(1)}, bf16[192,256]{1,0:T(8,128)(2,1)S(1)}, u32[]{:S(2)}, u32[]{:S(2)}) collective-permute-start(bf16[192,256]{1,0:T(8,128)(2,1)S(1)} %get-tuple-element.33), channel_id=1, source_target_pairs={{0,1},{1,2},{2,3},{3,4},{4,5},{5,6},{6,7},{7,0},{8,9},{9,10},{10,1... | collective-permute-start | bytes 294920 | tf_op jit(solution)/shard_map/ppermute | solution.py:51
  8.6 6.7 %copy-start.1 = (bf16[14,14,13,256]{3,1,2,0:T(8,128)(2,1)S(1)}, bf16[14,14,13,256]{3,1,2,0:T(8,128)(2,1)}, u32[]{:S(2)}) copy-start(bf16[14,14,13,256]{3,1,2,0:T(8,128)(2,1)} %param.3) | copy-start | bytes 3913732
  8.6 6.7 %collective-permute-start = (bf16[13,14,256]{2,1,0:T(8,128)(2,1)S(1)}, bf16[13,14,256]{2,1,0:T(8,128)(2,1)S(1)}, u32[]{:S(2)}, u32[]{:S(2)}) collective-permute-start(bf16[13,14,256]{2,1,0:T(8,128)(2,1)S(1)} %get-tuple-element.32), channel_id=1, source_target_pairs={{0,8},{1,9},{2,10},{3,11},{4,12},{5,13},{6,14},{7,15},{8,16},{9,17... | collective-permute-start | bytes 279560 | tf_op jit(solution)/shard_map/ppermute | solution.py:51
  17.4 4.9 %collective-permute-start.3 = (bf16[14,16,256]{2,1,0:T(8,128)(2,1)S(1)}, bf16[14,16,256]{2,1,0:T(8,128)(2,1)S(1)}, u32[]{:S(2)}, u32[]{:S(2)}) collective-permute-start(bf16[14,16,256]{2,1,0:T(8,128)(2,1)S(1)} %get-tuple-element.36), channel_id=1, source_target_pairs={{0,8},{1,9},{2,10},{3,11},{4,12},{5,13},{6,14},{7,15},{8,0},{9,1},... | collective-permute-start | bytes 344072 | tf_op jit(solution)/shard_map/ppermute | solution.py:41
  18.5 3.7 %collective-permute-start.4 = (bf16[14,16,256]{2,1,0:T(8,128)(2,1)S(1)}, bf16[14,16,256]{2,1,0:T(8,128)(2,1)S(1)}, u32[]{:S(2)}, u32[]{:S(2)}) collective-permute-start(bf16[14,16,256]{2,1,0:T(8,128)(2,1)S(1)} %get-tuple-element.37), channel_id=1, source_target_pairs={{0,0},{1,1},{2,2},{3,3},{4,4},{5,5},{6,6},{7,7},{8,16},{9,17},{10,... | collective-permute-start | bytes 344072 | tf_op jit(solution)/shard_map/ppermute | solution.py:41
  19.2 4.8 %collective-permute-start.5 = (bf16[4,64,256]{2,1,0:T(8,128)(2,1)S(1)}, bf16[4,64,256]{2,1,0:T(8,128)(2,1)S(1)}, u32[]{:S(2)}, u32[]{:S(2)}) collective-permute-start(bf16[4,64,256]{2,1,0:T(8,128)(2,1)S(1)} %get-tuple-element.38), channel_id=1, source_target_pairs={{0,1},{1,0},{2,3},{3,2},{4,5},{5,4},{6,7},{7,6},{8,9},{9,8},{10,11... | collective-permute-start | bytes 393224 | tf_op jit(solution)/shard_map/ppermute | solution.py:41
  19.3 6.1 %collective-permute-start.6 = (bf16[4,64,256]{2,1,0:T(8,128)(2,1)S(1)}, bf16[4,64,256]{2,1,0:T(8,128)(2,1)S(1)}, u32[]{:S(2)}, u32[]{:S(2)}) collective-permute-start(bf16[4,64,256]{2,1,0:T(8,128)(2,1)S(1)} %get-tuple-element.39), channel_id=1, source_target_pairs={{0,7},{1,2},{2,1},{3,4},{4,3},{5,6},{6,5},{7,0},{8,15},{9,10},{10,... | collective-permute-start | bytes 393224 | tf_op jit(solution)/shard_map/ppermute | solution.py:41
  22.4 3.0 %collective-permute-start.7 = (f32[2,16,256]{2,1,0:T(8,128)S(1)}, f32[2,16,256]{2,1,0:T(8,128)S(1)}, u32[]{:S(2)}, u32[]{:S(2)}) collective-permute-start(f32[2,16,256]{2,1,0:T(8,128)S(1)} %get-tuple-element.40), channel_id=1, source_target_pairs={{0,1},{1,0},{2,3},{3,2},{4,5},{5,4},{6,7},{7,6},{8,9},{9,8},{10,11... | collective-permute-start | bytes 98312 | tf_op jit(solution)/shard_map/ppermute | solution.py:41
  22.5 4.3 %collective-permute-start.8 = (f32[2,16,256]{2,1,0:T(8,128)S(1)}, f32[2,16,256]{2,1,0:T(8,128)S(1)}, u32[]{:S(2)}, u32[]{:S(2)}) collective-permute-start(f32[2,16,256]{2,1,0:T(8,128)S(1)} %get-tuple-element.41), channel_id=1, source_target_pairs={{0,7},{1,2},{2,1},{3,4},{4,3},{5,6},{6,5},{7,0},{8,15},{9,10},{10,... | collective-permute-start | bytes 98312 | tf_op jit(solution)/shard_map/ppermute | solution.py:41
  29.3 7.1 %collective-permute-start.9 = (bf16[14,16,256]{2,1,0:T(8,128)(2,1)S(1)}, bf16[14,16,256]{2,1,0:T(8,128)(2,1)S(1)}, u32[]{:S(2)}, u32[]{:S(2)}) collective-permute-start(bf16[14,16,256]{2,1,0:T(8,128)(2,1)S(1)} %get-tuple-element.44), channel_id=1, source_target_pairs={{0,8},{1,9},{2,10},{3,11},{4,12},{5,13},{6,14},{7,15},{8,0},{9,1},... | collective-permute-start | bytes 344072 | tf_op jit(solution)/shard_map/ppermute | solution.py:41
  33.3 3.1 %collective-permute-start.10 = (bf16[14,16,256]{2,1,0:T(8,128)(2,1)S(1)}, bf16[14,16,256]{2,1,0:T(8,128)(2,1)S(1)}, u32[]{:S(2)}, u32[]{:S(2)}) collective-permute-start(bf16[14,16,256]{2,1,0:T(8,128)(2,1)S(1)} %get-tuple-element.45), channel_id=1, source_target_pairs={{0,0},{1,1},{2,2},{3,3},{4,4},{5,5},{6,6},{7,7},{8,16},{9,17},{10,... | collective-permute-start | bytes 344072 | tf_op jit(solution)/shard_map/ppermute | solution.py:41
  33.9 3.6 %collective-permute-start.11 = (bf16[4,64,256]{2,1,0:T(8,128)(2,1)S(1)}, bf16[4,64,256]{2,1,0:T(8,128)(2,1)S(1)}, u32[]{:S(2)}, u32[]{:S(2)}) collective-permute-start(bf16[4,64,256]{2,1,0:T(8,128)(2,1)S(1)} %get-tuple-element.46), channel_id=1, source_target_pairs={{0,1},{1,0},{2,3},{3,2},{4,5},{5,4},{6,7},{7,6},{8,9},{9,8},{10,11... | collective-permute-start | bytes 393224 | tf_op jit(solution)/shard_map/ppermute | solution.py:41
  34.0 6.1 %collective-permute-start.12 = (bf16[4,64,256]{2,1,0:T(8,128)(2,1)S(1)}, bf16[4,64,256]{2,1,0:T(8,128)(2,1)S(1)}, u32[]{:S(2)}, u32[]{:S(2)}) collective-permute-start(bf16[4,64,256]{2,1,0:T(8,128)(2,1)S(1)} %get-tuple-element.47), channel_id=1, source_target_pairs={{0,7},{1,2},{2,1},{3,4},{4,3},{5,6},{6,5},{7,0},{8,15},{9,10},{10,... | collective-permute-start | bytes 393224 | tf_op jit(solution)/shard_map/ppermute | solution.py:41
  36.5 3.6 %collective-permute-start.13 = (f32[2,16,256]{2,1,0:T(8,128)S(1)}, f32[2,16,256]{2,1,0:T(8,128)S(1)}, u32[]{:S(2)}, u32[]{:S(2)}) collective-permute-start(f32[2,16,256]{2,1,0:T(8,128)S(1)} %get-tuple-element.48), channel_id=1, source_target_pairs={{0,1},{1,0},{2,3},{3,2},{4,5},{5,4},{6,7},{7,6},{8,9},{9,8},{10,11... | collective-permute-start | bytes 98312 | tf_op jit(solution)/shard_map/ppermute | solution.py:41
  36.6 4.5 %collective-permute-start.14 = (f32[2,16,256]{2,1,0:T(8,128)S(1)}, f32[2,16,256]{2,1,0:T(8,128)S(1)}, u32[]{:S(2)}, u32[]{:S(2)}) collective-permute-start(f32[2,16,256]{2,1,0:T(8,128)S(1)} %get-tuple-element.49), channel_id=1, source_target_pairs={{0,7},{1,2},{2,1},{3,4},{4,3},{5,6},{6,5},{7,0},{8,15},{9,10},{10,... | collective-permute-start | bytes 98312 | tf_op jit(solution)/shard_map/ppermute | solution.py:41
  43.6 8.0 %collective-permute-start.16 = (bf16[4,64,256]{2,1,0:T(8,128)(2,1)S(1)}, bf16[4,64,256]{2,1,0:T(8,128)(2,1)S(1)}, u32[]{:S(2)}, u32[]{:S(2)}) collective-permute-start(bf16[4,64,256]{2,1,0:T(8,128)(2,1)S(1)} %get-tuple-element.53), channel_id=1, source_target_pairs={{0,7},{1,0},{2,1},{3,2},{4,3},{5,4},{6,5},{7,6},{8,15},{9,8},{10,9... | collective-permute-start | bytes 393224 | tf_op jit(solution)/shard_map/ppermute | solution.py:51
  45.2 6.4 %collective-permute-start.15 = (bf16[14,16,256]{2,1,0:T(8,128)(2,1)S(1)}, bf16[14,16,256]{2,1,0:T(8,128)(2,1)S(1)}, u32[]{:S(2)}, u32[]{:S(2)}) collective-permute-start(bf16[14,16,256]{2,1,0:T(8,128)(2,1)S(1)} %get-tuple-element.52), channel_id=1, source_target_pairs={{0,24},{1,25},{2,26},{3,27},{4,28},{5,29},{6,30},{7,31},{8,0},{9,1... | collective-permute-start | bytes 344072 | tf_op jit(solution)/shard_map/ppermute | solution.py:51
  46.9 4.3 %collective-permute-start.17 = (f32[16,256]{1,0:T(8,128)S(1)}, f32[16,256]{1,0:T(8,128)S(1)}, u32[]{:S(2)}, u32[]{:S(2)}) collective-permute-start(f32[16,256]{1,0:T(8,128)S(1)} %get-tuple-element.54), channel_id=1, source_target_pairs={{0,31},{1,24},{2,25},{3,26},{4,27},{5,28},{6,29},{7,30},{8,7},{9,0... | collective-permute-start | bytes 49160 | tf_op jit(solution)/shard_map/ppermute | solution.py:51
  53.7 1.5 %collective-permute-start.18 = (f32[136,128]{1,0:T(8,128)S(1)}, f32[136,128]{1,0:T(8,128)S(1)}, u32[]{:S(2)}, u32[]{:S(2)}) collective-permute-start(f32[136,128]{1,0:T(8,128)S(1)} %get-tuple-element.56), channel_id=1, source_target_pairs={{0,1},{1,0},{2,3},{3,2},{4,5},{5,4},{6,7},{7,6},{8,9},{9,8},{10,11... | collective-permute-start | bytes 208904 | tf_op jit(solution)/shard_map/ppermute | solution.py:55
  55.2 6.3 %collective-permute-start.21 = (f32[136,128]{1,0:T(8,128)S(1)}, f32[136,128]{1,0:T(8,128)S(1)}, u32[]{:S(2)}, u32[]{:S(2)}) collective-permute-start(f32[136,128]{1,0:T(8,128)S(1)} %add.21), channel_id=1, source_target_pairs={{0,24},{1,7},{2,26},{3,5},{4,28},{5,3},{6,30},{7,1},{8,16},{9,15},... | collective-permute-start | bytes 208904 | tf_op jit(solution)/shard_map/ppermute | solution.py:66
  59.0 5.2 %collective-permute-start.20 = (f32[136,128]{1,0:T(8,128)S(1)}, f32[136,128]{1,0:T(8,128)S(1)}, u32[]{:S(2)}, u32[]{:S(2)}) collective-permute-start(f32[136,128]{1,0:T(8,128)S(1)} %add.21), channel_id=1, source_target_pairs={{0,16},{1,5},{2,18},{3,7},{4,20},{5,1},{6,22},{7,3},{8,24},{9,13},... | collective-permute-start | bytes 208904 | tf_op jit(solution)/shard_map/ppermute | solution.py:66
  59.0 5.2 %collective-permute-start.19 = (f32[136,128]{1,0:T(8,128)S(1)}, f32[136,128]{1,0:T(8,128)S(1)}, u32[]{:S(2)}, u32[]{:S(2)}) collective-permute-start(f32[136,128]{1,0:T(8,128)S(1)} %add.21), channel_id=1, source_target_pairs={{0,8},{1,3},{2,10},{3,1},{4,12},{5,7},{6,14},{7,5},{8,0},{9,11},{1... | collective-permute-start | bytes 208904 | tf_op jit(solution)/shard_map/ppermute | solution.py:66
  64.2 5.3 %collective-permute-start.24 = (f32[136,128]{1,0:T(8,128)S(1)}, f32[136,128]{1,0:T(8,128)S(1)}, u32[]{:S(2)}, u32[]{:S(2)}) collective-permute-start(f32[136,128]{1,0:T(8,128)S(1)} %add_add_fusion.1), channel_id=1, source_target_pairs={{0,6},{1,25},{2,4},{3,27},{4,2},{5,29},{6,0},{7,31},{8,14},{9,17},... | collective-permute-start | bytes 208904 | tf_op jit(solution)/shard_map/ppermute | solution.py:66
  65.9 4.3 %collective-permute-start.23 = (f32[136,128]{1,0:T(8,128)S(1)}, f32[136,128]{1,0:T(8,128)S(1)}, u32[]{:S(2)}, u32[]{:S(2)}) collective-permute-start(f32[136,128]{1,0:T(8,128)S(1)} %add_add_fusion.1), channel_id=1, source_target_pairs={{0,4},{1,17},{2,6},{3,19},{4,0},{5,21},{6,2},{7,23},{8,12},{9,25},... | collective-permute-start | bytes 208904 | tf_op jit(solution)/shard_map/ppermute | solution.py:66
  67.3 4.3 %collective-permute-start.22 = (f32[136,128]{1,0:T(8,128)S(1)}, f32[136,128]{1,0:T(8,128)S(1)}, u32[]{:S(2)}, u32[]{:S(2)}) collective-permute-start(f32[136,128]{1,0:T(8,128)S(1)} %add_add_fusion.1), channel_id=1, source_target_pairs={{0,2},{1,9},{2,0},{3,11},{4,6},{5,13},{6,4},{7,15},{8,10},{9,1},{1... | collective-permute-start | bytes 208904 | tf_op jit(solution)/shard_map/ppermute | solution.py:66
  71.6 1.3 %collective-permute-start.25 = (f32[136,128]{1,0:T(8,128)S(1)}, f32[136,128]{1,0:T(8,128)S(1)}, u32[]{:S(2)}, u32[]{:S(2)}) collective-permute-start(f32[136,128]{1,0:T(8,128)S(1)} %add_add_fusion.mine_ref), channel_id=1, source_target_pairs={{0,1},{1,0},{2,3},{3,2},{4,5},{5,4},{6,7},{7,6},{8,9},{9,8},{10,11... | collective-permute-start | bytes 208904 | tf_op jit(solution)/shard_map/ppermute | solution.py:55

commit v6 on v5

--- a/solution.py
+++ b/solution.py
@@ -373,8 +373,7 @@
     return jnp.concatenate(parts, axis=-1)
 
 
-def edge_kernel(orb_ref, mats_ref, conn_ref, x_ref, y_ref, line_ref, tiles_ref):
-    del mats_ref, conn_ref
+def edge_kernel(orb_ref, x_ref, y_ref, line_ref, tiles_ref):
     nx, nz, ny, bands = orb_ref.shape
     last = (ny - 1) % ROWS
     tail = slice(ny - 1 - last, ny)
@@ -727,7 +726,7 @@
             shape((2 * ROWS, bands), orb.dtype),
         ],
         [pltpu.VMEM((bands // LANES, tall, LANES), f32)],
-        (orb, elem_mats, conn),
+        (orb,),
         0,
     )
     below_x, below_y, below_xy = [
@@ -785,7 +784,7 @@
         8 * rows * bands**2,
     )
     mine, other = halved_total(kept, sent)
-    slabs = g.ex * g.deg // 2
+    slabs = g.ex
     spot = pl.BlockSpec((nx // slabs, nz, ny, bands), lambda i: (i, 0, 0, 0))
     basis = pl.pallas_call(
         functools.partial(basis_kernel, scale=math.sqrt(nx * ny * nz * lax.axis_size(AXES))),

time: 87.8 us -> 86.9 us (0.990)
  Pallas kernels: 28.7 us -> 26.9 us
  starting transfers between devices: 32.4 us -> 34.1 us
    pallas_call x1, Pallas kernels: 14.6 us -> 12.8 us  [shards(): pl.pallas_call(functools.partial(basis_kernel, scale=math.sqrt(nx * ny *...]
    ppermute x6, waiting for transfers between devices: 2.39 us -> 1.46 us  [ring(): return lax.ppermute(value, AXES, route)]
    ppermute x6, starting transfers between devices: 8.01 us -> 8.93 us  [sum_swap(): return lax.ppermute(value, AXES, route)]
    unnamed x10 -> x8, local copies, waits for them, and re-layouts: 4.29 us -> 4.29 us
  transfers between devices with their start and end apart: 26 -> 26, of which waited for: 16 -> 14; matrix products, arithmetic and copies ran while one was open for 0% -> 0% of each run, Pallas kernels for 5% -> 5%
where the time goes in v6:
time: 86.9 us; the launch traced here: 86.6 us
  starting transfers between devices  34.1 us (39%)
  Pallas kernels  26.9 us (31%)
  waiting for transfers between devices  21.1 us (24%)
  local copies, waits for them, and re-layouts  4.29 us (5%)
    pallas_call x1, Pallas kernels, shards(): pl.pallas_call(functools.partial(basis_kernel, scale=math.sqrt(nx * ny *...  12.8 us
    ppermute x6, starting transfers between devices, ring(): return lax.ppermute(value, AXES, route)  12.4 us
    ppermute x12, starting transfers between devices, pair_swap(): return lax.ppermute(value, AXES, route)  12.3 us
    pallas_call x7, Pallas kernels, call(): pl.pallas_call(kernel, out_shape=outs, in_specs=[VMEM] * len(operands), o...  9.59 us
    ppermute x6, starting transfers between devices, sum_swap(): return lax.ppermute(value, AXES, route)  8.93 us
    ppermute x6, waiting for transfers between devices, sum_swap(): return lax.ppermute(value, AXES, route)  8.87 us
    ppermute x12, waiting for transfers between devices, pair_swap(): return lax.ppermute(value, AXES, route)  8.65 us
    pallas_call x1, Pallas kernels, renumber(): pl.pallas_call(functools.partial(renumber_kernel, g=g, width=width, depth...  4.52 us
  transfers between devices with their start and end apart: 26, of which 14 were waited for; matrix products, arithmetic and copies ran while one was open for 0% of the time, Pallas kernels for 5%

profile of v6, /device:TPU:0, one launch (start us, length us, event | category | flops | bytes accessed | tf_op | source)
XLA Modules:
  0.0 86.6 jit_solution(14748179833211093867)
XLA Ops:
  0.0 1.4 %copy-done = bf16[14,14,13,256]{3,1,2,0:T(8,128)(2,1)S(1)} copy-done((bf16[14,14,13,256]{3,1,2,0:T(8,128)(2,1)S(1)}, bf16[14,14,13,256]{3,1,2,0:T(8,128)(2,1)}, u32[]{:S(2)}) %copy-start) | copy-done | bytes 1304600
  1.4 0.2 shard_map.37
  1.6 2.5 %collective-permute-start.2 = (bf16[16,256]{1,0:T(8,128)(2,1)S(1)}, bf16[16,256]{1,0:T(8,128)(2,1)S(1)}, u32[]{:S(2)}, u32[]{:S(2)}) collective-permute-start(bf16[16,256]{1,0:T(8,128)(2,1)S(1)} %get-tuple-element.34), channel_id=1, source_target_pairs={{0,9},{1,10},{2,11},{3,12},{4,13},{5,14},{6,15},{7,8},{8,17},{9,18... | collective-permute-start | bytes 24584 | tf_op jit(solution)/shard_map/ppermute | solution.py:51
  4.1 1.6 %collective-permute-start.1 = (bf16[192,256]{1,0:T(8,128)(2,1)S(1)}, bf16[192,256]{1,0:T(8,128)(2,1)S(1)}, u32[]{:S(2)}, u32[]{:S(2)}) collective-permute-start(bf16[192,256]{1,0:T(8,128)(2,1)S(1)} %get-tuple-element.33), channel_id=1, source_target_pairs={{0,1},{1,2},{2,3},{3,4},{4,5},{5,6},{6,7},{7,0},{8,9},{9,10},{10,1... | collective-permute-start | bytes 294920 | tf_op jit(solution)/shard_map/ppermute | solution.py:51
  5.7 1.6 %collective-permute-start = (bf16[13,14,256]{2,1,0:T(8,128)(2,1)S(1)}, bf16[13,14,256]{2,1,0:T(8,128)(2,1)S(1)}, u32[]{:S(2)}, u32[]{:S(2)}) collective-permute-start(bf16[13,14,256]{2,1,0:T(8,128)(2,1)S(1)} %get-tuple-element.32), channel_id=1, source_target_pairs={{0,8},{1,9},{2,10},{3,11},{4,12},{5,13},{6,14},{7,15},{8,16},{9,17... | collective-permute-start | bytes 279560 | tf_op jit(solution)/shard_map/ppermute | solution.py:51
  7.3 2.2 %copy-done.2 = bf16[2,2,2,512,512]{4,3,2,1,0:T(8,128)(2,1)S(1)} copy-done((bf16[2,2,2,512,512]{4,3,2,1,0:T(8,128)(2,1)S(1)}, bf16[2,2,2,512,512]{4,3,2,1,0:T(8,128)(2,1)}, u32[]{:S(2)}) %copy-start.2) | copy-done | bytes 4194328
  9.5 0.7 copy-done.3
  10.2 4.5 %renumber.1.refs_4_.refs_8_ = bf16[8,512,512]{2,1,0:T(8,128)(2,1)S(1)} custom-call(s32[2,2,2,512]{3,2,1,0:T(2,128)S(1)} %copy-done.3, bf16[8,512,512]{2,1,0:T(8,128)(2,1)S(1)} %bitcast.5), custom_call_target="tpu_custom_call" | custom-call | flops 4294967296 | bytes 8388608 | tf_op jit(solution)/shard_map/renumber/pallas_call | solution.py:127
  14.7 2.1 %shard_map.38 = (f32[8,2,512,128]{3,2,1,0:T(8,128)S(1)}, f32[8,2,512,128]{3,2,1,0:T(8,128)S(1)}, bf16[14,16,256]{2,1,0:T(8,128)(2,1)S(1)}, bf16[14,16,256]{2,1,0...) custom-call(bf16[14,13,14,256]{3,2,1,0:T(8,128)(2,1)S(1)} %bitcast.4, ...), custom_call_target="tpu_custom_call" | custom-call | flops 1073741824 | bytes 14578688 | tf_op jit(solution)/shard_map/pallas_call | solution.py:700
  16.9 1.6 %collective-permute-start.3 = (bf16[14,16,256]{2,1,0:T(8,128)(2,1)S(1)}, bf16[14,16,256]{2,1,0:T(8,128)(2,1)S(1)}, u32[]{:S(2)}, u32[]{:S(2)}) collective-permute-start(bf16[14,16,256]{2,1,0:T(8,128)(2,1)S(1)} %get-tuple-element.36), channel_id=1, source_target_pairs={{0,8},{1,9},{2,10},{3,11},{4,12},{5,13},{6,14},{7,15},{8,0},{9,1},... | collective-permute-start | bytes 344072 | tf_op jit(solution)/shard_map/ppermute | solution.py:41
  18.5 0.7 collective-permute-start.4
  19.2 0.1 collective-permute-start.5
  19.3 1.5 %collective-permute-start.6 = (bf16[4,64,256]{2,1,0:T(8,128)(2,1)S(1)}, bf16[4,64,256]{2,1,0:T(8,128)(2,1)S(1)}, u32[]{:S(2)}, u32[]{:S(2)}) collective-permute-start(bf16[4,64,256]{2,1,0:T(8,128)(2,1)S(1)} %get-tuple-element.39), channel_id=1, source_target_pairs={{0,7},{1,2},{2,1},{3,4},{4,3},{5,6},{6,5},{7,0},{8,15},{9,10},{10,... | collective-permute-start | bytes 393224 | tf_op jit(solution)/shard_map/ppermute | solution.py:41
  20.8 0.9 %collective-permute-done.3.from_a.refs_1_ = bf16[14,16,256]{2,1,0:T(8,128)(2,1)S(1)} collective-permute-done((bf16[14,16,256]{2,1,0:T(8,128)(2,1)S(1)}, bf16[14,16,256]{2,1,0:T(8,128)(2,1)S(1)}, u32[]{:S(2)}, u32[]{:S(2)}) %collective-permute-start.3) | collective-permute-done | bytes 114720 | tf_op jit(solution)/shard_map/ppermute | solution.py:41
  21.7 0.1 shard_map.39
  21.8 0.1 collective-permute-start.7
  21.9 1.5 %collective-permute-start.8 = (f32[2,16,256]{2,1,0:T(8,128)S(1)}, f32[2,16,256]{2,1,0:T(8,128)S(1)}, u32[]{:S(2)}, u32[]{:S(2)}) collective-permute-start(f32[2,16,256]{2,1,0:T(8,128)S(1)} %get-tuple-element.41), channel_id=1, source_target_pairs={{0,7},{1,2},{2,1},{3,4},{4,3},{5,6},{6,5},{7,0},{8,15},{9,10},{10,... | collective-permute-start | bytes 98312 | tf_op jit(solution)/shard_map/ppermute | solution.py:41
  23.5 2.0 %collective-permute-done.6.refs_4_ = bf16[4,64,256]{2,1,0:T(8,128)(2,1)S(1)} collective-permute-done((bf16[4,64,256]{2,1,0:T(8,128)(2,1)S(1)}, bf16[4,64,256]{2,1,0:T(8,128)(2,1)S(1)}, u32[]{:S(2)}, u32[]{:S(2)}) %collective-permute-start.6) | collective-permute-done | bytes 131104 | tf_op jit(solution)/shard_map/ppermute | solution.py:41
  25.4 1.0 %collective-permute-done.8.refs_6_ = f32[2,16,256]{2,1,0:T(8,128)S(1)} collective-permute-done((f32[2,16,256]{2,1,0:T(8,128)S(1)}, f32[2,16,256]{2,1,0:T(8,128)S(1)}, u32[]{:S(2)}, u32[]{:S(2)}) %collective-permute-start.8) | collective-permute-done | bytes 32800 | tf_op jit(solution)/shard_map/ppermute | solution.py:41
  26.4 2.5 %shard_map.40 = (f32[8,2,512,128]{3,2,1,0:T(8,128)S(1)}, f32[8,2,512,128]{3,2,1,0:T(8,128)S(1)}, bf16[14,16,256]{2,1,0:T(8,128)(2,1)S(1)}, bf16[14,16,256]{2,1,0...) custom-call(f32[8,2,512,128]{3,2,1,0:T(8,128)S(1)} %get-tuple-element.35.refs_0_, ...), custom_call_target="tpu_custom_call" | custom-call | flops 1073741824 | bytes 22020096 | tf_op jit(solution)/shard_map/pallas_call | solution.py:700
  28.9 3.8 %collective-permute-start.9 = (bf16[14,16,256]{2,1,0:T(8,128)(2,1)S(1)}, bf16[14,16,256]{2,1,0:T(8,128)(2,1)S(1)}, u32[]{:S(2)}, u32[]{:S(2)}) collective-permute-start(bf16[14,16,256]{2,1,0:T(8,128)(2,1)S(1)} %get-tuple-element.44), channel_id=1, source_target_pairs={{0,8},{1,9},{2,10},{3,11},{4,12},{5,13},{6,14},{7,15},{8,0},{9,1},... | collective-permute-start | bytes 344072 | tf_op jit(solution)/shard_map/ppermute | solution.py:41
  32.7 0.7 collective-permute-start.10
  33.4 0.1 collective-permute-start.11
  33.5 1.3 %collective-permute-start.12 = (bf16[4,64,256]{2,1,0:T(8,128)(2,1)S(1)}, bf16[4,64,256]{2,1,0:T(8,128)(2,1)S(1)}, u32[]{:S(2)}, u32[]{:S(2)}) collective-permute-start(bf16[4,64,256]{2,1,0:T(8,128)(2,1)S(1)} %get-tuple-element.47), channel_id=1, source_target_pairs={{0,7},{1,2},{2,1},{3,4},{4,3},{5,6},{6,5},{7,0},{8,15},{9,10},{10,... | collective-permute-start | bytes 393224 | tf_op jit(solution)/shard_map/ppermute | solution.py:41
  34.7 1.1 %collective-permute-done.9.from_a.refs_1_ = bf16[14,16,256]{2,1,0:T(8,128)(2,1)S(1)} collective-permute-done((bf16[14,16,256]{2,1,0:T(8,128)(2,1)S(1)}, bf16[14,16,256]{2,1,0:T(8,128)(2,1)S(1)}, u32[]{:S(2)}, u32[]{:S(2)}) %collective-permute-start.9) | collective-permute-done | bytes 114720 | tf_op jit(solution)/shard_map/ppermute | solution.py:41
  35.9 0.1 shard_map.41
  36.0 0.9 %collective-permute-start.14 = (f32[2,16,256]{2,1,0:T(8,128)S(1)}, f32[2,16,256]{2,1,0:T(8,128)S(1)}, u32[]{:S(2)}, u32[]{:S(2)}) collective-permute-start(f32[2,16,256]{2,1,0:T(8,128)S(1)} %get-tuple-element.49), channel_id=1, source_target_pairs={{0,7},{1,2},{2,1},{3,4},{4,3},{5,6},{6,5},{7,0},{8,15},{9,10},{10,... | collective-permute-start | bytes 98312 | tf_op jit(solution)/shard_map/ppermute | solution.py:41
  36.9 2.7 %collective-permute-done.12.refs_4_ = bf16[4,64,256]{2,1,0:T(8,128)(2,1)S(1)} collective-permute-done((bf16[4,64,256]{2,1,0:T(8,128)(2,1)S(1)}, bf16[4,64,256]{2,1,0:T(8,128)(2,1)S(1)}, u32[]{:S(2)}, u32[]{:S(2)}) %collective-permute-start.12) | collective-permute-done | bytes 131104 | tf_op jit(solution)/shard_map/ppermute | solution.py:41
  39.6 1.0 %collective-permute-done.14.refs_6_ = f32[2,16,256]{2,1,0:T(8,128)S(1)} collective-permute-done((f32[2,16,256]{2,1,0:T(8,128)S(1)}, f32[2,16,256]{2,1,0:T(8,128)S(1)}, u32[]{:S(2)}, u32[]{:S(2)}) %collective-permute-start.14) | collective-permute-done | bytes 32800 | tf_op jit(solution)/shard_map/ppermute | solution.py:41
  40.6 2.5 %shard_map.42 = (f32[8,2,512,128]{3,2,1,0:T(8,128)S(1)}, bf16[14,16,256]{2,1,0:T(8,128)(2,1)S(1)}, bf16[4,64,256]{2,1,0:T(8,128)(2,1)S(1)}, f32[16,256]{1,0:T(8,128)S(1)}) custom-call(f32[8,2,512,128]{3,2,1,0:T(8,128)S(1)} %get-tuple-element.43.refs_0_, bf16[14,16,256]{2,1,0:T(8,128)(2,1)S(1)} %collective-permute-done.9.from_a.refs_1_, ...), custom_call_target="tpu_custom_call" | custom-call | flops 1073741824 | bytes 17596416 | tf_op jit(solution)/shard_map/pallas_call | solution.py:700
  43.1 1.4 %collective-permute-start.16 = (bf16[4,64,256]{2,1,0:T(8,128)(2,1)S(1)}, bf16[4,64,256]{2,1,0:T(8,128)(2,1)S(1)}, u32[]{:S(2)}, u32[]{:S(2)}) collective-permute-start(bf16[4,64,256]{2,1,0:T(8,128)(2,1)S(1)} %get-tuple-element.53), channel_id=1, source_target_pairs={{0,7},{1,0},{2,1},{3,2},{4,3},{5,4},{6,5},{7,6},{8,15},{9,8},{10,9... | collective-permute-start | bytes 393224 | tf_op jit(solution)/shard_map/ppermute | solution.py:51
  44.4 2.3 %collective-permute-start.15 = (bf16[14,16,256]{2,1,0:T(8,128)(2,1)S(1)}, bf16[14,16,256]{2,1,0:T(8,128)(2,1)S(1)}, u32[]{:S(2)}, u32[]{:S(2)}) collective-permute-start(bf16[14,16,256]{2,1,0:T(8,128)(2,1)S(1)} %get-tuple-element.52), channel_id=1, source_target_pairs={{0,24},{1,25},{2,26},{3,27},{4,28},{5,29},{6,30},{7,31},{8,0},{9,1... | collective-permute-start | bytes 344072 | tf_op jit(solution)/shard_map/ppermute | solution.py:51
  46.7 3.0 %collective-permute-start.17 = (f32[16,256]{1,0:T(8,128)S(1)}, f32[16,256]{1,0:T(8,128)S(1)}, u32[]{:S(2)}, u32[]{:S(2)}) collective-permute-start(f32[16,256]{1,0:T(8,128)S(1)} %get-tuple-element.54), channel_id=1, source_target_pairs={{0,31},{1,24},{2,25},{3,26},{4,27},{5,28},{6,29},{7,30},{8,7},{9,0... | collective-permute-start | bytes 49160 | tf_op jit(solution)/shard_map/ppermute | solution.py:51
  49.7 1.4 %collective-permute-done.17.from_xy = f32[16,256]{1,0:T(8,128)S(1)} collective-permute-done((f32[16,256]{1,0:T(8,128)S(1)}, f32[16,256]{1,0:T(8,128)S(1)}, u32[]{:S(2)}, u32[]{:S(2)}) %collective-permute-start.17) | collective-permute-done | bytes 16416 | tf_op jit(solution)/shard_map/ppermute | solution.py:51
  51.2 2.1 %shard_map.43 = (bf16[2912,256]{1,0:T(8,128)(2,1)S(1)}, bf16[2912,256]{1,0:T(8,128)(2,1)S(1)}, f32[136,128]{1,0:T(8,128)S(1)}, f32[136,128]{1,0:T(8,128)S(1)}) custom-call(f32[8,2,512,128]{3,2,1,0:T(8,128)S(1)} %get-tuple-element.51.part_ref, bf16[14,16,256]{2,1,0:T(8,128)(2,1)S(1)} %collective-permute-done.15.from_x, ...), custom_call_target="tpu_custom_call" | custom-call | flops 1526726656 | bytes 7577600 | tf_op jit(solution)/shard_map/pallas_call | solution.py:700
  53.3 0.5 collective-permute-start.18
  53.7 0.9 %collective-permute-done.18 = f32[136,128]{1,0:T(8,128)S(1)} collective-permute-done((f32[136,128]{1,0:T(8,128)S(1)}, f32[136,128]{1,0:T(8,128)S(1)}, u32[]{:S(2)}, u32[]{:S(2)}) %collective-permute-start.18) | collective-permute-done | bytes 69664 | tf_op jit(solution)/shard_map/ppermute | solution.py:55
  54.7 4.3 %collective-permute-start.21 = (f32[136,128]{1,0:T(8,128)S(1)}, f32[136,128]{1,0:T(8,128)S(1)}, u32[]{:S(2)}, u32[]{:S(2)}) collective-permute-start(f32[136,128]{1,0:T(8,128)S(1)} %add.21), channel_id=1, source_target_pairs={{0,24},{1,7},{2,26},{3,5},{4,28},{5,3},{6,30},{7,1},{8,16},{9,15},... | collective-permute-start | bytes 208904 | tf_op jit(solution)/shard_map/ppermute | solution.py:66
  58.9 0.6 collective-permute-start.19
  59.6 1.6 %collective-permute-done.21 = f32[136,128]{1,0:T(8,128)S(1)} collective-permute-done((f32[136,128]{1,0:T(8,128)S(1)}, f32[136,128]{1,0:T(8,128)S(1)}, u32[]{:S(2)}, u32[]{:S(2)}) %collective-permute-start.21) | collective-permute-done | bytes 69664 | tf_op jit(solution)/shard_map/ppermute | solution.py:66
  61.2 2.9 %collective-permute-done.20 = f32[136,128]{1,0:T(8,128)S(1)} collective-permute-done((f32[136,128]{1,0:T(8,128)S(1)}, f32[136,128]{1,0:T(8,128)S(1)}, u32[]{:S(2)}, u32[]{:S(2)}) %collective-permute-start.20) | collective-permute-done | bytes 69664 | tf_op jit(solution)/shard_map/ppermute | solution.py:66
  64.2 2.3 %collective-permute-start.24 = (f32[136,128]{1,0:T(8,128)S(1)}, f32[136,128]{1,0:T(8,128)S(1)}, u32[]{:S(2)}, u32[]{:S(2)}) collective-permute-start(f32[136,128]{1,0:T(8,128)S(1)} %add_add_fusion.1), channel_id=1, source_target_pairs={{0,6},{1,25},{2,4},{3,27},{4,2},{5,29},{6,0},{7,31},{8,14},{9,17},... | collective-permute-start | bytes 208904 | tf_op jit(solution)/shard_map/ppermute | solution.py:66
  66.5 1.7 %collective-permute-start.23 = (f32[136,128]{1,0:T(8,128)S(1)}, f32[136,128]{1,0:T(8,128)S(1)}, u32[]{:S(2)}, u32[]{:S(2)}) collective-permute-start(f32[136,128]{1,0:T(8,128)S(1)} %add_add_fusion.1), channel_id=1, source_target_pairs={{0,4},{1,17},{2,6},{3,19},{4,0},{5,21},{6,2},{7,23},{8,12},{9,25},... | collective-permute-start | bytes 208904 | tf_op jit(solution)/shard_map/ppermute | solution.py:66
  68.2 1.3 %collective-permute-done.24 = f32[136,128]{1,0:T(8,128)S(1)} collective-permute-done((f32[136,128]{1,0:T(8,128)S(1)}, f32[136,128]{1,0:T(8,128)S(1)}, u32[]{:S(2)}, u32[]{:S(2)}) %collective-permute-start.24) | collective-permute-done | bytes 69664 | tf_op jit(solution)/shard_map/ppermute | solution.py:66
  69.4 1.3 %collective-permute-done.23 = f32[136,128]{1,0:T(8,128)S(1)} collective-permute-done((f32[136,128]{1,0:T(8,128)S(1)}, f32[136,128]{1,0:T(8,128)S(1)}, u32[]{:S(2)}, u32[]{:S(2)}) %collective-permute-start.23) | collective-permute-done | bytes 69664 | tf_op jit(solution)/shard_map/ppermute | solution.py:66
  70.8 1.7 %collective-permute-done.22 = f32[136,128]{1,0:T(8,128)S(1)} collective-permute-done((f32[136,128]{1,0:T(8,128)S(1)}, f32[136,128]{1,0:T(8,128)S(1)}, u32[]{:S(2)}, u32[]{:S(2)}) %collective-permute-start.22) | collective-permute-done | bytes 69664 | tf_op jit(solution)/shard_map/ppermute | solution.py:66
  72.6 1.2 %collective-permute-done.25.other_ref = f32[136,128]{1,0:T(8,128)S(1)} collective-permute-done((f32[136,128]{1,0:T(8,128)S(1)}, f32[136,128]{1,0:T(8,128)S(1)}, u32[]{:S(2)}, u32[]{:S(2)}) %collective-permute-start.25) | collective-permute-done | bytes 69664 | tf_op jit(solution)/shard_map/ppermute | solution.py:55
  73.8 12.8 %basis.1 = f32[14,13,14,256]{3,2,1,0:T(8,128)} custom-call(f32[136,128]{1,0:T(8,128)S(1)} %add_add_fusion.mine_ref, f32[136,128]{1,0:T(8,128)S(1)} %collective-permute-done.25.other_ref, bf16[2912,256]{1,0:T(8,128)(2,1)S(1)} %get-tuple-element.57.high_ref, bf16[2912,256]{1,0:T(8,128)(2,1)S(1)} %get-tuple-element.58.low_ref), custom_call_target="tpu_custom_call" | custom-call | tf_op jit(solution)/shard_map/basis/pallas_call | solution.py:789
  (24 shorter events, 0.2 us)
Async XLA Ops:
  0.0 1.4 %copy-start = (bf16[14,14,13,256]{3,1,2,0:T(8,128)(2,1)S(1)}, bf16[14,14,13,256]{3,1,2,0:T(8,128)(2,1)}, u32[]{:S(2)}) copy-start(bf16[14,14,13,256]{3,1,2,0:T(8,128)(2,1)} %param.3) | copy-start | bytes 3913732
  1.6 13.1 %collective-permute-start.2 = (bf16[16,256]{1,0:T(8,128)(2,1)S(1)}, bf16[16,256]{1,0:T(8,128)(2,1)S(1)}, u32[]{:S(2)}, u32[]{:S(2)}) collective-permute-start(bf16[16,256]{1,0:T(8,128)(2,1)S(1)} %get-tuple-element.34), channel_id=1, source_target_pairs={{0,9},{1,10},{2,11},{3,12},{4,13},{5,14},{6,15},{7,8},{8,17},{9,18... | collective-permute-start | bytes 24584 | tf_op jit(solution)/shard_map/ppermute | solution.py:51
  4.1 10.6 %collective-permute-start.1 = (bf16[192,256]{1,0:T(8,128)(2,1)S(1)}, bf16[192,256]{1,0:T(8,128)(2,1)S(1)}, u32[]{:S(2)}, u32[]{:S(2)}) collective-permute-start(bf16[192,256]{1,0:T(8,128)(2,1)S(1)} %get-tuple-element.33), channel_id=1, source_target_pairs={{0,1},{1,2},{2,3},{3,4},{4,5},{5,6},{6,7},{7,0},{8,9},{9,10},{10,1... | collective-permute-start | bytes 294920 | tf_op jit(solution)/shard_map/ppermute | solution.py:51
  5.7 9.0 %collective-permute-start = (bf16[13,14,256]{2,1,0:T(8,128)(2,1)S(1)}, bf16[13,14,256]{2,1,0:T(8,128)(2,1)S(1)}, u32[]{:S(2)}, u32[]{:S(2)}) collective-permute-start(bf16[13,14,256]{2,1,0:T(8,128)(2,1)S(1)} %get-tuple-element.32), channel_id=1, source_target_pairs={{0,8},{1,9},{2,10},{3,11},{4,12},{5,13},{6,14},{7,15},{8,16},{9,17... | collective-permute-start | bytes 279560 | tf_op jit(solution)/shard_map/ppermute | solution.py:51
  7.3 2.2 %copy-start.2 = (bf16[2,2,2,512,512]{4,3,2,1,0:T(8,128)(2,1)S(1)}, bf16[2,2,2,512,512]{4,3,2,1,0:T(8,128)(2,1)}, u32[]{:S(2)}) copy-start(bf16[2,2,2,512,512]{4,3,2,1,0:T(8,128)(2,1)} %param.4) | copy-start | bytes 12582916
  9.5 0.7 copy-start.3
  10.2 4.6 %copy-start.1 = (bf16[14,14,13,256]{3,1,2,0:T(8,128)(2,1)S(1)}, bf16[14,14,13,256]{3,1,2,0:T(8,128)(2,1)}, u32[]{:S(2)}) copy-start(bf16[14,14,13,256]{3,1,2,0:T(8,128)(2,1)} %param.3) | copy-start | bytes 3913732
  16.9 4.9 %collective-permute-start.3 = (bf16[14,16,256]{2,1,0:T(8,128)(2,1)S(1)}, bf16[14,16,256]{2,1,0:T(8,128)(2,1)S(1)}, u32[]{:S(2)}, u32[]{:S(2)}) collective-permute-start(bf16[14,16,256]{2,1,0:T(8,128)(2,1)S(1)} %get-tuple-element.36), channel_id=1, source_target_pairs={{0,8},{1,9},{2,10},{3,11},{4,12},{5,13},{6,14},{7,15},{8,0},{9,1},... | collective-permute-start | bytes 344072 | tf_op jit(solution)/shard_map/ppermute | solution.py:41
  18.5 3.2 %collective-permute-start.4 = (bf16[14,16,256]{2,1,0:T(8,128)(2,1)S(1)}, bf16[14,16,256]{2,1,0:T(8,128)(2,1)S(1)}, u32[]{:S(2)}, u32[]{:S(2)}) collective-permute-start(bf16[14,16,256]{2,1,0:T(8,128)(2,1)S(1)} %get-tuple-element.37), channel_id=1, source_target_pairs={{0,0},{1,1},{2,2},{3,3},{4,4},{5,5},{6,6},{7,7},{8,16},{9,17},{10,... | collective-permute-start | bytes 344072 | tf_op jit(solution)/shard_map/ppermute | solution.py:41
  19.2 4.3 %collective-permute-start.5 = (bf16[4,64,256]{2,1,0:T(8,128)(2,1)S(1)}, bf16[4,64,256]{2,1,0:T(8,128)(2,1)S(1)}, u32[]{:S(2)}, u32[]{:S(2)}) collective-permute-start(bf16[4,64,256]{2,1,0:T(8,128)(2,1)S(1)} %get-tuple-element.38), channel_id=1, source_target_pairs={{0,1},{1,0},{2,3},{3,2},{4,5},{5,4},{6,7},{7,6},{8,9},{9,8},{10,11... | collective-permute-start | bytes 393224 | tf_op jit(solution)/shard_map/ppermute | solution.py:41
  19.3 6.1 %collective-permute-start.6 = (bf16[4,64,256]{2,1,0:T(8,128)(2,1)S(1)}, bf16[4,64,256]{2,1,0:T(8,128)(2,1)S(1)}, u32[]{:S(2)}, u32[]{:S(2)}) collective-permute-start(bf16[4,64,256]{2,1,0:T(8,128)(2,1)S(1)} %get-tuple-element.39), channel_id=1, source_target_pairs={{0,7},{1,2},{2,1},{3,4},{4,3},{5,6},{6,5},{7,0},{8,15},{9,10},{10,... | collective-permute-start | bytes 393224 | tf_op jit(solution)/shard_map/ppermute | solution.py:41
  21.8 3.6 %collective-permute-start.7 = (f32[2,16,256]{2,1,0:T(8,128)S(1)}, f32[2,16,256]{2,1,0:T(8,128)S(1)}, u32[]{:S(2)}, u32[]{:S(2)}) collective-permute-start(f32[2,16,256]{2,1,0:T(8,128)S(1)} %get-tuple-element.40), channel_id=1, source_target_pairs={{0,1},{1,0},{2,3},{3,2},{4,5},{5,4},{6,7},{7,6},{8,9},{9,8},{10,11... | collective-permute-start | bytes 98312 | tf_op jit(solution)/shard_map/ppermute | solution.py:41
  21.9 4.5 %collective-permute-start.8 = (f32[2,16,256]{2,1,0:T(8,128)S(1)}, f32[2,16,256]{2,1,0:T(8,128)S(1)}, u32[]{:S(2)}, u32[]{:S(2)}) collective-permute-start(f32[2,16,256]{2,1,0:T(8,128)S(1)} %get-tuple-element.41), channel_id=1, source_target_pairs={{0,7},{1,2},{2,1},{3,4},{4,3},{5,6},{6,5},{7,0},{8,15},{9,10},{10,... | collective-permute-start | bytes 98312 | tf_op jit(solution)/shard_map/ppermute | solution.py:41
  28.9 6.9 %collective-permute-start.9 = (bf16[14,16,256]{2,1,0:T(8,128)(2,1)S(1)}, bf16[14,16,256]{2,1,0:T(8,128)(2,1)S(1)}, u32[]{:S(2)}, u32[]{:S(2)}) collective-permute-start(bf16[14,16,256]{2,1,0:T(8,128)(2,1)S(1)} %get-tuple-element.44), channel_id=1, source_target_pairs={{0,8},{1,9},{2,10},{3,11},{4,12},{5,13},{6,14},{7,15},{8,0},{9,1},... | collective-permute-start | bytes 344072 | tf_op jit(solution)/shard_map/ppermute | solution.py:41
  32.7 3.1 %collective-permute-start.10 = (bf16[14,16,256]{2,1,0:T(8,128)(2,1)S(1)}, bf16[14,16,256]{2,1,0:T(8,128)(2,1)S(1)}, u32[]{:S(2)}, u32[]{:S(2)}) collective-permute-start(bf16[14,16,256]{2,1,0:T(8,128)(2,1)S(1)} %get-tuple-element.45), channel_id=1, source_target_pairs={{0,0},{1,1},{2,2},{3,3},{4,4},{5,5},{6,6},{7,7},{8,16},{9,17},{10,... | collective-permute-start | bytes 344072 | tf_op jit(solution)/shard_map/ppermute | solution.py:41
  33.4 3.6 %collective-permute-start.11 = (bf16[4,64,256]{2,1,0:T(8,128)(2,1)S(1)}, bf16[4,64,256]{2,1,0:T(8,128)(2,1)S(1)}, u32[]{:S(2)}, u32[]{:S(2)}) collective-permute-start(bf16[4,64,256]{2,1,0:T(8,128)(2,1)S(1)} %get-tuple-element.46), channel_id=1, source_target_pairs={{0,1},{1,0},{2,3},{3,2},{4,5},{5,4},{6,7},{7,6},{8,9},{9,8},{10,11... | collective-permute-start | bytes 393224 | tf_op jit(solution)/shard_map/ppermute | solution.py:41
  33.5 6.1 %collective-permute-start.12 = (bf16[4,64,256]{2,1,0:T(8,128)(2,1)S(1)}, bf16[4,64,256]{2,1,0:T(8,128)(2,1)S(1)}, u32[]{:S(2)}, u32[]{:S(2)}) collective-permute-start(bf16[4,64,256]{2,1,0:T(8,128)(2,1)S(1)} %get-tuple-element.47), channel_id=1, source_target_pairs={{0,7},{1,2},{2,1},{3,4},{4,3},{5,6},{6,5},{7,0},{8,15},{9,10},{10,... | collective-permute-start | bytes 393224 | tf_op jit(solution)/shard_map/ppermute | solution.py:41
  36.0 3.6 %collective-permute-start.13 = (f32[2,16,256]{2,1,0:T(8,128)S(1)}, f32[2,16,256]{2,1,0:T(8,128)S(1)}, u32[]{:S(2)}, u32[]{:S(2)}) collective-permute-start(f32[2,16,256]{2,1,0:T(8,128)S(1)} %get-tuple-element.48), channel_id=1, source_target_pairs={{0,1},{1,0},{2,3},{3,2},{4,5},{5,4},{6,7},{7,6},{8,9},{9,8},{10,11... | collective-permute-start | bytes 98312 | tf_op jit(solution)/shard_map/ppermute | solution.py:41
  36.0 4.5 %collective-permute-start.14 = (f32[2,16,256]{2,1,0:T(8,128)S(1)}, f32[2,16,256]{2,1,0:T(8,128)S(1)}, u32[]{:S(2)}, u32[]{:S(2)}) collective-permute-start(f32[2,16,256]{2,1,0:T(8,128)S(1)} %get-tuple-element.49), channel_id=1, source_target_pairs={{0,7},{1,2},{2,1},{3,4},{4,3},{5,6},{6,5},{7,0},{8,15},{9,10},{10,... | collective-permute-start | bytes 98312 | tf_op jit(solution)/shard_map/ppermute | solution.py:41
  43.1 8.1 %collective-permute-start.16 = (bf16[4,64,256]{2,1,0:T(8,128)(2,1)S(1)}, bf16[4,64,256]{2,1,0:T(8,128)(2,1)S(1)}, u32[]{:S(2)}, u32[]{:S(2)}) collective-permute-start(bf16[4,64,256]{2,1,0:T(8,128)(2,1)S(1)} %get-tuple-element.53), channel_id=1, source_target_pairs={{0,7},{1,0},{2,1},{3,2},{4,3},{5,4},{6,5},{7,6},{8,15},{9,8},{10,9... | collective-permute-start | bytes 393224 | tf_op jit(solution)/shard_map/ppermute | solution.py:51
  44.4 6.7 %collective-permute-start.15 = (bf16[14,16,256]{2,1,0:T(8,128)(2,1)S(1)}, bf16[14,16,256]{2,1,0:T(8,128)(2,1)S(1)}, u32[]{:S(2)}, u32[]{:S(2)}) collective-permute-start(bf16[14,16,256]{2,1,0:T(8,128)(2,1)S(1)} %get-tuple-element.52), channel_id=1, source_target_pairs={{0,24},{1,25},{2,26},{3,27},{4,28},{5,29},{6,30},{7,31},{8,0},{9,1... | collective-permute-start | bytes 344072 | tf_op jit(solution)/shard_map/ppermute | solution.py:51
  46.7 4.5 %collective-permute-start.17 = (f32[16,256]{1,0:T(8,128)S(1)}, f32[16,256]{1,0:T(8,128)S(1)}, u32[]{:S(2)}, u32[]{:S(2)}) collective-permute-start(f32[16,256]{1,0:T(8,128)S(1)} %get-tuple-element.54), channel_id=1, source_target_pairs={{0,31},{1,24},{2,25},{3,26},{4,27},{5,28},{6,29},{7,30},{8,7},{9,0... | collective-permute-start | bytes 49160 | tf_op jit(solution)/shard_map/ppermute | solution.py:51
  53.3 1.4 %collective-permute-start.18 = (f32[136,128]{1,0:T(8,128)S(1)}, f32[136,128]{1,0:T(8,128)S(1)}, u32[]{:S(2)}, u32[]{:S(2)}) collective-permute-start(f32[136,128]{1,0:T(8,128)S(1)} %get-tuple-element.56), channel_id=1, source_target_pairs={{0,1},{1,0},{2,3},{3,2},{4,5},{5,4},{6,7},{7,6},{8,9},{9,8},{10,11... | collective-permute-start | bytes 208904 | tf_op jit(solution)/shard_map/ppermute | solution.py:55
  54.7 6.6 %collective-permute-start.21 = (f32[136,128]{1,0:T(8,128)S(1)}, f32[136,128]{1,0:T(8,128)S(1)}, u32[]{:S(2)}, u32[]{:S(2)}) collective-permute-start(f32[136,128]{1,0:T(8,128)S(1)} %add.21), channel_id=1, source_target_pairs={{0,24},{1,7},{2,26},{3,5},{4,28},{5,3},{6,30},{7,1},{8,16},{9,15},... | collective-permute-start | bytes 208904 | tf_op jit(solution)/shard_map/ppermute | solution.py:66
  58.9 5.2 %collective-permute-start.20 = (f32[136,128]{1,0:T(8,128)S(1)}, f32[136,128]{1,0:T(8,128)S(1)}, u32[]{:S(2)}, u32[]{:S(2)}) collective-permute-start(f32[136,128]{1,0:T(8,128)S(1)} %add.21), channel_id=1, source_target_pairs={{0,16},{1,5},{2,18},{3,7},{4,20},{5,1},{6,22},{7,3},{8,24},{9,13},... | collective-permute-start | bytes 208904 | tf_op jit(solution)/shard_map/ppermute | solution.py:66
  58.9 5.2 %collective-permute-start.19 = (f32[136,128]{1,0:T(8,128)S(1)}, f32[136,128]{1,0:T(8,128)S(1)}, u32[]{:S(2)}, u32[]{:S(2)}) collective-permute-start(f32[136,128]{1,0:T(8,128)S(1)} %add.21), channel_id=1, source_target_pairs={{0,8},{1,3},{2,10},{3,1},{4,12},{5,7},{6,14},{7,5},{8,0},{9,11},{1... | collective-permute-start | bytes 208904 | tf_op jit(solution)/shard_map/ppermute | solution.py:66
  64.2 5.3 %collective-permute-start.24 = (f32[136,128]{1,0:T(8,128)S(1)}, f32[136,128]{1,0:T(8,128)S(1)}, u32[]{:S(2)}, u32[]{:S(2)}) collective-permute-start(f32[136,128]{1,0:T(8,128)S(1)} %add_add_fusion.1), channel_id=1, source_target_pairs={{0,6},{1,25},{2,4},{3,27},{4,2},{5,29},{6,0},{7,31},{8,14},{9,17},... | collective-permute-start | bytes 208904 | tf_op jit(solution)/shard_map/ppermute | solution.py:66
  66.5 4.3 %collective-permute-start.23 = (f32[136,128]{1,0:T(8,128)S(1)}, f32[136,128]{1,0:T(8,128)S(1)}, u32[]{:S(2)}, u32[]{:S(2)}) collective-permute-start(f32[136,128]{1,0:T(8,128)S(1)} %add_add_fusion.1), channel_id=1, source_target_pairs={{0,4},{1,17},{2,6},{3,19},{4,0},{5,21},{6,2},{7,23},{8,12},{9,25},... | collective-permute-start | bytes 208904 | tf_op jit(solution)/shard_map/ppermute | solution.py:66
  68.2 4.3 %collective-permute-start.22 = (f32[136,128]{1,0:T(8,128)S(1)}, f32[136,128]{1,0:T(8,128)S(1)}, u32[]{:S(2)}, u32[]{:S(2)}) collective-permute-start(f32[136,128]{1,0:T(8,128)S(1)} %add_add_fusion.1), channel_id=1, source_target_pairs={{0,2},{1,9},{2,0},{3,11},{4,6},{5,13},{6,4},{7,15},{8,10},{9,1},{1... | collective-permute-start | bytes 208904 | tf_op jit(solution)/shard_map/ppermute | solution.py:66
  72.5 1.3 %collective-permute-start.25 = (f32[136,128]{1,0:T(8,128)S(1)}, f32[136,128]{1,0:T(8,128)S(1)}, u32[]{:S(2)}, u32[]{:S(2)}) collective-permute-start(f32[136,128]{1,0:T(8,128)S(1)} %add_add_fusion.mine_ref), channel_id=1, source_target_pairs={{0,1},{1,0},{2,3},{3,2},{4,5},{5,4},{6,7},{7,6},{8,9},{9,8},{10,11... | collective-permute-start | bytes 208904 | tf_op jit(solution)/shard_map/ppermute | solution.py:55

commit v7 on v6

--- a/solution.py
+++ b/solution.py
@@ -784,7 +784,7 @@
         8 * rows * bands**2,
     )
     mine, other = halved_total(kept, sent)
-    slabs = g.ex
+    slabs = 1
     spot = pl.BlockSpec((nx // slabs, nz, ny, bands), lambda i: (i, 0, 0, 0))
     basis = pl.pallas_call(
         functools.partial(basis_kernel, scale=math.sqrt(nx * ny * nz * lax.axis_size(AXES))),

time: 86.9 us -> 87.4 us (level)
  no operation moved by 1% of the time
where the time goes in v7:
time: 87.4 us; the launch traced here: 87.1 us
  starting transfers between devices  34.1 us (39%)
  Pallas kernels  27.4 us (31%)
  waiting for transfers between devices  21.1 us (24%)
  local copies, waits for them, and re-layouts  4.29 us (5%)
    pallas_call x1, Pallas kernels, shards(): pl.pallas_call(functools.partial(basis_kernel, scale=math.sqrt(nx * ny *...  13.3 us
    ppermute x6, starting transfers between devices, ring(): return lax.ppermute(value, AXES, route)  12.4 us
    ppermute x12, starting transfers between devices, pair_swap(): return lax.ppermute(value, AXES, route)  12.3 us
    pallas_call x7, Pallas kernels, call(): pl.pallas_call(kernel, out_shape=outs, in_specs=[VMEM] * len(operands), o...  9.59 us
    ppermute x6, starting transfers between devices, sum_swap(): return lax.ppermute(value, AXES, route)  8.93 us
    ppermute x6, waiting for transfers between devices, sum_swap(): return lax.ppermute(value, AXES, route)  8.87 us
    ppermute x12, waiting for transfers between devices, pair_swap(): return lax.ppermute(value, AXES, route)  8.65 us
    pallas_call x1, Pallas kernels, renumber(): pl.pallas_call(functools.partial(renumber_kernel, g=g, width=width, depth...  4.52 us
  transfers between devices with their start and end apart: 26, of which 14 were waited for; matrix products, arithmetic and copies ran while one was open for 0% of the time, Pallas kernels for 5%

profile of v7, /device:TPU:0, one launch (start us, length us, event | category | flops | bytes accessed | tf_op | source)
XLA Modules:
  0.0 87.1 jit_solution(16114341912022734223)
XLA Ops:
  0.0 1.4 %copy-done = bf16[14,14,13,256]{3,1,2,0:T(8,128)(2,1)S(1)} copy-done((bf16[14,14,13,256]{3,1,2,0:T(8,128)(2,1)S(1)}, bf16[14,14,13,256]{3,1,2,0:T(8,128)(2,1)}, u32[]{:S(2)}) %copy-start) | copy-done | bytes 1304600
  1.4 0.2 shard_map.37
  1.6 2.5 %collective-permute-start.2 = (bf16[16,256]{1,0:T(8,128)(2,1)S(1)}, bf16[16,256]{1,0:T(8,128)(2,1)S(1)}, u32[]{:S(2)}, u32[]{:S(2)}) collective-permute-start(bf16[16,256]{1,0:T(8,128)(2,1)S(1)} %get-tuple-element.34), channel_id=1, source_target_pairs={{0,9},{1,10},{2,11},{3,12},{4,13},{5,14},{6,15},{7,8},{8,17},{9,18... | collective-permute-start | bytes 24584 | tf_op jit(solution)/shard_map/ppermute | solution.py:51
  4.1 1.6 %collective-permute-start.1 = (bf16[192,256]{1,0:T(8,128)(2,1)S(1)}, bf16[192,256]{1,0:T(8,128)(2,1)S(1)}, u32[]{:S(2)}, u32[]{:S(2)}) collective-permute-start(bf16[192,256]{1,0:T(8,128)(2,1)S(1)} %get-tuple-element.33), channel_id=1, source_target_pairs={{0,1},{1,2},{2,3},{3,4},{4,5},{5,6},{6,7},{7,0},{8,9},{9,10},{10,1... | collective-permute-start | bytes 294920 | tf_op jit(solution)/shard_map/ppermute | solution.py:51
  5.7 1.6 %collective-permute-start = (bf16[13,14,256]{2,1,0:T(8,128)(2,1)S(1)}, bf16[13,14,256]{2,1,0:T(8,128)(2,1)S(1)}, u32[]{:S(2)}, u32[]{:S(2)}) collective-permute-start(bf16[13,14,256]{2,1,0:T(8,128)(2,1)S(1)} %get-tuple-element.32), channel_id=1, source_target_pairs={{0,8},{1,9},{2,10},{3,11},{4,12},{5,13},{6,14},{7,15},{8,16},{9,17... | collective-permute-start | bytes 279560 | tf_op jit(solution)/shard_map/ppermute | solution.py:51
  7.3 2.2 %copy-done.2 = bf16[2,2,2,512,512]{4,3,2,1,0:T(8,128)(2,1)S(1)} copy-done((bf16[2,2,2,512,512]{4,3,2,1,0:T(8,128)(2,1)S(1)}, bf16[2,2,2,512,512]{4,3,2,1,0:T(8,128)(2,1)}, u32[]{:S(2)}) %copy-start.2) | copy-done | bytes 4194328
  9.5 0.7 copy-done.3
  10.2 4.5 %renumber.1.refs_4_.refs_8_ = bf16[8,512,512]{2,1,0:T(8,128)(2,1)S(1)} custom-call(s32[2,2,2,512]{3,2,1,0:T(2,128)S(1)} %copy-done.3, bf16[8,512,512]{2,1,0:T(8,128)(2,1)S(1)} %bitcast.5), custom_call_target="tpu_custom_call" | custom-call | flops 4294967296 | bytes 8388608 | tf_op jit(solution)/shard_map/renumber/pallas_call | solution.py:127
  14.7 2.1 %shard_map.38 = (f32[8,2,512,128]{3,2,1,0:T(8,128)S(1)}, f32[8,2,512,128]{3,2,1,0:T(8,128)S(1)}, bf16[14,16,256]{2,1,0:T(8,128)(2,1)S(1)}, bf16[14,16,256]{2,1,0...) custom-call(bf16[14,13,14,256]{3,2,1,0:T(8,128)(2,1)S(1)} %bitcast.4, ...), custom_call_target="tpu_custom_call" | custom-call | flops 1073741824 | bytes 14578688 | tf_op jit(solution)/shard_map/pallas_call | solution.py:700
  16.9 1.6 %collective-permute-start.3 = (bf16[14,16,256]{2,1,0:T(8,128)(2,1)S(1)}, bf16[14,16,256]{2,1,0:T(8,128)(2,1)S(1)}, u32[]{:S(2)}, u32[]{:S(2)}) collective-permute-start(bf16[14,16,256]{2,1,0:T(8,128)(2,1)S(1)} %get-tuple-element.36), channel_id=1, source_target_pairs={{0,8},{1,9},{2,10},{3,11},{4,12},{5,13},{6,14},{7,15},{8,0},{9,1},... | collective-permute-start | bytes 344072 | tf_op jit(solution)/shard_map/ppermute | solution.py:41
  18.5 0.7 collective-permute-start.4
  19.2 0.1 collective-permute-start.5
  19.3 1.5 %collective-permute-start.6 = (bf16[4,64,256]{2,1,0:T(8,128)(2,1)S(1)}, bf16[4,64,256]{2,1,0:T(8,128)(2,1)S(1)}, u32[]{:S(2)}, u32[]{:S(2)}) collective-permute-start(bf16[4,64,256]{2,1,0:T(8,128)(2,1)S(1)} %get-tuple-element.39), channel_id=1, source_target_pairs={{0,7},{1,2},{2,1},{3,4},{4,3},{5,6},{6,5},{7,0},{8,15},{9,10},{10,... | collective-permute-start | bytes 393224 | tf_op jit(solution)/shard_map/ppermute | solution.py:41
  20.8 0.9 %collective-permute-done.3.from_a.refs_1_ = bf16[14,16,256]{2,1,0:T(8,128)(2,1)S(1)} collective-permute-done((bf16[14,16,256]{2,1,0:T(8,128)(2,1)S(1)}, bf16[14,16,256]{2,1,0:T(8,128)(2,1)S(1)}, u32[]{:S(2)}, u32[]{:S(2)}) %collective-permute-start.3) | collective-permute-done | bytes 114720 | tf_op jit(solution)/shard_map/ppermute | solution.py:41
  21.7 0.1 shard_map.39
  21.8 0.1 collective-permute-start.7
  21.9 1.5 %collective-permute-start.8 = (f32[2,16,256]{2,1,0:T(8,128)S(1)}, f32[2,16,256]{2,1,0:T(8,128)S(1)}, u32[]{:S(2)}, u32[]{:S(2)}) collective-permute-start(f32[2,16,256]{2,1,0:T(8,128)S(1)} %get-tuple-element.41), channel_id=1, source_target_pairs={{0,7},{1,2},{2,1},{3,4},{4,3},{5,6},{6,5},{7,0},{8,15},{9,10},{10,... | collective-permute-start | bytes 98312 | tf_op jit(solution)/shard_map/ppermute | solution.py:41
  23.5 2.0 %collective-permute-done.6.refs_4_ = bf16[4,64,256]{2,1,0:T(8,128)(2,1)S(1)} collective-permute-done((bf16[4,64,256]{2,1,0:T(8,128)(2,1)S(1)}, bf16[4,64,256]{2,1,0:T(8,128)(2,1)S(1)}, u32[]{:S(2)}, u32[]{:S(2)}) %collective-permute-start.6) | collective-permute-done | bytes 131104 | tf_op jit(solution)/shard_map/ppermute | solution.py:41
  25.4 1.0 %collective-permute-done.8.refs_6_ = f32[2,16,256]{2,1,0:T(8,128)S(1)} collective-permute-done((f32[2,16,256]{2,1,0:T(8,128)S(1)}, f32[2,16,256]{2,1,0:T(8,128)S(1)}, u32[]{:S(2)}, u32[]{:S(2)}) %collective-permute-start.8) | collective-permute-done | bytes 32800 | tf_op jit(solution)/shard_map/ppermute | solution.py:41
  26.4 2.5 %shard_map.40 = (f32[8,2,512,128]{3,2,1,0:T(8,128)S(1)}, f32[8,2,512,128]{3,2,1,0:T(8,128)S(1)}, bf16[14,16,256]{2,1,0:T(8,128)(2,1)S(1)}, bf16[14,16,256]{2,1,0...) custom-call(f32[8,2,512,128]{3,2,1,0:T(8,128)S(1)} %get-tuple-element.35.refs_0_, ...), custom_call_target="tpu_custom_call" | custom-call | flops 1073741824 | bytes 22020096 | tf_op jit(solution)/shard_map/pallas_call | solution.py:700
  28.9 3.8 %collective-permute-start.9 = (bf16[14,16,256]{2,1,0:T(8,128)(2,1)S(1)}, bf16[14,16,256]{2,1,0:T(8,128)(2,1)S(1)}, u32[]{:S(2)}, u32[]{:S(2)}) collective-permute-start(bf16[14,16,256]{2,1,0:T(8,128)(2,1)S(1)} %get-tuple-element.44), channel_id=1, source_target_pairs={{0,8},{1,9},{2,10},{3,11},{4,12},{5,13},{6,14},{7,15},{8,0},{9,1},... | collective-permute-start | bytes 344072 | tf_op jit(solution)/shard_map/ppermute | solution.py:41
  32.7 0.7 collective-permute-start.10
  33.4 0.1 collective-permute-start.11
  33.5 1.3 %collective-permute-start.12 = (bf16[4,64,256]{2,1,0:T(8,128)(2,1)S(1)}, bf16[4,64,256]{2,1,0:T(8,128)(2,1)S(1)}, u32[]{:S(2)}, u32[]{:S(2)}) collective-permute-start(bf16[4,64,256]{2,1,0:T(8,128)(2,1)S(1)} %get-tuple-element.47), channel_id=1, source_target_pairs={{0,7},{1,2},{2,1},{3,4},{4,3},{5,6},{6,5},{7,0},{8,15},{9,10},{10,... | collective-permute-start | bytes 393224 | tf_op jit(solution)/shard_map/ppermute | solution.py:41
  34.7 1.1 %collective-permute-done.9.from_a.refs_1_ = bf16[14,16,256]{2,1,0:T(8,128)(2,1)S(1)} collective-permute-done((bf16[14,16,256]{2,1,0:T(8,128)(2,1)S(1)}, bf16[14,16,256]{2,1,0:T(8,128)(2,1)S(1)}, u32[]{:S(2)}, u32[]{:S(2)}) %collective-permute-start.9) | collective-permute-done | bytes 114720 | tf_op jit(solution)/shard_map/ppermute | solution.py:41
  35.9 0.1 shard_map.41
  36.0 0.9 %collective-permute-start.14 = (f32[2,16,256]{2,1,0:T(8,128)S(1)}, f32[2,16,256]{2,1,0:T(8,128)S(1)}, u32[]{:S(2)}, u32[]{:S(2)}) collective-permute-start(f32[2,16,256]{2,1,0:T(8,128)S(1)} %get-tuple-element.49), channel_id=1, source_target_pairs={{0,7},{1,2},{2,1},{3,4},{4,3},{5,6},{6,5},{7,0},{8,15},{9,10},{10,... | collective-permute-start | bytes 98312 | tf_op jit(solution)/shard_map/ppermute | solution.py:41
  36.9 2.7 %collective-permute-done.12.refs_4_ = bf16[4,64,256]{2,1,0:T(8,128)(2,1)S(1)} collective-permute-done((bf16[4,64,256]{2,1,0:T(8,128)(2,1)S(1)}, bf16[4,64,256]{2,1,0:T(8,128)(2,1)S(1)}, u32[]{:S(2)}, u32[]{:S(2)}) %collective-permute-start.12) | collective-permute-done | bytes 131104 | tf_op jit(solution)/shard_map/ppermute | solution.py:41
  39.6 1.0 %collective-permute-done.14.refs_6_ = f32[2,16,256]{2,1,0:T(8,128)S(1)} collective-permute-done((f32[2,16,256]{2,1,0:T(8,128)S(1)}, f32[2,16,256]{2,1,0:T(8,128)S(1)}, u32[]{:S(2)}, u32[]{:S(2)}) %collective-permute-start.14) | collective-permute-done | bytes 32800 | tf_op jit(solution)/shard_map/ppermute | solution.py:41
  40.6 2.5 %shard_map.42 = (f32[8,2,512,128]{3,2,1,0:T(8,128)S(1)}, bf16[14,16,256]{2,1,0:T(8,128)(2,1)S(1)}, bf16[4,64,256]{2,1,0:T(8,128)(2,1)S(1)}, f32[16,256]{1,0:T(8,128)S(1)}) custom-call(f32[8,2,512,128]{3,2,1,0:T(8,128)S(1)} %get-tuple-element.43.refs_0_, bf16[14,16,256]{2,1,0:T(8,128)(2,1)S(1)} %collective-permute-done.9.from_a.refs_1_, ...), custom_call_target="tpu_custom_call" | custom-call | flops 1073741824 | bytes 17596416 | tf_op jit(solution)/shard_map/pallas_call | solution.py:700
  43.1 1.4 %collective-permute-start.16 = (bf16[4,64,256]{2,1,0:T(8,128)(2,1)S(1)}, bf16[4,64,256]{2,1,0:T(8,128)(2,1)S(1)}, u32[]{:S(2)}, u32[]{:S(2)}) collective-permute-start(bf16[4,64,256]{2,1,0:T(8,128)(2,1)S(1)} %get-tuple-element.53), channel_id=1, source_target_pairs={{0,7},{1,0},{2,1},{3,2},{4,3},{5,4},{6,5},{7,6},{8,15},{9,8},{10,9... | collective-permute-start | bytes 393224 | tf_op jit(solution)/shard_map/ppermute | solution.py:51
  44.4 2.3 %collective-permute-start.15 = (bf16[14,16,256]{2,1,0:T(8,128)(2,1)S(1)}, bf16[14,16,256]{2,1,0:T(8,128)(2,1)S(1)}, u32[]{:S(2)}, u32[]{:S(2)}) collective-permute-start(bf16[14,16,256]{2,1,0:T(8,128)(2,1)S(1)} %get-tuple-element.52), channel_id=1, source_target_pairs={{0,24},{1,25},{2,26},{3,27},{4,28},{5,29},{6,30},{7,31},{8,0},{9,1... | collective-permute-start | bytes 344072 | tf_op jit(solution)/shard_map/ppermute | solution.py:51
  46.7 3.0 %collective-permute-start.17 = (f32[16,256]{1,0:T(8,128)S(1)}, f32[16,256]{1,0:T(8,128)S(1)}, u32[]{:S(2)}, u32[]{:S(2)}) collective-permute-start(f32[16,256]{1,0:T(8,128)S(1)} %get-tuple-element.54), channel_id=1, source_target_pairs={{0,31},{1,24},{2,25},{3,26},{4,27},{5,28},{6,29},{7,30},{8,7},{9,0... | collective-permute-start | bytes 49160 | tf_op jit(solution)/shard_map/ppermute | solution.py:51
  49.7 1.4 %collective-permute-done.17.from_xy = f32[16,256]{1,0:T(8,128)S(1)} collective-permute-done((f32[16,256]{1,0:T(8,128)S(1)}, f32[16,256]{1,0:T(8,128)S(1)}, u32[]{:S(2)}, u32[]{:S(2)}) %collective-permute-start.17) | collective-permute-done | bytes 16416 | tf_op jit(solution)/shard_map/ppermute | solution.py:51
  51.2 2.1 %shard_map.43 = (bf16[2912,256]{1,0:T(8,128)(2,1)S(1)}, bf16[2912,256]{1,0:T(8,128)(2,1)S(1)}, f32[136,128]{1,0:T(8,128)S(1)}, f32[136,128]{1,0:T(8,128)S(1)}) custom-call(f32[8,2,512,128]{3,2,1,0:T(8,128)S(1)} %get-tuple-element.51.part_ref, bf16[14,16,256]{2,1,0:T(8,128)(2,1)S(1)} %collective-permute-done.15.from_x, ...), custom_call_target="tpu_custom_call" | custom-call | flops 1526726656 | bytes 7577600 | tf_op jit(solution)/shard_map/pallas_call | solution.py:700
  53.3 0.5 collective-permute-start.18
  53.7 0.9 %collective-permute-done.18 = f32[136,128]{1,0:T(8,128)S(1)} collective-permute-done((f32[136,128]{1,0:T(8,128)S(1)}, f32[136,128]{1,0:T(8,128)S(1)}, u32[]{:S(2)}, u32[]{:S(2)}) %collective-permute-start.18) | collective-permute-done | bytes 69664 | tf_op jit(solution)/shard_map/ppermute | solution.py:55
  54.7 4.3 %collective-permute-start.21 = (f32[136,128]{1,0:T(8,128)S(1)}, f32[136,128]{1,0:T(8,128)S(1)}, u32[]{:S(2)}, u32[]{:S(2)}) collective-permute-start(f32[136,128]{1,0:T(8,128)S(1)} %add.21), channel_id=1, source_target_pairs={{0,24},{1,7},{2,26},{3,5},{4,28},{5,3},{6,30},{7,1},{8,16},{9,15},... | collective-permute-start | bytes 208904 | tf_op jit(solution)/shard_map/ppermute | solution.py:66
  58.9 0.6 collective-permute-start.19
  59.6 1.6 %collective-permute-done.21 = f32[136,128]{1,0:T(8,128)S(1)} collective-permute-done((f32[136,128]{1,0:T(8,128)S(1)}, f32[136,128]{1,0:T(8,128)S(1)}, u32[]{:S(2)}, u32[]{:S(2)}) %collective-permute-start.21) | collective-permute-done | bytes 69664 | tf_op jit(solution)/shard_map/ppermute | solution.py:66
  61.2 2.9 %collective-permute-done.20 = f32[136,128]{1,0:T(8,128)S(1)} collective-permute-done((f32[136,128]{1,0:T(8,128)S(1)}, f32[136,128]{1,0:T(8,128)S(1)}, u32[]{:S(2)}, u32[]{:S(2)}) %collective-permute-start.20) | collective-permute-done | bytes 69664 | tf_op jit(solution)/shard_map/ppermute | solution.py:66
  64.2 2.3 %collective-permute-start.24 = (f32[136,128]{1,0:T(8,128)S(1)}, f32[136,128]{1,0:T(8,128)S(1)}, u32[]{:S(2)}, u32[]{:S(2)}) collective-permute-start(f32[136,128]{1,0:T(8,128)S(1)} %add_add_fusion.1), channel_id=1, source_target_pairs={{0,6},{1,25},{2,4},{3,27},{4,2},{5,29},{6,0},{7,31},{8,14},{9,17},... | collective-permute-start | bytes 208904 | tf_op jit(solution)/shard_map/ppermute | solution.py:66
  66.5 1.7 %collective-permute-start.23 = (f32[136,128]{1,0:T(8,128)S(1)}, f32[136,128]{1,0:T(8,128)S(1)}, u32[]{:S(2)}, u32[]{:S(2)}) collective-permute-start(f32[136,128]{1,0:T(8,128)S(1)} %add_add_fusion.1), channel_id=1, source_target_pairs={{0,4},{1,17},{2,6},{3,19},{4,0},{5,21},{6,2},{7,23},{8,12},{9,25},... | collective-permute-start | bytes 208904 | tf_op jit(solution)/shard_map/ppermute | solution.py:66
  68.2 1.3 %collective-permute-done.24 = f32[136,128]{1,0:T(8,128)S(1)} collective-permute-done((f32[136,128]{1,0:T(8,128)S(1)}, f32[136,128]{1,0:T(8,128)S(1)}, u32[]{:S(2)}, u32[]{:S(2)}) %collective-permute-start.24) | collective-permute-done | bytes 69664 | tf_op jit(solution)/shard_map/ppermute | solution.py:66
  69.4 1.3 %collective-permute-done.23 = f32[136,128]{1,0:T(8,128)S(1)} collective-permute-done((f32[136,128]{1,0:T(8,128)S(1)}, f32[136,128]{1,0:T(8,128)S(1)}, u32[]{:S(2)}, u32[]{:S(2)}) %collective-permute-start.23) | collective-permute-done | bytes 69664 | tf_op jit(solution)/shard_map/ppermute | solution.py:66
  70.8 1.7 %collective-permute-done.22 = f32[136,128]{1,0:T(8,128)S(1)} collective-permute-done((f32[136,128]{1,0:T(8,128)S(1)}, f32[136,128]{1,0:T(8,128)S(1)}, u32[]{:S(2)}, u32[]{:S(2)}) %collective-permute-start.22) | collective-permute-done | bytes 69664 | tf_op jit(solution)/shard_map/ppermute | solution.py:66
  72.6 1.2 %collective-permute-done.25.other_ref = f32[136,128]{1,0:T(8,128)S(1)} collective-permute-done((f32[136,128]{1,0:T(8,128)S(1)}, f32[136,128]{1,0:T(8,128)S(1)}, u32[]{:S(2)}, u32[]{:S(2)}) %collective-permute-start.25) | collective-permute-done | bytes 69664 | tf_op jit(solution)/shard_map/ppermute | solution.py:55
  73.8 13.3 %basis.1 = f32[14,13,14,256]{3,2,1,0:T(8,128)} custom-call(f32[136,128]{1,0:T(8,128)S(1)} %add_add_fusion.mine_ref, f32[136,128]{1,0:T(8,128)S(1)} %collective-permute-done.25.other_ref, bf16[2912,256]{1,0:T(8,128)(2,1)S(1)} %get-tuple-element.57.high_ref, bf16[2912,256]{1,0:T(8,128)(2,1)S(1)} %get-tuple-element.58.low_ref), custom_call_target="tpu_custom_call" | custom-call | tf_op jit(solution)/shard_map/basis/pallas_call | solution.py:789
  (24 shorter events, 0.2 us)
Async XLA Ops:
  0.0 1.4 %copy-start = (bf16[14,14,13,256]{3,1,2,0:T(8,128)(2,1)S(1)}, bf16[14,14,13,256]{3,1,2,0:T(8,128)(2,1)}, u32[]{:S(2)}) copy-start(bf16[14,14,13,256]{3,1,2,0:T(8,128)(2,1)} %param.3) | copy-start | bytes 3913732
  1.6 13.1 %collective-permute-start.2 = (bf16[16,256]{1,0:T(8,128)(2,1)S(1)}, bf16[16,256]{1,0:T(8,128)(2,1)S(1)}, u32[]{:S(2)}, u32[]{:S(2)}) collective-permute-start(bf16[16,256]{1,0:T(8,128)(2,1)S(1)} %get-tuple-element.34), channel_id=1, source_target_pairs={{0,9},{1,10},{2,11},{3,12},{4,13},{5,14},{6,15},{7,8},{8,17},{9,18... | collective-permute-start | bytes 24584 | tf_op jit(solution)/shard_map/ppermute | solution.py:51
  4.1 10.6 %collective-permute-start.1 = (bf16[192,256]{1,0:T(8,128)(2,1)S(1)}, bf16[192,256]{1,0:T(8,128)(2,1)S(1)}, u32[]{:S(2)}, u32[]{:S(2)}) collective-permute-start(bf16[192,256]{1,0:T(8,128)(2,1)S(1)} %get-tuple-element.33), channel_id=1, source_target_pairs={{0,1},{1,2},{2,3},{3,4},{4,5},{5,6},{6,7},{7,0},{8,9},{9,10},{10,1... | collective-permute-start | bytes 294920 | tf_op jit(solution)/shard_map/ppermute | solution.py:51
  5.7 9.0 %collective-permute-start = (bf16[13,14,256]{2,1,0:T(8,128)(2,1)S(1)}, bf16[13,14,256]{2,1,0:T(8,128)(2,1)S(1)}, u32[]{:S(2)}, u32[]{:S(2)}) collective-permute-start(bf16[13,14,256]{2,1,0:T(8,128)(2,1)S(1)} %get-tuple-element.32), channel_id=1, source_target_pairs={{0,8},{1,9},{2,10},{3,11},{4,12},{5,13},{6,14},{7,15},{8,16},{9,17... | collective-permute-start | bytes 279560 | tf_op jit(solution)/shard_map/ppermute | solution.py:51
  7.3 2.2 %copy-start.2 = (bf16[2,2,2,512,512]{4,3,2,1,0:T(8,128)(2,1)S(1)}, bf16[2,2,2,512,512]{4,3,2,1,0:T(8,128)(2,1)}, u32[]{:S(2)}) copy-start(bf16[2,2,2,512,512]{4,3,2,1,0:T(8,128)(2,1)} %param.4) | copy-start | bytes 12582916
  9.5 0.7 copy-start.3
  10.2 4.6 %copy-start.1 = (bf16[14,14,13,256]{3,1,2,0:T(8,128)(2,1)S(1)}, bf16[14,14,13,256]{3,1,2,0:T(8,128)(2,1)}, u32[]{:S(2)}) copy-start(bf16[14,14,13,256]{3,1,2,0:T(8,128)(2,1)} %param.3) | copy-start | bytes 3913732
  16.9 4.9 %collective-permute-start.3 = (bf16[14,16,256]{2,1,0:T(8,128)(2,1)S(1)}, bf16[14,16,256]{2,1,0:T(8,128)(2,1)S(1)}, u32[]{:S(2)}, u32[]{:S(2)}) collective-permute-start(bf16[14,16,256]{2,1,0:T(8,128)(2,1)S(1)} %get-tuple-element.36), channel_id=1, source_target_pairs={{0,8},{1,9},{2,10},{3,11},{4,12},{5,13},{6,14},{7,15},{8,0},{9,1},... | collective-permute-start | bytes 344072 | tf_op jit(solution)/shard_map/ppermute | solution.py:41
  18.5 3.2 %collective-permute-start.4 = (bf16[14,16,256]{2,1,0:T(8,128)(2,1)S(1)}, bf16[14,16,256]{2,1,0:T(8,128)(2,1)S(1)}, u32[]{:S(2)}, u32[]{:S(2)}) collective-permute-start(bf16[14,16,256]{2,1,0:T(8,128)(2,1)S(1)} %get-tuple-element.37), channel_id=1, source_target_pairs={{0,0},{1,1},{2,2},{3,3},{4,4},{5,5},{6,6},{7,7},{8,16},{9,17},{10,... | collective-permute-start | bytes 344072 | tf_op jit(solution)/shard_map/ppermute | solution.py:41
  19.2 4.3 %collective-permute-start.5 = (bf16[4,64,256]{2,1,0:T(8,128)(2,1)S(1)}, bf16[4,64,256]{2,1,0:T(8,128)(2,1)S(1)}, u32[]{:S(2)}, u32[]{:S(2)}) collective-permute-start(bf16[4,64,256]{2,1,0:T(8,128)(2,1)S(1)} %get-tuple-element.38), channel_id=1, source_target_pairs={{0,1},{1,0},{2,3},{3,2},{4,5},{5,4},{6,7},{7,6},{8,9},{9,8},{10,11... | collective-permute-start | bytes 393224 | tf_op jit(solution)/shard_map/ppermute | solution.py:41
  19.3 6.1 %collective-permute-start.6 = (bf16[4,64,256]{2,1,0:T(8,128)(2,1)S(1)}, bf16[4,64,256]{2,1,0:T(8,128)(2,1)S(1)}, u32[]{:S(2)}, u32[]{:S(2)}) collective-permute-start(bf16[4,64,256]{2,1,0:T(8,128)(2,1)S(1)} %get-tuple-element.39), channel_id=1, source_target_pairs={{0,7},{1,2},{2,1},{3,4},{4,3},{5,6},{6,5},{7,0},{8,15},{9,10},{10,... | collective-permute-start | bytes 393224 | tf_op jit(solution)/shard_map/ppermute | solution.py:41
  21.8 3.6 %collective-permute-start.7 = (f32[2,16,256]{2,1,0:T(8,128)S(1)}, f32[2,16,256]{2,1,0:T(8,128)S(1)}, u32[]{:S(2)}, u32[]{:S(2)}) collective-permute-start(f32[2,16,256]{2,1,0:T(8,128)S(1)} %get-tuple-element.40), channel_id=1, source_target_pairs={{0,1},{1,0},{2,3},{3,2},{4,5},{5,4},{6,7},{7,6},{8,9},{9,8},{10,11... | collective-permute-start | bytes 98312 | tf_op jit(solution)/shard_map/ppermute | solution.py:41
  21.9 4.5 %collective-permute-start.8 = (f32[2,16,256]{2,1,0:T(8,128)S(1)}, f32[2,16,256]{2,1,0:T(8,128)S(1)}, u32[]{:S(2)}, u32[]{:S(2)}) collective-permute-start(f32[2,16,256]{2,1,0:T(8,128)S(1)} %get-tuple-element.41), channel_id=1, source_target_pairs={{0,7},{1,2},{2,1},{3,4},{4,3},{5,6},{6,5},{7,0},{8,15},{9,10},{10,... | collective-permute-start | bytes 98312 | tf_op jit(solution)/shard_map/ppermute | solution.py:41
  28.9 6.9 %collective-permute-start.9 = (bf16[14,16,256]{2,1,0:T(8,128)(2,1)S(1)}, bf16[14,16,256]{2,1,0:T(8,128)(2,1)S(1)}, u32[]{:S(2)}, u32[]{:S(2)}) collective-permute-start(bf16[14,16,256]{2,1,0:T(8,128)(2,1)S(1)} %get-tuple-element.44), channel_id=1, source_target_pairs={{0,8},{1,9},{2,10},{3,11},{4,12},{5,13},{6,14},{7,15},{8,0},{9,1},... | collective-permute-start | bytes 344072 | tf_op jit(solution)/shard_map/ppermute | solution.py:41
  32.7 3.1 %collective-permute-start.10 = (bf16[14,16,256]{2,1,0:T(8,128)(2,1)S(1)}, bf16[14,16,256]{2,1,0:T(8,128)(2,1)S(1)}, u32[]{:S(2)}, u32[]{:S(2)}) collective-permute-start(bf16[14,16,256]{2,1,0:T(8,128)(2,1)S(1)} %get-tuple-element.45), channel_id=1, source_target_pairs={{0,0},{1,1},{2,2},{3,3},{4,4},{5,5},{6,6},{7,7},{8,16},{9,17},{10,... | collective-permute-start | bytes 344072 | tf_op jit(solution)/shard_map/ppermute | solution.py:41
  33.4 3.6 %collective-permute-start.11 = (bf16[4,64,256]{2,1,0:T(8,128)(2,1)S(1)}, bf16[4,64,256]{2,1,0:T(8,128)(2,1)S(1)}, u32[]{:S(2)}, u32[]{:S(2)}) collective-permute-start(bf16[4,64,256]{2,1,0:T(8,128)(2,1)S(1)} %get-tuple-element.46), channel_id=1, source_target_pairs={{0,1},{1,0},{2,3},{3,2},{4,5},{5,4},{6,7},{7,6},{8,9},{9,8},{10,11... | collective-permute-start | bytes 393224 | tf_op jit(solution)/shard_map/ppermute | solution.py:41
  33.5 6.1 %collective-permute-start.12 = (bf16[4,64,256]{2,1,0:T(8,128)(2,1)S(1)}, bf16[4,64,256]{2,1,0:T(8,128)(2,1)S(1)}, u32[]{:S(2)}, u32[]{:S(2)}) collective-permute-start(bf16[4,64,256]{2,1,0:T(8,128)(2,1)S(1)} %get-tuple-element.47), channel_id=1, source_target_pairs={{0,7},{1,2},{2,1},{3,4},{4,3},{5,6},{6,5},{7,0},{8,15},{9,10},{10,... | collective-permute-start | bytes 393224 | tf_op jit(solution)/shard_map/ppermute | solution.py:41
  36.0 3.6 %collective-permute-start.13 = (f32[2,16,256]{2,1,0:T(8,128)S(1)}, f32[2,16,256]{2,1,0:T(8,128)S(1)}, u32[]{:S(2)}, u32[]{:S(2)}) collective-permute-start(f32[2,16,256]{2,1,0:T(8,128)S(1)} %get-tuple-element.48), channel_id=1, source_target_pairs={{0,1},{1,0},{2,3},{3,2},{4,5},{5,4},{6,7},{7,6},{8,9},{9,8},{10,11... | collective-permute-start | bytes 98312 | tf_op jit(solution)/shard_map/ppermute | solution.py:41
  36.0 4.5 %collective-permute-start.14 = (f32[2,16,256]{2,1,0:T(8,128)S(1)}, f32[2,16,256]{2,1,0:T(8,128)S(1)}, u32[]{:S(2)}, u32[]{:S(2)}) collective-permute-start(f32[2,16,256]{2,1,0:T(8,128)S(1)} %get-tuple-element.49), channel_id=1, source_target_pairs={{0,7},{1,2},{2,1},{3,4},{4,3},{5,6},{6,5},{7,0},{8,15},{9,10},{10,... | collective-permute-start | bytes 98312 | tf_op jit(solution)/shard_map/ppermute | solution.py:41
  43.1 8.1 %collective-permute-start.16 = (bf16[4,64,256]{2,1,0:T(8,128)(2,1)S(1)}, bf16[4,64,256]{2,1,0:T(8,128)(2,1)S(1)}, u32[]{:S(2)}, u32[]{:S(2)}) collective-permute-start(bf16[4,64,256]{2,1,0:T(8,128)(2,1)S(1)} %get-tuple-element.53), channel_id=1, source_target_pairs={{0,7},{1,0},{2,1},{3,2},{4,3},{5,4},{6,5},{7,6},{8,15},{9,8},{10,9... | collective-permute-start | bytes 393224 | tf_op jit(solution)/shard_map/ppermute | solution.py:51
  44.4 6.7 %collective-permute-start.15 = (bf16[14,16,256]{2,1,0:T(8,128)(2,1)S(1)}, bf16[14,16,256]{2,1,0:T(8,128)(2,1)S(1)}, u32[]{:S(2)}, u32[]{:S(2)}) collective-permute-start(bf16[14,16,256]{2,1,0:T(8,128)(2,1)S(1)} %get-tuple-element.52), channel_id=1, source_target_pairs={{0,24},{1,25},{2,26},{3,27},{4,28},{5,29},{6,30},{7,31},{8,0},{9,1... | collective-permute-start | bytes 344072 | tf_op jit(solution)/shard_map/ppermute | solution.py:51
  46.7 4.5 %collective-permute-start.17 = (f32[16,256]{1,0:T(8,128)S(1)}, f32[16,256]{1,0:T(8,128)S(1)}, u32[]{:S(2)}, u32[]{:S(2)}) collective-permute-start(f32[16,256]{1,0:T(8,128)S(1)} %get-tuple-element.54), channel_id=1, source_target_pairs={{0,31},{1,24},{2,25},{3,26},{4,27},{5,28},{6,29},{7,30},{8,7},{9,0... | collective-permute-start | bytes 49160 | tf_op jit(solution)/shard_map/ppermute | solution.py:51
  53.3 1.4 %collective-permute-start.18 = (f32[136,128]{1,0:T(8,128)S(1)}, f32[136,128]{1,0:T(8,128)S(1)}, u32[]{:S(2)}, u32[]{:S(2)}) collective-permute-start(f32[136,128]{1,0:T(8,128)S(1)} %get-tuple-element.56), channel_id=1, source_target_pairs={{0,1},{1,0},{2,3},{3,2},{4,5},{5,4},{6,7},{7,6},{8,9},{9,8},{10,11... | collective-permute-start | bytes 208904 | tf_op jit(solution)/shard_map/ppermute | solution.py:55
  54.7 6.6 %collective-permute-start.21 = (f32[136,128]{1,0:T(8,128)S(1)}, f32[136,128]{1,0:T(8,128)S(1)}, u32[]{:S(2)}, u32[]{:S(2)}) collective-permute-start(f32[136,128]{1,0:T(8,128)S(1)} %add.21), channel_id=1, source_target_pairs={{0,24},{1,7},{2,26},{3,5},{4,28},{5,3},{6,30},{7,1},{8,16},{9,15},... | collective-permute-start | bytes 208904 | tf_op jit(solution)/shard_map/ppermute | solution.py:66
  58.9 5.2 %collective-permute-start.20 = (f32[136,128]{1,0:T(8,128)S(1)}, f32[136,128]{1,0:T(8,128)S(1)}, u32[]{:S(2)}, u32[]{:S(2)}) collective-permute-start(f32[136,128]{1,0:T(8,128)S(1)} %add.21), channel_id=1, source_target_pairs={{0,16},{1,5},{2,18},{3,7},{4,20},{5,1},{6,22},{7,3},{8,24},{9,13},... | collective-permute-start | bytes 208904 | tf_op jit(solution)/shard_map/ppermute | solution.py:66
  58.9 5.2 %collective-permute-start.19 = (f32[136,128]{1,0:T(8,128)S(1)}, f32[136,128]{1,0:T(8,128)S(1)}, u32[]{:S(2)}, u32[]{:S(2)}) collective-permute-start(f32[136,128]{1,0:T(8,128)S(1)} %add.21), channel_id=1, source_target_pairs={{0,8},{1,3},{2,10},{3,1},{4,12},{5,7},{6,14},{7,5},{8,0},{9,11},{1... | collective-permute-start | bytes 208904 | tf_op jit(solution)/shard_map/ppermute | solution.py:66
  64.2 5.3 %collective-permute-start.24 = (f32[136,128]{1,0:T(8,128)S(1)}, f32[136,128]{1,0:T(8,128)S(1)}, u32[]{:S(2)}, u32[]{:S(2)}) collective-permute-start(f32[136,128]{1,0:T(8,128)S(1)} %add_add_fusion.1), channel_id=1, source_target_pairs={{0,6},{1,25},{2,4},{3,27},{4,2},{5,29},{6,0},{7,31},{8,14},{9,17},... | collective-permute-start | bytes 208904 | tf_op jit(solution)/shard_map/ppermute | solution.py:66
  66.5 4.3 %collective-permute-start.23 = (f32[136,128]{1,0:T(8,128)S(1)}, f32[136,128]{1,0:T(8,128)S(1)}, u32[]{:S(2)}, u32[]{:S(2)}) collective-permute-start(f32[136,128]{1,0:T(8,128)S(1)} %add_add_fusion.1), channel_id=1, source_target_pairs={{0,4},{1,17},{2,6},{3,19},{4,0},{5,21},{6,2},{7,23},{8,12},{9,25},... | collective-permute-start | bytes 208904 | tf_op jit(solution)/shard_map/ppermute | solution.py:66
  68.2 4.3 %collective-permute-start.22 = (f32[136,128]{1,0:T(8,128)S(1)}, f32[136,128]{1,0:T(8,128)S(1)}, u32[]{:S(2)}, u32[]{:S(2)}) collective-permute-start(f32[136,128]{1,0:T(8,128)S(1)} %add_add_fusion.1), channel_id=1, source_target_pairs={{0,2},{1,9},{2,0},{3,11},{4,6},{5,13},{6,4},{7,15},{8,10},{9,1},{1... | collective-permute-start | bytes 208904 | tf_op jit(solution)/shard_map/ppermute | solution.py:66
  72.5 1.3 %collective-permute-start.25 = (f32[136,128]{1,0:T(8,128)S(1)}, f32[136,128]{1,0:T(8,128)S(1)}, u32[]{:S(2)}, u32[]{:S(2)}) collective-permute-start(f32[136,128]{1,0:T(8,128)S(1)} %add_add_fusion.mine_ref), channel_id=1, source_target_pairs={{0,1},{1,0},{2,3},{3,2},{4,5},{5,4},{6,7},{7,6},{8,9},{9,8},{10,11... | collective-permute-start | bytes 208904 | tf_op jit(solution)/shard_map/ppermute | solution.py:55
